TPU v7x, 512 devices: a whole 4x8x8 slice. The times are simulated.
512 devices in a mesh: row: 16 (over x, z_lo, core), col: 32 (over y, z_hi).
Axes of the slice: x: 4, y: 8, z: 8 (z_hi: 4, z_lo: 2; z = z_hi * 2 + z_lo), core: 2. Of those that a mesh axis runs over, the one named last changes fastest.
Arguments:
- features: float32 [65536, 256], P(('row', 'col')), may hold values from -6 to 6
- adjacency_tiles: float32 [32768, 128, 128], P(('row', 'col')), may hold values from -0.0625 to 0.0625
- tile_rows: int32 [32768], P(('row', 'col')), may hold values from 0 to 31
- tile_cols: int32 [32768], P(('row', 'col')), may hold values from 0 to 15
- tile_count: int32 [512], P(('row', 'col')), may hold values from 8 to 64, as said below
- weight: float32 [256, 256], replicated, may hold values from -0.375 to 0.375
- cotangent: float32 [65536, 256], P(('row', 'col')), may hold values from -0.0234375 to 0.0234375
Outputs:
- activated: float32 [65536, 256], P(('row', 'col'))
- weight_grad: float32 [256, 256], replicated
Inputs may be any that keep to these rules, and one draw needn't show every extreme that they name: `tile_count`: some device has all 64 slots live and some other has 8; the rest are skewed toward few live slots.
All inputs are finite; a program needn't handle non-finite values.
Results may differ from a plain program's by a relative error of at most 0.0003.
Values sent between devices are 32-bit elements; how exact they have to be, the bound alone decides.
No kernel may reach another device: no remote copies, remote signals or barrier semaphores. Data moves between devices by JAX's collectives and lax.ppermute only.
A program may use at most 64 MiB of HBM per device.

v0:
```python
import jax
import jax.numpy as jnp
from jax import lax
from jax.sharding import PartitionSpec as P

root_two_pi = 0.7978845608028654
cubic = 0.044715


def gelu_parts(z):
    inner = root_two_pi * (z + cubic * z * z * z)
    slope_t = jnp.tanh(inner)
    value = 0.5 * z * (1.0 + slope_t)
    slope = 0.5 * (1.0 + slope_t) + 0.5 * z * (1.0 - slope_t * slope_t) * root_two_pi * (
        1.0 + 3.0 * cubic * z * z
    )
    return (value, slope)


def body(features, adjacency_tiles, tile_rows, tile_cols, tile_count, weight, cotangent):
    highest = lax.Precision.HIGHEST
    nodes_dev, width = features.shape
    slots, tile, _ = adjacency_tiles.shape
    row_tiles = lax.axis_size("col") * nodes_dev // tile
    gathered = lax.all_gather(features, "row", axis=0, tiled=True)
    blocks = gathered.reshape(-1, tile, width)
    live = (jnp.arange(slots, dtype=jnp.int32) < tile_count[0]).astype(jnp.float32)
    chosen = blocks[tile_cols]
    prods = jnp.einsum("sij,sjf->sif", adjacency_tiles, chosen, precision=highest)
    selector = (tile_rows[None, :] == jnp.arange(row_tiles, dtype=jnp.int32)[:, None]).astype(
        jnp.float32
    ) * live[None, :]
    flat = prods.reshape(slots, tile * width)
    partial_value = jnp.dot(selector, flat, precision=highest).reshape(row_tiles * tile, width)
    aggregated = lax.psum_scatter(partial_value, "col", scatter_dimension=0, tiled=True)
    pre = jnp.dot(aggregated, weight, precision=highest)
    activated, slope = gelu_parts(pre)
    grad_pre = cotangent * slope
    local_grad = lax.dot_general(aggregated, grad_pre, (((0,), (0,)), ((), ())), precision=highest)
    weight_grad = lax.psum(local_grad, ("row", "col"))
    return (activated, weight_grad)


def solution(mesh):
    placed = (
        P(("row", "col"), None),
        P(("row", "col"), None, None),
        P(("row", "col")),
        P(("row", "col")),
        P(("row", "col")),
        P(),
        P(("row", "col"), None),
    )
    return jax.shard_map(
        body, mesh=mesh, in_specs=placed, out_specs=(P(("row", "col"), None), P()), check_vma=False
    )
```

profile of v0, /device:TPU:1, one launch (start us, length us, event | category | flops | bytes accessed | tf_op | source)
XLA Modules:
  0.0 616.2 jit_solution(6345813075010275557)
XLA Ops:
  7.2 0.0 copy-start
  7.2 0.0 all-gather.2.cloned.1.call-start
  7.2 0.7 all-gather.2.cloned.1.call-update
  7.9 0.0 reduce-scatter.2.cloned.1.call-start
  8.6 0.7 compare_select_fusion
  9.3 46.3 %all-gather.2.cloned.1.call-done = f32[2048,256]{1,0:T(8,128)} async-done(((f32[128,256]{1,0:T(8,128)}), f32[2048,256]{1,0:T(8,128)}) %all-gather.2.cloned.1.call-update) | async-done | bytes 2097168 | tf_op jit(solution)/shard_map/all_gather | solution.py:25
  55.6 5.9 gather_fusion
  61.5 19.6 %convolution_bitcast_fusion = f32[64,128,256]{1,2,0:T(8,128)} fusion(f32[64,128,256]{2,1,0:T(8,128)} %gather_fusion, f32[64,128,128]{2,1,0:T(8,128)} %param.8), kind=kOutput, calls=%fused_computation.1 | convolution fusion | flops 3221225472 | bytes 20971520 | tf_op jit(solution)/shard_map/sij,sjf->sif/dot_general | solution.py:29
  81.1 0.0 copy-start.1
  81.1 9.2 %copy.12 = f32[8,8,128,256]{3,1,2,0:T(8,128)} copy(f32[8,8,128,256]{2,3,1,0:T(8,128)} %bitcast.16) | data formatting | bytes 16777216
  90.3 0.0 copy-done.1
  90.3 7.7 %fusion.21 = f32[32,32768]{1,0:T(8,128)} fusion(f32[64,32768]{1,0:T(8,128)} %bitcast.15, f32[64]{0:T(128)S(1)} %compare_convert_fusion, s32[64]{0:T(128)S(1)} %copy-done.1), kind=kOutput, calls=%fused_computation.24 | convolution fusion | flops 805310464 | bytes 12583424 | tf_op jit(solution)/shard_map/dot_general | solution.py:34
  98.0 0.0 copy-start.2
  98.0 4.9 reshape.21
  102.9 0.0 reduce-scatter.2.cloned.1.call-update
  102.9 0.0 all-reduce.2.cloned.1.call-start
  103.0 229.4 %reduce-scatter.2.cloned.1.call-done = f32[128,256]{1,0:T(8,128)} async-done(((f32[4096,256]{1,0:T(8,128)}), f32[128,256]{1,0:T(8,128)}) %reduce-scatter.2.cloned.1.call-update) | async-done | bytes 131088 | tf_op jit(solution)/shard_map/reduce_scatter | solution.py:35
  332.3 0.0 copy-done
  332.3 1.9 add_multiply_fusion
  334.2 0.0 copy-done.2
  334.2 2.1 fusion.6
  336.3 0.0 all-reduce.2.cloned.1.call-update
  336.3 271.7 %all-reduce.2.cloned.1.call-done = f32[256,256]{1,0:T(8,128)} async-done(((f32[256,256]{1,0:T(8,128)}), f32[256,256]{1,0:T(8,128)}) %all-reduce.2.cloned.1.call-update) | async-done | bytes 262160 | tf_op jit(solution)/shard_map/psum | solution.py:40
  608.0 1.7 copy.16
  (2 shorter events, 0.0 us)
Async XLA Ops:
  7.2 325.2 %copy-start = (f32[256,256]{1,0:T(8,128)S(1)}, f32[256,256]{1,0:T(8,128)}, u32[]{:S(2)}) copy-start(f32[256,256]{1,0:T(8,128)} %param.12) | copy-start | bytes 786436
  7.2 48.4 %all-gather.2.cloned.1.call-start = ((), (), s32[]{:S(2)}) async-start(), calls=%async_computation.1 | async-start | bytes 2228224 | tf_op jit(solution)/shard_map/all_gather | solution.py:25
  7.9 324.4 %reduce-scatter.2.cloned.1.call-start = ((), (), s32[]{:S(2)}) async-start(), calls=%async_computation.2 | async-start | bytes 4325376 | tf_op jit(solution)/shard_map/reduce_scatter | solution.py:35
  81.1 9.2 %copy-start.1 = (s32[64]{0:T(128)S(1)}, s32[64]{0:T(128)}, u32[]{:S(2)}) copy-start(s32[64]{0:T(128)} %param.9) | copy-start | bytes 772
  98.0 236.2 %copy-start.2 = (f32[128,256]{1,0:T(8,128)S(1)}, f32[128,256]{1,0:T(8,128)}, u32[]{:S(2)}) copy-start(f32[128,256]{1,0:T(8,128)} %param.13) | copy-start | bytes 393220
  102.9 505.1 %all-reduce.2.cloned.1.call-start = ((), (), s32[]{:S(2)}) async-start(), calls=%async_computation.3 | async-start | bytes 524288 | tf_op jit(solution)/shard_map/psum | solution.py:40
Sparse Core Ops, SparseCore 0:
  10.2 45.3 all-gather.1
  103.0 229.2 reduce-scatter.1
  338.7 269.2 all-reduce.1
where the time goes:
time: 617 us; the launch traced here: 616 us
  waiting for transfers between devices  548 us (89%)
  matrix products  31.2 us (5%)
  local copies, waits for them, and re-layouts  21.7 us (4%)
  between operations  14.4 us (2%)
    psum x1, waiting for transfers between devices, body(): weight_grad = lax.psum(local_grad, ('row', 'col'))  272 us
    reduce_scatter x1, waiting for transfers between devices, body(): lax.psum_scatter(partial_value, 'col', scatter_dimension=0, tiled=True)  229 us
    all_gather x1, waiting for transfers between devices, body(): gathered = lax.all_gather(features, 'row', axis=0, tiled=True)  46.3 us
    dot_general x1, matrix products, body(): jnp.einsum('sij,sjf->sif', adjacency_tiles, chosen, precision=highest)  19.6 us
  transfers between devices with their start and end apart: 3, of which 3 were waited for; matrix products, arithmetic and copies ran while one was open for 0% of the time, Pallas kernels for 0%

commit v1 on v0

v1 whole, which is shorter than its diff:
```python
import functools

import jax
import jax.numpy as jnp
from jax import lax
from jax.experimental import pallas as pl
from jax.experimental.pallas import tpu as pltpu
from jax.sharding import Mesh, PartitionSpec as P

root_two_pi = 0.7978845608028654
cubic = 0.044715

AXES = ("x", "zl", "c", "yh", "yl", "zh")
SIZES = (4, 2, 2, 4, 2, 4)
NX, NZL, NC, _, _, NZH = SIZES
RING = ("yh", "yl")
NY = 8
ROUNDS = NY // 2
LANES = 128
GROUP = 4
NEAR = ("x", "zl", "c", "yl")
FAR = ("yh", "zh")
NEAR_SIZE = 32


def halves(v):
    high = v.astype(jnp.bfloat16)
    return high, (v - high.astype(jnp.float32)).astype(jnp.bfloat16)


def dot3(a, b, dims):
    ah, al = halves(a)
    bh, bl = halves(b)

    def one(u, v):
        return lax.dot_general(u, v, (dims, ((), ())), preferred_element_type=jnp.float32)

    return one(ah, bh) + (one(al, bh) + one(ah, bl))


def gelu_parts(z):
    inner = root_two_pi * (z + cubic * z * z * z)
    slope_t = jnp.tanh(inner)
    value = 0.5 * z * (1.0 + slope_t)
    slope = 0.5 * (1.0 + slope_t) + 0.5 * z * (1.0 - slope_t * slope_t) * root_two_pi * (
        1.0 + 3.0 * cubic * z * z
    )
    return (value, slope)


def trade(v, axis, way):
    n = lax.axis_size(axis)
    return lax.ppermute(v, axis, [(k, (k + 1 - 2 * ((k + way) % 2)) % n) for k in range(n)])


def ahead(place, axis):
    n = lax.axis_size(axis)
    me = lax.axis_index(axis)
    return lax.rem((1 - 2 * (me % 2)) * (place - me) + n, n)


def swap(v, axes):
    return lax.all_to_all(v, axes, split_axis=0, concat_axis=0, tiled=True)


def share(v, axes):
    return swap(jnp.broadcast_to(v[None], (lax.axis_size(axes),) + v.shape), axes)


def slot_plan(tile_rows, tile_cols, tile_count):
    ids = jnp.arange(tile_rows.shape[0], dtype=jnp.int32)
    place = ahead(tile_rows // NZH, RING) * NZH + ahead(tile_rows % NZH, "zh")
    place = jnp.where(ids < tile_count[0], place, NY * NZH)
    core = lax.rem(tile_cols % NC + lax.axis_index("c"), NC)
    return place * 16 + core * (NX * NZL) + tile_cols // NC


def split_kernel(tiles_ref, out_ref):
    for k in range(tiles_ref.shape[0]):
        out_ref[k] = jnp.concatenate(halves(tiles_ref[k]), axis=1)


def split_tiles(tiles):
    slots, tile, _ = tiles.shape
    step = 8
    return pl.pallas_call(
        split_kernel,
        grid=(slots // step,),
        out_shape=jax.ShapeDtypeStruct((slots, tile, 2 * tile), jnp.bfloat16),
        in_specs=[pl.BlockSpec((step, tile, tile), lambda k: (k, 0, 0))],
        out_specs=pl.BlockSpec((step, tile, 2 * tile), lambda k: (k, 0, 0)),
        compiler_params=pltpu.CompilerParams(vmem_limit_bytes=8 * 1024 * 1024),
        cost_estimate=pl.CostEstimate(flops=4 * 10**6, bytes_accessed=8 * 2**20, transcendentals=0),
    )(tiles)


def product_kernel(half, count_ref, plan_ref, left_ref, own_ref, other_ref, out_ref, pairs):
    blocks = own_ref.shape[0]
    lanes = slice(half * LANES, (half + 1) * LANES)
    for k, source in enumerate((own_ref, other_ref)):
        for b in range(blocks):
            pairs[k * blocks + b] = jnp.concatenate(halves(source[b, :, lanes]), axis=1)
    out_ref[...] = jnp.zeros_like(out_ref)

    @pl.loop(0, (count_ref[0] + GROUP - 1) // GROUP)
    def _(step):
        values = []
        for k in range(GROUP):
            slot = step * GROUP + k
            plan = plan_ref[slot]
            pair = pairs[plan % 16]
            value = jnp.dot(
                left_ref[slot],
                jnp.concatenate([pair, pair], axis=0),
                preferred_element_type=jnp.float32,
            )
            values.append((plan // 16, value[:, :LANES] + value[:, LANES:]))
        for place, value in values:
            out_ref[place] += value


def products(half, count, plan, left, own, other):
    slots, tile, _ = left.shape
    smem = pl.BlockSpec(memory_space=pltpu.SMEM)
    vmem = pl.BlockSpec(memory_space=pltpu.VMEM)
    return pl.pallas_call(
        functools.partial(product_kernel, half),
        out_shape=jax.ShapeDtypeStruct((NY * NZH + 1, tile, LANES), jnp.float32),
        in_specs=[smem, smem, vmem, vmem, vmem],
        out_specs=vmem,
        scratch_shapes=[pltpu.VMEM((NX * NZL * NC, tile, 2 * LANES), jnp.bfloat16)],
        compiler_params=pltpu.CompilerParams(vmem_limit_bytes=20 * 1024 * 1024),
        cost_estimate=pl.CostEstimate(
            flops=8 * slots * tile * tile * LANES, bytes_accessed=8 * 2**20, transcendentals=0
        ),
    )(count, plan, left, own, other)


def node_kernel(*refs):
    *terms, weight_ref, cot_ref, act_ref, grad_ref = refs
    agg = jnp.concatenate([(t[0][...] + t[1][...]) + t[2][...] for t in (terms[:3], terms[3:])], axis=1)
    pre = dot3(agg, weight_ref[...], ((1,), (0,)))
    value, slope = gelu_parts(pre)
    act_ref[...] = value
    grad = dot3(agg, cot_ref[...] * slope, ((0,), (0,)))
    rows = grad.shape[0] // NEAR_SIZE
    for r in range(NEAR_SIZE):
        for h in range(2):
            grad_ref[r, h] = grad[rows * r : rows * (r + 1), h * LANES : (h + 1) * LANES]


def node_step(terms, weight, cotangent):
    vmem = pl.BlockSpec(memory_space=pltpu.VMEM)
    return pl.pallas_call(
        node_kernel,
        out_shape=(
            jax.ShapeDtypeStruct(cotangent.shape, jnp.float32),
            jax.ShapeDtypeStruct((NEAR_SIZE, 2, weight.shape[0] // NEAR_SIZE, LANES), jnp.float32),
        ),
        in_specs=[vmem] * (len(terms) + 2),
        out_specs=(vmem, vmem),
        compiler_params=pltpu.CompilerParams(vmem_limit_bytes=8 * 1024 * 1024),
    )(*terms, weight, cotangent)


def after(values, witness):
    here = lax.optimization_barrier((*(v for v in values if v is not None), witness))
    return [None if v is None else here[sum(u is not None for u in values[:k])] for k, v in enumerate(values)]


def chunk(sums, ahead):
    return sums[ahead * NZH : (ahead + 1) * NZH]


def advance(sums, step, got):
    pair = [chunk(sums, ROUNDS - step), chunk(sums, (ROUNDS + step) % NY)]
    if step == ROUNDS:
        return pair[0] + (got[0] + got[1])
    return [v if g is None else v + g for v, g in zip(pair, got[::-1])]


def send(pair):
    return trade(pair[0], RING, 0), trade(pair[1], RING, 1)


def spread(own, first):
    got = trade(own[2], "zh", first)
    direct = trade(own[1 + 2 * first], "zh", first)
    return own[0], direct, trade(own[3 - 2 * first] + got, "zh", 1 - first)


def body(features, adjacency_tiles, tile_rows, tile_cols, tile_count, weight, cotangent):
    plan = slot_plan(tile_rows, tile_cols, tile_count)
    own = share(features, ("x", "zl"))
    other = lax.ppermute(own, "c", [(0, 1), (1, 0)])
    arrays = (tile_count, plan, split_tiles(adjacency_tiles), own, other)
    sums_a = products(0, *arrays)
    out_a = chunk(sums_a, ROUNDS)
    got_a = (trade(out_a, RING, 0), None)
    sums_b = products(1, *arrays)
    out_b = [chunk(sums_b, ROUNDS)]
    got_b = (None, trade(out_b[0], RING, 1))
    for step in range(1, ROUNDS):
        out_a = advance(sums_a, step, after(got_a, out_b[0]))
        got_a = send(out_a)
        out_b = advance(sums_b, step, after(got_b, out_a[0]))
        got_b = send(out_b)
    last_a = advance(sums_a, ROUNDS, after(got_a, out_b[0]))
    terms = spread(last_a, 0)
    last_b = advance(sums_b, ROUNDS, after(got_b, last_a))
    terms += spread(last_b, 1)
    activated, grad = node_step(terms, weight, cotangent)
    grad = jnp.sum(swap(grad, NEAR), axis=0)
    grad = jnp.sum(share(grad, FAR), axis=0)
    grad = share(grad, NEAR)
    width = weight.shape[0]
    weight_grad = grad.swapaxes(1, 2).reshape(width, width)
    return (activated, weight_grad)


def solution(mesh):
    split = Mesh(mesh.devices.reshape(SIZES), AXES)
    placed = (P(AXES, None), P(AXES, None, None), P(AXES), P(AXES), P(AXES), P(), P(AXES, None))
    return jax.shard_map(
        body, mesh=split, in_specs=placed, out_specs=(P(AXES, None), P()), check_vma=False
    )
```

time: 617 us -> 163 us (0.26)
  waiting for transfers between devices: 548 us -> 4.09 us
  starting transfers between devices: 0.12 us -> 78.9 us
  blocking collectives: 0 us -> 67.5 us
  matrix products: 31.2 us -> 0 us
  local copies, waits for them, and re-layouts: 21.7 us -> 4.03 us
  between operations: 14.4 us -> 1.78 us
    psum x1 -> x0, waiting for transfers between devices: 272 us -> none  [body(): weight_grad = lax.psum(local_grad, ('row', 'col'))]
    reduce_scatter x1 -> x0, waiting for transfers between devices: 229 us -> none  [body(): lax.psum_scatter(partial_value, 'col', scatter_dimension=0, tiled=True)]
    ppermute x0 -> x21, starting transfers between devices: none -> 78.9 us  [the longest x20 73.2 us: trade(): lax.ppermute(v, axis, [(k, (k + 1 - 2 * ((k + way) % 2)) % n) for k in ra...]
    all_to_all x0 -> x4, blocking collectives: none -> 67.5 us  [swap(): return lax.all_to_all(v, axes, split_axis=0, concat_axis=0, tiled=True)]
    all_gather x1 -> x0, waiting for transfers between devices: 46.3 us -> none  [body(): gathered = lax.all_gather(features, 'row', axis=0, tiled=True)]
    dot_general x4 -> x0, matrix products: 31.2 us -> none  [the longest x1 19.6 us: body(): jnp.einsum('sij,sjf->sif', adjacency_tiles, chosen, precision=highest)]
    unnamed x8 -> x11, local copies, waits for them, and re-layouts: 10.9 us -> 2.95 us
  transfers between devices with their start and end apart: 3 -> 21, of which waited for: 3 -> 1; matrix products, arithmetic and copies ran while one was open for 0% -> 0% of each run, Pallas kernels for 0% -> 2%
where the time goes in v1:
time: 163 us
  starting transfers between devices  78.9 us (48%)
  blocking collectives  67.5 us (41%)
  Pallas kernels  5.69 us (3%)
  waiting for transfers between devices  4.09 us (3%)
  local copies, waits for them, and re-layouts  4.03 us (2%)
  between operations  1.78 us (1%)
    ppermute x20, starting transfers between devices, trade(): lax.ppermute(v, axis, [(k, (k + 1 - 2 * ((k + way) % 2)) % n) for k in ra...  73.2 us
    all_to_all x4, blocking collectives, swap(): return lax.all_to_all(v, axes, split_axis=0, concat_axis=0, tiled=True)  67.5 us
    ppermute x1, starting transfers between devices, body(): other = lax.ppermute(own, 'c', [(0, 1), (1, 0)])  5.67 us
    pallas_call x2, Pallas kernels, products(): pl.pallas_call(functools.partial(product_kernel, half), out_shape=jax.Sha...  4.09 us
    ppermute x20, waiting for transfers between devices, trade(): lax.ppermute(v, axis, [(k, (k + 1 - 2 * ((k + way) % 2)) % n) for k in ra...  4.08 us
  transfers between devices with their start and end apart: 21, of which 1 were waited for; matrix products, arithmetic and copies ran while one was open for 0% of the time, Pallas kernels for 2%

profile of v1, /device:TPU:1, one launch (start us, length us, event | category | flops | bytes accessed | tf_op | source)
XLA Modules:
  0.0 162.5 jit_solution(5150452375329311938)
XLA Ops:
  0.6 1.0 broadcast_in_dim.11
  1.6 19.3 %all_to_all.20.own_ref = f32[8,128,256]{2,1,0:T(8,128)S(1)} all-to-all(f32[8,128,256]{2,1,0:T(8,128)S(1)} %broadcast_in_dim.11), channel_id=1, replica_groups=mesh['x'=4,'zl'=2,'c'=2,'yh'=4,'yl'=2,'zh'=4] {'x','zl'}, dimensions={0} | all-to-all | bytes 2097152 | tf_op jit(solution)/shard_map/all_to_all | solution.py:63
  21.0 5.7 %collective-permute-start = (f32[8,128,256]{2,1,0:T(8,128)S(1)}, f32[8,128,256]{2,1,0:T(8,128)S(1)}, u32[]{:S(2)}, u32[]{:S(2)}) collective-permute-start(f32[8,128,256]{2,1,0:T(8,128)S(1)} %all_to_all.20.own_ref), channel_id=1, source_target_pairs={{0,32},{32,0},{1,33},{33,1},{2,34},{34,2},{3,35},{35,3},{4,36},{36... | collective-permute-start | bytes 3145736 | tf_op jit(solution)/shard_map/ppermute | solution.py:195
  27.3 2.2 %copy-done = f32[64,128,128]{2,1,0:T(8,128)S(1)} copy-done((f32[64,128,128]{2,1,0:T(8,128)S(1)}, f32[64,128,128]{2,1,0:T(8,128)}, u32[]{:S(2)}) %copy-start) | copy-done | bytes 4194328
  30.2 2.0 %shard_map.87 = f32[33,128,128]{2,1,0:T(8,128)S(1)} custom-call(s32[1]{0:T(128)} %copy.10.count_ref, s32[64]{0:T(128)S(1)} %fusion.14.plan_ref, bf16[64,128,256]{2,1,0:T(8,128)(2,1)S(1)} %shard_map.86.left_ref, f32[8,128,256]{2,1,0:T(8,128)S(1)} %all_to_all.20.own_ref, f32[8,128,256]{2,1,0:T(8,128)S(1)} %collective-permute-done.other_ref), custom_call_target="tpu_custom_call" | custom-call | flops 1073741824 | bytes 8388608 | tf_op jit(solution)/shard_map/pallas_call | solution.py:126
  32.3 3.8 %collective-permute-start.2 = (f32[4,128,128]{2,1,0:T(8,128)S(1)}, f32[4,128,128]{2,1,0:T(8,128)S(1)}, u32[]{:S(2)}, u32[]{:S(2)}) collective-permute-start(f32[4,128,128]{2,1,0:T(8,128)S(1)} %slice.101), channel_id=1, source_target_pairs={{0,4},{4,0},{8,12},{12,8},{16,20},{20,16},{24,28},{28,24},{1,5},{5... | collective-permute-start | bytes 786440 | tf_op jit(solution)/shard_map/ppermute | solution.py:53
  36.1 2.0 %shard_map.88 = f32[33,128,128]{2,1,0:T(8,128)S(1)} custom-call(s32[1]{0:T(128)} %copy.10.count_ref, s32[64]{0:T(128)S(1)} %fusion.14.plan_ref, bf16[64,128,256]{2,1,0:T(8,128)(2,1)S(1)} %shard_map.86.left_ref, f32[8,128,256]{2,1,0:T(8,128)S(1)} %all_to_all.20.own_ref, f32[8,128,256]{2,1,0:T(8,128)S(1)} %collective-permute-done.other_ref), custom_call_target="tpu_custom_call" | custom-call | flops 1073741824 | bytes 8388608 | tf_op jit(solution)/shard_map/pallas_call | solution.py:126
  38.2 4.6 %collective-permute-start.4 = (f32[4,128,128]{2,1,0:T(8,128)S(1)}, f32[4,128,128]{2,1,0:T(8,128)S(1)}, u32[]{:S(2)}, u32[]{:S(2)}) collective-permute-start(f32[4,128,128]{2,1,0:T(8,128)S(1)} %slice.102), channel_id=1, source_target_pairs={{0,28},{4,8},{8,4},{12,16},{16,12},{20,24},{24,20},{28,0},{1,29},{... | collective-permute-start | bytes 786440 | tf_op jit(solution)/shard_map/ppermute | solution.py:53
  42.9 4.1 %collective-permute-start.3 = (f32[4,128,128]{2,1,0:T(8,128)S(1)}, f32[4,128,128]{2,1,0:T(8,128)S(1)}, u32[]{:S(2)}, u32[]{:S(2)}) collective-permute-start(f32[4,128,128]{2,1,0:T(8,128)S(1)} %get-tuple-element.44), channel_id=1, source_target_pairs={{0,28},{4,8},{8,4},{12,16},{16,12},{20,24},{24,20},{28,0},{1,29},{... | collective-permute-start | bytes 786440 | tf_op jit(solution)/shard_map/ppermute | solution.py:53
  47.0 1.9 %collective-permute-start.1 = (f32[4,128,128]{2,1,0:T(8,128)S(1)}, f32[4,128,128]{2,1,0:T(8,128)S(1)}, u32[]{:S(2)}, u32[]{:S(2)}) collective-permute-start(f32[4,128,128]{2,1,0:T(8,128)S(1)} %get-tuple-element.45), channel_id=1, source_target_pairs={{0,4},{4,0},{8,12},{12,8},{16,20},{20,16},{24,28},{28,24},{1,5},{5... | collective-permute-start | bytes 786440 | tf_op jit(solution)/shard_map/ppermute | solution.py:53
  49.0 4.9 %collective-permute-start.8 = (f32[4,128,128]{2,1,0:T(8,128)S(1)}, f32[4,128,128]{2,1,0:T(8,128)S(1)}, u32[]{:S(2)}, u32[]{:S(2)}) collective-permute-start(f32[4,128,128]{2,1,0:T(8,128)S(1)} %get-tuple-element.40), channel_id=1, source_target_pairs={{0,28},{4,8},{8,4},{12,16},{16,12},{20,24},{24,20},{28,0},{1,29},{... | collective-permute-start | bytes 786440 | tf_op jit(solution)/shard_map/ppermute | solution.py:53
  53.9 3.6 %collective-permute-start.7 = (f32[4,128,128]{2,1,0:T(8,128)S(1)}, f32[4,128,128]{2,1,0:T(8,128)S(1)}, u32[]{:S(2)}, u32[]{:S(2)}) collective-permute-start(f32[4,128,128]{2,1,0:T(8,128)S(1)} %get-tuple-element.41), channel_id=1, source_target_pairs={{0,4},{4,0},{8,12},{12,8},{16,20},{20,16},{24,28},{28,24},{1,5},{5... | collective-permute-start | bytes 786440 | tf_op jit(solution)/shard_map/ppermute | solution.py:53
  57.6 3.0 %collective-permute-start.6 = (f32[4,128,128]{2,1,0:T(8,128)S(1)}, f32[4,128,128]{2,1,0:T(8,128)S(1)}, u32[]{:S(2)}, u32[]{:S(2)}) collective-permute-start(f32[4,128,128]{2,1,0:T(8,128)S(1)} %get-tuple-element.42), channel_id=1, source_target_pairs={{0,28},{4,8},{8,4},{12,16},{16,12},{20,24},{24,20},{28,0},{1,29},{... | collective-permute-start | bytes 786440 | tf_op jit(solution)/shard_map/ppermute | solution.py:53
  60.7 3.6 %collective-permute-start.5 = (f32[4,128,128]{2,1,0:T(8,128)S(1)}, f32[4,128,128]{2,1,0:T(8,128)S(1)}, u32[]{:S(2)}, u32[]{:S(2)}) collective-permute-start(f32[4,128,128]{2,1,0:T(8,128)S(1)} %get-tuple-element.43), channel_id=1, source_target_pairs={{0,4},{4,0},{8,12},{12,8},{16,20},{20,16},{24,28},{28,24},{1,5},{5... | collective-permute-start | bytes 786440 | tf_op jit(solution)/shard_map/ppermute | solution.py:53
  64.3 3.1 %collective-permute-start.12 = (f32[4,128,128]{2,1,0:T(8,128)S(1)}, f32[4,128,128]{2,1,0:T(8,128)S(1)}, u32[]{:S(2)}, u32[]{:S(2)}) collective-permute-start(f32[4,128,128]{2,1,0:T(8,128)S(1)} %get-tuple-element.36), channel_id=1, source_target_pairs={{0,28},{4,8},{8,4},{12,16},{16,12},{20,24},{24,20},{28,0},{1,29},{... | collective-permute-start | bytes 786440 | tf_op jit(solution)/shard_map/ppermute | solution.py:53
  67.5 2.9 %collective-permute-start.11 = (f32[4,128,128]{2,1,0:T(8,128)S(1)}, f32[4,128,128]{2,1,0:T(8,128)S(1)}, u32[]{:S(2)}, u32[]{:S(2)}) collective-permute-start(f32[4,128,128]{2,1,0:T(8,128)S(1)} %get-tuple-element.37), channel_id=1, source_target_pairs={{0,4},{4,0},{8,12},{12,8},{16,20},{20,16},{24,28},{28,24},{1,5},{5... | collective-permute-start | bytes 786440 | tf_op jit(solution)/shard_map/ppermute | solution.py:53
  70.4 3.9 %collective-permute-start.10 = (f32[4,128,128]{2,1,0:T(8,128)S(1)}, f32[4,128,128]{2,1,0:T(8,128)S(1)}, u32[]{:S(2)}, u32[]{:S(2)}) collective-permute-start(f32[4,128,128]{2,1,0:T(8,128)S(1)} %get-tuple-element.38), channel_id=1, source_target_pairs={{0,28},{4,8},{8,4},{12,16},{16,12},{20,24},{24,20},{28,0},{1,29},{... | collective-permute-start | bytes 786440 | tf_op jit(solution)/shard_map/ppermute | solution.py:53
  74.3 2.9 %collective-permute-start.9 = (f32[4,128,128]{2,1,0:T(8,128)S(1)}, f32[4,128,128]{2,1,0:T(8,128)S(1)}, u32[]{:S(2)}, u32[]{:S(2)}) collective-permute-start(f32[4,128,128]{2,1,0:T(8,128)S(1)} %get-tuple-element.39), channel_id=1, source_target_pairs={{0,4},{4,0},{8,12},{12,8},{16,20},{20,16},{24,28},{28,24},{1,5},{5... | collective-permute-start | bytes 786440 | tf_op jit(solution)/shard_map/ppermute | solution.py:53
  77.3 2.8 %collective-permute-start.17 = (f32[4,128,128]{2,1,0:T(8,128)S(1)}, f32[4,128,128]{2,1,0:T(8,128)S(1)}, u32[]{:S(2)}, u32[]{:S(2)}) collective-permute-start(f32[4,128,128]{2,1,0:T(8,128)S(1)} %get-tuple-element.34), channel_id=1, source_target_pairs={{0,28},{4,8},{8,4},{12,16},{16,12},{20,24},{24,20},{28,0},{1,29},{... | collective-permute-start | bytes 786440 | tf_op jit(solution)/shard_map/ppermute | solution.py:53
  80.2 3.0 %collective-permute-start.16 = (f32[4,128,128]{2,1,0:T(8,128)S(1)}, f32[4,128,128]{2,1,0:T(8,128)S(1)}, u32[]{:S(2)}, u32[]{:S(2)}) collective-permute-start(f32[4,128,128]{2,1,0:T(8,128)S(1)} %get-tuple-element.35), channel_id=1, source_target_pairs={{0,4},{4,0},{8,12},{12,8},{16,20},{20,16},{24,28},{28,24},{1,5},{5... | collective-permute-start | bytes 786440 | tf_op jit(solution)/shard_map/ppermute | solution.py:53
  83.3 5.7 %collective-permute-start.14 = (f32[128,128]{1,0:T(8,128)S(1)}, f32[128,128]{1,0:T(8,128)S(1)}, u32[]{:S(2)}, u32[]{:S(2)}) collective-permute-start(f32[128,128]{1,0:T(8,128)S(1)} %get-tuple-element.49), channel_id=1, source_target_pairs={{0,1},{1,0},{2,3},{3,2},{4,5},{5,4},{6,7},{7,6},{8,9},{9,8},{10,11... | collective-permute-start | bytes 196616 | tf_op jit(solution)/shard_map/ppermute | solution.py:53
  89.0 1.9 %collective-permute-start.13 = (f32[128,128]{1,0:T(8,128)S(1)}, f32[128,128]{1,0:T(8,128)S(1)}, u32[]{:S(2)}, u32[]{:S(2)}) collective-permute-start(f32[128,128]{1,0:T(8,128)S(1)} %get-tuple-element.50), channel_id=1, source_target_pairs={{0,1},{1,0},{2,3},{3,2},{4,5},{5,4},{6,7},{7,6},{8,9},{9,8},{10,11... | collective-permute-start | bytes 196616 | tf_op jit(solution)/shard_map/ppermute | solution.py:53
  91.1 8.1 %collective-permute-start.19 = (f32[128,128]{1,0:T(8,128)S(1)}, f32[128,128]{1,0:T(8,128)S(1)}, u32[]{:S(2)}, u32[]{:S(2)}) collective-permute-start(f32[128,128]{1,0:T(8,128)S(1)} %get-tuple-element.46), channel_id=1, source_target_pairs={{0,3},{1,2},{2,1},{3,0},{4,7},{5,6},{6,5},{7,4},{8,11},{9,10},{10,... | collective-permute-start | bytes 196616 | tf_op jit(solution)/shard_map/ppermute | solution.py:53
  99.2 1.9 %collective-permute-start.18 = (f32[128,128]{1,0:T(8,128)S(1)}, f32[128,128]{1,0:T(8,128)S(1)}, u32[]{:S(2)}, u32[]{:S(2)}) collective-permute-start(f32[128,128]{1,0:T(8,128)S(1)} %get-tuple-element.47), channel_id=1, source_target_pairs={{0,3},{1,2},{2,1},{3,0},{4,7},{5,6},{6,5},{7,4},{8,11},{9,10},{10,... | collective-permute-start | bytes 196616 | tf_op jit(solution)/shard_map/ppermute | solution.py:53
  101.1 5.5 %collective-permute-start.15 = (f32[128,128]{1,0:T(8,128)S(1)}, f32[128,128]{1,0:T(8,128)S(1)}, u32[]{:S(2)}, u32[]{:S(2)}) collective-permute-start(f32[128,128]{1,0:T(8,128)S(1)} %fusion.1), channel_id=1, source_target_pairs={{0,3},{1,2},{2,1},{3,0},{4,7},{5,6},{6,5},{7,4},{8,11},{9,10},{10,... | collective-permute-start | bytes 196616 | tf_op jit(solution)/shard_map/ppermute | solution.py:53
  106.6 1.9 %collective-permute-start.20 = (f32[128,128]{1,0:T(8,128)S(1)}, f32[128,128]{1,0:T(8,128)S(1)}, u32[]{:S(2)}, u32[]{:S(2)}) collective-permute-start(f32[128,128]{1,0:T(8,128)S(1)} %fusion), channel_id=1, source_target_pairs={{0,1},{1,0},{2,3},{3,2},{4,5},{5,4},{6,7},{7,6},{8,9},{9,8},{10,11... | collective-permute-start | bytes 196616 | tf_op jit(solution)/shard_map/ppermute | solution.py:53
  108.6 4.0 %collective-permute-done.20.refs_5_ = f32[128,128]{1,0:T(8,128)S(1)} collective-permute-done((f32[128,128]{1,0:T(8,128)S(1)}, f32[128,128]{1,0:T(8,128)S(1)}, u32[]{:S(2)}, u32[]{:S(2)}) %collective-permute-start.20) | collective-permute-done | bytes 65568 | tf_op jit(solution)/shard_map/ppermute | solution.py:53
  112.6 1.0 shard_map.89
  113.6 18.4 %all_to_all.21 = f32[32,2,8,128]{3,2,1,0:T(8,128)S(1)} all-to-all(f32[32,2,8,128]{3,2,1,0:T(8,128)S(1)} %get-tuple-element.33), channel_id=1, replica_groups=mesh['x'=4,'zl'=2,'c'=2,'yh'=4,'yl'=2,'zh'=4] {'x','zl','c','yl'}, dimensions={0} | all-to-all | bytes 524288 | tf_op jit(solution)/shard_map/all_to_all | solution.py:63
  132.0 16.6 %all_to_all.22 = f32[16,2,8,128]{3,2,1,0:T(8,128)S(1)} all-to-all(f32[16,2,8,128]{3,2,1,0:T(8,128)S(1)} %broadcast_in_dim.12), channel_id=1, replica_groups=mesh['x'=4,'zl'=2,'c'=2,'yh'=4,'yl'=2,'zh'=4] {'yh','zh'}, dimensions={0} | all-to-all | bytes 262144 | tf_op jit(solution)/shard_map/all_to_all | solution.py:63
  148.7 13.1 %all_to_all.23 = f32[32,2,8,128]{3,2,1,0:T(8,128)S(1)} all-to-all(f32[32,2,8,128]{3,2,1,0:T(8,128)S(1)} %broadcast_in_dim.13), channel_id=1, replica_groups=mesh['x'=4,'zl'=2,'c'=2,'yh'=4,'yl'=2,'zh'=4] {'x','zl','c','yl'}, dimensions={0} | all-to-all | bytes 524288 | tf_op jit(solution)/shard_map/all_to_all | solution.py:63
  161.8 0.7 copy.11
  (49 shorter events, 1.4 us)
Async XLA Ops:
  21.0 9.2 %collective-permute-start = (f32[8,128,256]{2,1,0:T(8,128)S(1)}, f32[8,128,256]{2,1,0:T(8,128)S(1)}, u32[]{:S(2)}, u32[]{:S(2)}) collective-permute-start(f32[8,128,256]{2,1,0:T(8,128)S(1)} %all_to_all.20.own_ref), channel_id=1, source_target_pairs={{0,32},{32,0},{1,33},{33,1},{2,34},{34,2},{3,35},{35,3},{4,36},{36... | collective-permute-start | bytes 3145736 | tf_op jit(solution)/shard_map/ppermute | solution.py:195
  27.3 2.2 %copy-start = (f32[64,128,128]{2,1,0:T(8,128)S(1)}, f32[64,128,128]{2,1,0:T(8,128)}, u32[]{:S(2)}) copy-start(f32[64,128,128]{2,1,0:T(8,128)} %tiles_ref.1) | copy-start | bytes 12582916
  29.5 0.7 copy-start.3
  29.5 0.7 copy-start.4
  32.3 10.6 %collective-permute-start.2 = (f32[4,128,128]{2,1,0:T(8,128)S(1)}, f32[4,128,128]{2,1,0:T(8,128)S(1)}, u32[]{:S(2)}, u32[]{:S(2)}) collective-permute-start(f32[4,128,128]{2,1,0:T(8,128)S(1)} %slice.101), channel_id=1, source_target_pairs={{0,4},{4,0},{8,12},{12,8},{16,20},{20,16},{24,28},{28,24},{1,5},{5... | collective-permute-start | bytes 786440 | tf_op jit(solution)/shard_map/ppermute | solution.py:53
  38.2 10.8 %collective-permute-start.4 = (f32[4,128,128]{2,1,0:T(8,128)S(1)}, f32[4,128,128]{2,1,0:T(8,128)S(1)}, u32[]{:S(2)}, u32[]{:S(2)}) collective-permute-start(f32[4,128,128]{2,1,0:T(8,128)S(1)} %slice.102), channel_id=1, source_target_pairs={{0,28},{4,8},{8,4},{12,16},{16,12},{20,24},{24,20},{28,0},{1,29},{... | collective-permute-start | bytes 786440 | tf_op jit(solution)/shard_map/ppermute | solution.py:53
  42.9 14.6 %collective-permute-start.3 = (f32[4,128,128]{2,1,0:T(8,128)S(1)}, f32[4,128,128]{2,1,0:T(8,128)S(1)}, u32[]{:S(2)}, u32[]{:S(2)}) collective-permute-start(f32[4,128,128]{2,1,0:T(8,128)S(1)} %get-tuple-element.44), channel_id=1, source_target_pairs={{0,28},{4,8},{8,4},{12,16},{16,12},{20,24},{24,20},{28,0},{1,29},{... | collective-permute-start | bytes 786440 | tf_op jit(solution)/shard_map/ppermute | solution.py:53
  47.0 10.5 %collective-permute-start.1 = (f32[4,128,128]{2,1,0:T(8,128)S(1)}, f32[4,128,128]{2,1,0:T(8,128)S(1)}, u32[]{:S(2)}, u32[]{:S(2)}) collective-permute-start(f32[4,128,128]{2,1,0:T(8,128)S(1)} %get-tuple-element.45), channel_id=1, source_target_pairs={{0,4},{4,0},{8,12},{12,8},{16,20},{20,16},{24,28},{28,24},{1,5},{5... | collective-permute-start | bytes 786440 | tf_op jit(solution)/shard_map/ppermute | solution.py:53
  49.0 15.2 %collective-permute-start.8 = (f32[4,128,128]{2,1,0:T(8,128)S(1)}, f32[4,128,128]{2,1,0:T(8,128)S(1)}, u32[]{:S(2)}, u32[]{:S(2)}) collective-permute-start(f32[4,128,128]{2,1,0:T(8,128)S(1)} %get-tuple-element.40), channel_id=1, source_target_pairs={{0,28},{4,8},{8,4},{12,16},{16,12},{20,24},{24,20},{28,0},{1,29},{... | collective-permute-start | bytes 786440 | tf_op jit(solution)/shard_map/ppermute | solution.py:53
  53.9 10.3 %collective-permute-start.7 = (f32[4,128,128]{2,1,0:T(8,128)S(1)}, f32[4,128,128]{2,1,0:T(8,128)S(1)}, u32[]{:S(2)}, u32[]{:S(2)}) collective-permute-start(f32[4,128,128]{2,1,0:T(8,128)S(1)} %get-tuple-element.41), channel_id=1, source_target_pairs={{0,4},{4,0},{8,12},{12,8},{16,20},{20,16},{24,28},{28,24},{1,5},{5... | collective-permute-start | bytes 786440 | tf_op jit(solution)/shard_map/ppermute | solution.py:53
  57.6 12.7 %collective-permute-start.6 = (f32[4,128,128]{2,1,0:T(8,128)S(1)}, f32[4,128,128]{2,1,0:T(8,128)S(1)}, u32[]{:S(2)}, u32[]{:S(2)}) collective-permute-start(f32[4,128,128]{2,1,0:T(8,128)S(1)} %get-tuple-element.42), channel_id=1, source_target_pairs={{0,28},{4,8},{8,4},{12,16},{16,12},{20,24},{24,20},{28,0},{1,29},{... | collective-permute-start | bytes 786440 | tf_op jit(solution)/shard_map/ppermute | solution.py:53
  60.7 9.7 %collective-permute-start.5 = (f32[4,128,128]{2,1,0:T(8,128)S(1)}, f32[4,128,128]{2,1,0:T(8,128)S(1)}, u32[]{:S(2)}, u32[]{:S(2)}) collective-permute-start(f32[4,128,128]{2,1,0:T(8,128)S(1)} %get-tuple-element.43), channel_id=1, source_target_pairs={{0,4},{4,0},{8,12},{12,8},{16,20},{20,16},{24,28},{28,24},{1,5},{5... | collective-permute-start | bytes 786440 | tf_op jit(solution)/shard_map/ppermute | solution.py:53
  64.3 12.9 %collective-permute-start.12 = (f32[4,128,128]{2,1,0:T(8,128)S(1)}, f32[4,128,128]{2,1,0:T(8,128)S(1)}, u32[]{:S(2)}, u32[]{:S(2)}) collective-permute-start(f32[4,128,128]{2,1,0:T(8,128)S(1)} %get-tuple-element.36), channel_id=1, source_target_pairs={{0,28},{4,8},{8,4},{12,16},{16,12},{20,24},{24,20},{28,0},{1,29},{... | collective-permute-start | bytes 786440 | tf_op jit(solution)/shard_map/ppermute | solution.py:53
  67.5 9.8 %collective-permute-start.11 = (f32[4,128,128]{2,1,0:T(8,128)S(1)}, f32[4,128,128]{2,1,0:T(8,128)S(1)}, u32[]{:S(2)}, u32[]{:S(2)}) collective-permute-start(f32[4,128,128]{2,1,0:T(8,128)S(1)} %get-tuple-element.37), channel_id=1, source_target_pairs={{0,4},{4,0},{8,12},{12,8},{16,20},{20,16},{24,28},{28,24},{1,5},{5... | collective-permute-start | bytes 786440 | tf_op jit(solution)/shard_map/ppermute | solution.py:53
  70.4 12.8 %collective-permute-start.10 = (f32[4,128,128]{2,1,0:T(8,128)S(1)}, f32[4,128,128]{2,1,0:T(8,128)S(1)}, u32[]{:S(2)}, u32[]{:S(2)}) collective-permute-start(f32[4,128,128]{2,1,0:T(8,128)S(1)} %get-tuple-element.38), channel_id=1, source_target_pairs={{0,28},{4,8},{8,4},{12,16},{16,12},{20,24},{24,20},{28,0},{1,29},{... | collective-permute-start | bytes 786440 | tf_op jit(solution)/shard_map/ppermute | solution.py:53
  74.3 38.3 %copy-start.1 = (f32[256,256]{1,0:T(8,128)S(1)}, f32[256,256]{1,0:T(8,128)}, u32[]{:S(2)}) copy-start(f32[256,256]{1,0:T(8,128)} %refs_6_.1) | copy-start | bytes 786436
  74.3 38.3 %copy-start.2 = (f32[128,256]{1,0:T(8,128)S(1)}, f32[128,256]{1,0:T(8,128)}, u32[]{:S(2)}) copy-start(f32[128,256]{1,0:T(8,128)} %refs_7_.1) | copy-start | bytes 393220
  74.3 8.9 %collective-permute-start.9 = (f32[4,128,128]{2,1,0:T(8,128)S(1)}, f32[4,128,128]{2,1,0:T(8,128)S(1)}, u32[]{:S(2)}, u32[]{:S(2)}) collective-permute-start(f32[4,128,128]{2,1,0:T(8,128)S(1)} %get-tuple-element.39), channel_id=1, source_target_pairs={{0,4},{4,0},{8,12},{12,8},{16,20},{20,16},{24,28},{28,24},{1,5},{5... | collective-permute-start | bytes 786440 | tf_op jit(solution)/shard_map/ppermute | solution.py:53
  77.3 13.6 %collective-permute-start.17 = (f32[4,128,128]{2,1,0:T(8,128)S(1)}, f32[4,128,128]{2,1,0:T(8,128)S(1)}, u32[]{:S(2)}, u32[]{:S(2)}) collective-permute-start(f32[4,128,128]{2,1,0:T(8,128)S(1)} %get-tuple-element.34), channel_id=1, source_target_pairs={{0,28},{4,8},{8,4},{12,16},{16,12},{20,24},{24,20},{28,0},{1,29},{... | collective-permute-start | bytes 786440 | tf_op jit(solution)/shard_map/ppermute | solution.py:53
  80.2 10.8 %collective-permute-start.16 = (f32[4,128,128]{2,1,0:T(8,128)S(1)}, f32[4,128,128]{2,1,0:T(8,128)S(1)}, u32[]{:S(2)}, u32[]{:S(2)}) collective-permute-start(f32[4,128,128]{2,1,0:T(8,128)S(1)} %get-tuple-element.35), channel_id=1, source_target_pairs={{0,4},{4,0},{8,12},{12,8},{16,20},{20,16},{24,28},{28,24},{1,5},{5... | collective-permute-start | bytes 786440 | tf_op jit(solution)/shard_map/ppermute | solution.py:53
  83.3 17.7 %collective-permute-start.14 = (f32[128,128]{1,0:T(8,128)S(1)}, f32[128,128]{1,0:T(8,128)S(1)}, u32[]{:S(2)}, u32[]{:S(2)}) collective-permute-start(f32[128,128]{1,0:T(8,128)S(1)} %get-tuple-element.49), channel_id=1, source_target_pairs={{0,1},{1,0},{2,3},{3,2},{4,5},{5,4},{6,7},{7,6},{8,9},{9,8},{10,11... | collective-permute-start | bytes 196616 | tf_op jit(solution)/shard_map/ppermute | solution.py:53
  89.0 19.5 %collective-permute-start.13 = (f32[128,128]{1,0:T(8,128)S(1)}, f32[128,128]{1,0:T(8,128)S(1)}, u32[]{:S(2)}, u32[]{:S(2)}) collective-permute-start(f32[128,128]{1,0:T(8,128)S(1)} %get-tuple-element.50), channel_id=1, source_target_pairs={{0,1},{1,0},{2,3},{3,2},{4,5},{5,4},{6,7},{7,6},{8,9},{9,8},{10,11... | collective-permute-start | bytes 196616 | tf_op jit(solution)/shard_map/ppermute | solution.py:53
  91.1 15.5 %collective-permute-start.19 = (f32[128,128]{1,0:T(8,128)S(1)}, f32[128,128]{1,0:T(8,128)S(1)}, u32[]{:S(2)}, u32[]{:S(2)}) collective-permute-start(f32[128,128]{1,0:T(8,128)S(1)} %get-tuple-element.46), channel_id=1, source_target_pairs={{0,3},{1,2},{2,1},{3,0},{4,7},{5,6},{6,5},{7,4},{8,11},{9,10},{10,... | collective-permute-start | bytes 196616 | tf_op jit(solution)/shard_map/ppermute | solution.py:53
  99.2 9.4 %collective-permute-start.18 = (f32[128,128]{1,0:T(8,128)S(1)}, f32[128,128]{1,0:T(8,128)S(1)}, u32[]{:S(2)}, u32[]{:S(2)}) collective-permute-start(f32[128,128]{1,0:T(8,128)S(1)} %get-tuple-element.47), channel_id=1, source_target_pairs={{0,3},{1,2},{2,1},{3,0},{4,7},{5,6},{6,5},{7,4},{8,11},{9,10},{10,... | collective-permute-start | bytes 196616 | tf_op jit(solution)/shard_map/ppermute | solution.py:53
  101.1 7.5 %collective-permute-start.15 = (f32[128,128]{1,0:T(8,128)S(1)}, f32[128,128]{1,0:T(8,128)S(1)}, u32[]{:S(2)}, u32[]{:S(2)}) collective-permute-start(f32[128,128]{1,0:T(8,128)S(1)} %fusion.1), channel_id=1, source_target_pairs={{0,3},{1,2},{2,1},{3,0},{4,7},{5,6},{6,5},{7,4},{8,11},{9,10},{10,... | collective-permute-start | bytes 196616 | tf_op jit(solution)/shard_map/ppermute | solution.py:53
  106.6 6.0 %collective-permute-start.20 = (f32[128,128]{1,0:T(8,128)S(1)}, f32[128,128]{1,0:T(8,128)S(1)}, u32[]{:S(2)}, u32[]{:S(2)}) collective-permute-start(f32[128,128]{1,0:T(8,128)S(1)} %fusion), channel_id=1, source_target_pairs={{0,1},{1,0},{2,3},{3,2},{4,5},{5,4},{6,7},{7,6},{8,9},{9,8},{10,11... | collective-permute-start | bytes 196616 | tf_op jit(solution)/shard_map/ppermute | solution.py:53

commit v2 on v1

--- a/solution.py
+++ b/solution.py
@@ -69,7 +69,7 @@
 
 def slot_plan(tile_rows, tile_cols, tile_count):
     ids = jnp.arange(tile_rows.shape[0], dtype=jnp.int32)
-    place = ahead(tile_rows // NZH, RING) * NZH + ahead(tile_rows % NZH, "zh")
+    place = ahead(tile_rows // NZH, RING) * NZH + tile_rows % NZH
     place = jnp.where(ids < tile_count[0], place, NY * NZH)
     core = lax.rem(tile_cols % NC + lax.axis_index("c"), NC)
     return place * 16 + core * (NX * NZL) + tile_cols // NC
@@ -94,51 +94,50 @@
     )(tiles)
 
 
-def product_kernel(half, count_ref, plan_ref, left_ref, own_ref, other_ref, out_ref, pairs):
+def product_kernel(count_ref, plan_ref, left_ref, own_ref, other_ref, out_a_ref, out_b_ref, high, low):
     blocks = own_ref.shape[0]
-    lanes = slice(half * LANES, (half + 1) * LANES)
     for k, source in enumerate((own_ref, other_ref)):
         for b in range(blocks):
-            pairs[k * blocks + b] = jnp.concatenate(halves(source[b, :, lanes]), axis=1)
-    out_ref[...] = jnp.zeros_like(out_ref)
+            high[k * blocks + b], low[k * blocks + b] = halves(source[b])
+    out_a_ref[...] = jnp.zeros_like(out_a_ref)
+    out_b_ref[...] = jnp.zeros_like(out_b_ref)
 
     @pl.loop(0, (count_ref[0] + GROUP - 1) // GROUP)
     def _(step):
-        values = []
         for k in range(GROUP):
             slot = step * GROUP + k
             plan = plan_ref[slot]
-            pair = pairs[plan % 16]
+            left = left_ref[slot]
+            right = high[plan % 16]
             value = jnp.dot(
-                left_ref[slot],
-                jnp.concatenate([pair, pair], axis=0),
+                jnp.concatenate([left, left[:, : left.shape[0]]], axis=1),
+                jnp.concatenate([right, right, low[plan % 16]], axis=0),
                 preferred_element_type=jnp.float32,
             )
-            values.append((plan // 16, value[:, :LANES] + value[:, LANES:]))
-        for place, value in values:
-            out_ref[place] += value
-
-
-def products(half, count, plan, left, own, other):
+            out_a_ref[plan // 16] += value[:, :LANES]
+            out_b_ref[plan // 16] += value[:, LANES:]
+
+
+def products(count, plan, left, own, other):
     slots, tile, _ = left.shape
+    blocks = (2 * own.shape[0], tile, 2 * LANES)
     smem = pl.BlockSpec(memory_space=pltpu.SMEM)
     vmem = pl.BlockSpec(memory_space=pltpu.VMEM)
     return pl.pallas_call(
-        functools.partial(product_kernel, half),
-        out_shape=jax.ShapeDtypeStruct((NY * NZH + 1, tile, LANES), jnp.float32),
+        product_kernel,
+        out_shape=[jax.ShapeDtypeStruct((NY * NZH + 1, tile, LANES), jnp.float32)] * 2,
         in_specs=[smem, smem, vmem, vmem, vmem],
-        out_specs=vmem,
-        scratch_shapes=[pltpu.VMEM((NX * NZL * NC, tile, 2 * LANES), jnp.bfloat16)],
+        out_specs=[vmem, vmem],
+        scratch_shapes=[pltpu.VMEM(blocks, jnp.bfloat16)] * 2,
         compiler_params=pltpu.CompilerParams(vmem_limit_bytes=20 * 1024 * 1024),
         cost_estimate=pl.CostEstimate(
-            flops=8 * slots * tile * tile * LANES, bytes_accessed=8 * 2**20, transcendentals=0
+            flops=12 * slots * tile * tile * LANES, bytes_accessed=8 * 2**20, transcendentals=0
         ),
     )(count, plan, left, own, other)
 
 
-def node_kernel(*refs):
-    *terms, weight_ref, cot_ref, act_ref, grad_ref = refs
-    agg = jnp.concatenate([(t[0][...] + t[1][...]) + t[2][...] for t in (terms[:3], terms[3:])], axis=1)
+def node_kernel(terms_ref, weight_ref, cot_ref, act_ref, grad_ref):
+    agg = (terms_ref[0] + terms_ref[1]) + (terms_ref[2] + terms_ref[3])
     pre = dot3(agg, weight_ref[...], ((1,), (0,)))
     value, slope = gelu_parts(pre)
     act_ref[...] = value
@@ -157,10 +156,10 @@
             jax.ShapeDtypeStruct(cotangent.shape, jnp.float32),
             jax.ShapeDtypeStruct((NEAR_SIZE, 2, weight.shape[0] // NEAR_SIZE, LANES), jnp.float32),
         ),
-        in_specs=[vmem] * (len(terms) + 2),
+        in_specs=[vmem] * 3,
         out_specs=(vmem, vmem),
         compiler_params=pltpu.CompilerParams(vmem_limit_bytes=8 * 1024 * 1024),
-    )(*terms, weight, cotangent)
+    )(terms, weight, cotangent)
 
 
 def after(values, witness):
@@ -183,32 +182,23 @@
     return trade(pair[0], RING, 0), trade(pair[1], RING, 1)
 
 
-def spread(own, first):
-    got = trade(own[2], "zh", first)
-    direct = trade(own[1 + 2 * first], "zh", first)
-    return own[0], direct, trade(own[3 - 2 * first] + got, "zh", 1 - first)
-
-
 def body(features, adjacency_tiles, tile_rows, tile_cols, tile_count, weight, cotangent):
     plan = slot_plan(tile_rows, tile_cols, tile_count)
     own = share(features, ("x", "zl"))
     other = lax.ppermute(own, "c", [(0, 1), (1, 0)])
     arrays = (tile_count, plan, split_tiles(adjacency_tiles), own, other)
-    sums_a = products(0, *arrays)
-    out_a = chunk(sums_a, ROUNDS)
-    got_a = (trade(out_a, RING, 0), None)
-    sums_b = products(1, *arrays)
+    sums_a, sums_b = products(*arrays)
+    got_a = (None, trade(chunk(sums_a, ROUNDS), RING, 1))
     out_b = [chunk(sums_b, ROUNDS)]
-    got_b = (None, trade(out_b[0], RING, 1))
+    got_b = (trade(out_b[0], RING, 0), None)
     for step in range(1, ROUNDS):
         out_a = advance(sums_a, step, after(got_a, out_b[0]))
         got_a = send(out_a)
         out_b = advance(sums_b, step, after(got_b, out_a[0]))
         got_b = send(out_b)
     last_a = advance(sums_a, ROUNDS, after(got_a, out_b[0]))
-    terms = spread(last_a, 0)
     last_b = advance(sums_b, ROUNDS, after(got_b, last_a))
-    terms += spread(last_b, 1)
+    terms = swap(jnp.concatenate([last_a, last_b], axis=2), "zh")
     activated, grad = node_step(terms, weight, cotangent)
     grad = jnp.sum(swap(grad, NEAR), axis=0)
     grad = jnp.sum(share(grad, FAR), axis=0)

time: 163 us -> 160 us (0.982)
  starting transfers between devices: 78.9 us -> 49 us
  blocking collectives: 67.5 us -> 90.8 us
  waiting for transfers between devices: 4.09 us -> 9.12 us
  Pallas kernels: 5.69 us -> 3.62 us
    ppermute x20 -> x14, starting transfers between devices: 73.2 us -> 43.3 us  [trade(): lax.ppermute(v, axis, [(k, (k + 1 - 2 * ((k + way) % 2)) % n) for k in ra...]
    all_to_all x4 -> x5, blocking collectives: 67.5 us -> 90.8 us  [swap(): return lax.all_to_all(v, axes, split_axis=0, concat_axis=0, tiled=True)]
    ppermute x20 -> x14, waiting for transfers between devices: 4.08 us -> 9.12 us  [trade(): lax.ppermute(v, axis, [(k, (k + 1 - 2 * ((k + way) % 2)) % n) for k in ra...]
    pallas_call x2 -> x1, Pallas kernels: 4.09 us -> 2.02 us  [products(): pl.pallas_call(product_kernel, out_shape=[jax.ShapeDtypeStruct((NY * NZH...]
  transfers between devices with their start and end apart: 21 -> 15, of which waited for: 1 -> 6; matrix products, arithmetic and copies ran while one was open for 0% -> 0% of each run, Pallas kernels for 2% -> 0%
where the time goes in v2:
time: 160 us; the launch traced here: 159 us
  blocking collectives  90.8 us (57%)
  starting transfers between devices  49 us (31%)
  waiting for transfers between devices  9.12 us (6%)
  local copies, waits for them, and re-layouts  4.02 us (3%)
  Pallas kernels  3.62 us (2%)
  between operations  1.63 us (1%)
    all_to_all x5, blocking collectives, swap(): return lax.all_to_all(v, axes, split_axis=0, concat_axis=0, tiled=True)  90.8 us
    ppermute x14, starting transfers between devices, trade(): lax.ppermute(v, axis, [(k, (k + 1 - 2 * ((k + way) % 2)) % n) for k in ra...  43.3 us
    ppermute x14, waiting for transfers between devices, trade(): lax.ppermute(v, axis, [(k, (k + 1 - 2 * ((k + way) % 2)) % n) for k in ra...  9.12 us
    ppermute x1, starting transfers between devices, body(): other = lax.ppermute(own, 'c', [(0, 1), (1, 0)])  5.67 us
  transfers between devices with their start and end apart: 15, of which 6 were waited for; matrix products, arithmetic and copies ran while one was open for 0% of the time, Pallas kernels for 0%

profile of v2, /device:TPU:1, one launch (start us, length us, event | category | flops | bytes accessed | tf_op | source)
XLA Modules:
  0.0 158.8 jit_solution(15315701319840196054)
XLA Ops:
  0.6 1.0 broadcast_in_dim.11
  1.6 19.3 %all_to_all.25.own_ref = f32[8,128,256]{2,1,0:T(8,128)S(1)} all-to-all(f32[8,128,256]{2,1,0:T(8,128)S(1)} %broadcast_in_dim.11), channel_id=1, replica_groups=mesh['x'=4,'zl'=2,'c'=2,'yh'=4,'yl'=2,'zh'=4] {'x','zl'}, dimensions={0} | all-to-all | bytes 2097152 | tf_op jit(solution)/shard_map/all_to_all | solution.py:63
  21.0 5.7 %collective-permute-start = (f32[8,128,256]{2,1,0:T(8,128)S(1)}, f32[8,128,256]{2,1,0:T(8,128)S(1)}, u32[]{:S(2)}, u32[]{:S(2)}) collective-permute-start(f32[8,128,256]{2,1,0:T(8,128)S(1)} %all_to_all.25.own_ref), channel_id=1, source_target_pairs={{0,32},{32,0},{1,33},{33,1},{2,34},{34,2},{3,35},{35,3},{4,36},{36... | collective-permute-start | bytes 3145736 | tf_op jit(solution)/shard_map/ppermute | solution.py:188
  27.3 2.2 %copy-done = f32[64,128,128]{2,1,0:T(8,128)S(1)} copy-done((f32[64,128,128]{2,1,0:T(8,128)S(1)}, f32[64,128,128]{2,1,0:T(8,128)}, u32[]{:S(2)}) %copy-start) | copy-done | bytes 4194328
  29.5 0.6 shard_map.86.left_ref
  30.2 2.0 %shard_map.87 = (f32[33,128,128]{2,1,0:T(8,128)S(1)}, f32[33,128,128]{2,1,0:T(8,128)S(1)}) custom-call(s32[1]{0:T(128)} %copy.10.count_ref, s32[64]{0:T(128)S(1)} %fusion.7.plan_ref, bf16[64,128,256]{2,1,0:T(8,128)(2,1)S(1)} %shard_map.86.left_ref, f32[8,128,256]{2,1,0:T(8,128)S(1)} %all_to_all.25.own_ref, f32[8,128,256]{2,1,0:T(8,128)S(1)} %collective-permute-done.other_ref), custom_call_target="tpu_custom_call" | custom-call | flops 1610612736 | bytes 8388608 | tf_op jit(solution)/shard_map/pallas_call | solution.py:126
  32.3 5.2 %collective-permute-start.1 = (f32[4,128,128]{2,1,0:T(8,128)S(1)}, f32[4,128,128]{2,1,0:T(8,128)S(1)}, u32[]{:S(2)}, u32[]{:S(2)}) collective-permute-start(f32[4,128,128]{2,1,0:T(8,128)S(1)} %get-tuple-element.47), channel_id=1, source_target_pairs={{0,28},{4,8},{8,4},{12,16},{16,12},{20,24},{24,20},{28,0},{1,29},{... | collective-permute-start | bytes 786440 | tf_op jit(solution)/shard_map/ppermute | solution.py:53
  37.5 1.9 %collective-permute-start.7 = (f32[4,128,128]{2,1,0:T(8,128)S(1)}, f32[4,128,128]{2,1,0:T(8,128)S(1)}, u32[]{:S(2)}, u32[]{:S(2)}) collective-permute-start(f32[4,128,128]{2,1,0:T(8,128)S(1)} %slice.53), channel_id=1, source_target_pairs={{0,4},{4,0},{8,12},{12,8},{16,20},{20,16},{24,28},{28,24},{1,5},{5... | collective-permute-start | bytes 786440 | tf_op jit(solution)/shard_map/ppermute | solution.py:53
  39.5 4.0 %collective-permute-start.3 = (f32[4,128,128]{2,1,0:T(8,128)S(1)}, f32[4,128,128]{2,1,0:T(8,128)S(1)}, u32[]{:S(2)}, u32[]{:S(2)}) collective-permute-start(f32[4,128,128]{2,1,0:T(8,128)S(1)} %get-tuple-element.46), channel_id=1, source_target_pairs={{0,28},{4,8},{8,4},{12,16},{16,12},{20,24},{24,20},{28,0},{1,29},{... | collective-permute-start | bytes 786440 | tf_op jit(solution)/shard_map/ppermute | solution.py:53
  43.5 0.7 collective-permute-done.1
  44.2 3.9 %collective-permute-start.2 = (f32[4,128,128]{2,1,0:T(8,128)S(1)}, f32[4,128,128]{2,1,0:T(8,128)S(1)}, u32[]{:S(2)}, u32[]{:S(2)}) collective-permute-start(f32[4,128,128]{2,1,0:T(8,128)S(1)} %slice_add_fusion.7), channel_id=1, source_target_pairs={{0,4},{4,0},{8,12},{12,8},{16,20},{20,16},{24,28},{28,24},{1,5},{5... | collective-permute-start | bytes 786440 | tf_op jit(solution)/shard_map/ppermute | solution.py:53
  48.2 2.4 %collective-permute-start.8 = (f32[4,128,128]{2,1,0:T(8,128)S(1)}, f32[4,128,128]{2,1,0:T(8,128)S(1)}, u32[]{:S(2)}, u32[]{:S(2)}) collective-permute-start(f32[4,128,128]{2,1,0:T(8,128)S(1)} %get-tuple-element.48), channel_id=1, source_target_pairs={{0,28},{4,8},{8,4},{12,16},{16,12},{20,24},{24,20},{28,0},{1,29},{... | collective-permute-start | bytes 786440 | tf_op jit(solution)/shard_map/ppermute | solution.py:53
  50.6 1.9 %collective-permute-start.6 = (f32[4,128,128]{2,1,0:T(8,128)S(1)}, f32[4,128,128]{2,1,0:T(8,128)S(1)}, u32[]{:S(2)}, u32[]{:S(2)}) collective-permute-start(f32[4,128,128]{2,1,0:T(8,128)S(1)} %get-tuple-element.49), channel_id=1, source_target_pairs={{0,4},{4,0},{8,12},{12,8},{16,20},{20,16},{24,28},{28,24},{1,5},{5... | collective-permute-start | bytes 786440 | tf_op jit(solution)/shard_map/ppermute | solution.py:53
  52.6 5.0 %collective-permute-start.5 = (f32[4,128,128]{2,1,0:T(8,128)S(1)}, f32[4,128,128]{2,1,0:T(8,128)S(1)}, u32[]{:S(2)}, u32[]{:S(2)}) collective-permute-start(f32[4,128,128]{2,1,0:T(8,128)S(1)} %get-tuple-element.42), channel_id=1, source_target_pairs={{0,28},{4,8},{8,4},{12,16},{16,12},{20,24},{24,20},{28,0},{1,29},{... | collective-permute-start | bytes 786440 | tf_op jit(solution)/shard_map/ppermute | solution.py:53
  57.6 1.9 %collective-permute-start.4 = (f32[4,128,128]{2,1,0:T(8,128)S(1)}, f32[4,128,128]{2,1,0:T(8,128)S(1)}, u32[]{:S(2)}, u32[]{:S(2)}) collective-permute-start(f32[4,128,128]{2,1,0:T(8,128)S(1)} %get-tuple-element.43), channel_id=1, source_target_pairs={{0,4},{4,0},{8,12},{12,8},{16,20},{20,16},{24,28},{28,24},{1,5},{5... | collective-permute-start | bytes 786440 | tf_op jit(solution)/shard_map/ppermute | solution.py:53
  59.6 2.6 %collective-permute-start.12 = (f32[4,128,128]{2,1,0:T(8,128)S(1)}, f32[4,128,128]{2,1,0:T(8,128)S(1)}, u32[]{:S(2)}, u32[]{:S(2)}) collective-permute-start(f32[4,128,128]{2,1,0:T(8,128)S(1)} %get-tuple-element.44), channel_id=1, source_target_pairs={{0,28},{4,8},{8,4},{12,16},{16,12},{20,24},{24,20},{28,0},{1,29},{... | collective-permute-start | bytes 786440 | tf_op jit(solution)/shard_map/ppermute | solution.py:53
  62.2 2.7 %collective-permute-start.11 = (f32[4,128,128]{2,1,0:T(8,128)S(1)}, f32[4,128,128]{2,1,0:T(8,128)S(1)}, u32[]{:S(2)}, u32[]{:S(2)}) collective-permute-start(f32[4,128,128]{2,1,0:T(8,128)S(1)} %get-tuple-element.45), channel_id=1, source_target_pairs={{0,4},{4,0},{8,12},{12,8},{16,20},{20,16},{24,28},{28,24},{1,5},{5... | collective-permute-start | bytes 786440 | tf_op jit(solution)/shard_map/ppermute | solution.py:53
  64.9 0.1 collective-permute-done.4
  65.0 2.6 %collective-permute-start.9 = (f32[4,128,128]{2,1,0:T(8,128)S(1)}, f32[4,128,128]{2,1,0:T(8,128)S(1)}, u32[]{:S(2)}, u32[]{:S(2)}) collective-permute-start(f32[4,128,128]{2,1,0:T(8,128)S(1)} %get-tuple-element.39), channel_id=1, source_target_pairs={{0,4},{4,0},{8,12},{12,8},{16,20},{20,16},{24,28},{28,24},{1,5},{5... | collective-permute-start | bytes 786440 | tf_op jit(solution)/shard_map/ppermute | solution.py:53
  67.7 1.7 %collective-permute-done.12 = f32[4,128,128]{2,1,0:T(8,128)S(1)} collective-permute-done((f32[4,128,128]{2,1,0:T(8,128)S(1)}, f32[4,128,128]{2,1,0:T(8,128)S(1)}, u32[]{:S(2)}, u32[]{:S(2)}) %collective-permute-start.12) | collective-permute-done | bytes 262176 | tf_op jit(solution)/shard_map/ppermute | solution.py:53
  69.4 1.8 %collective-permute-done.11 = f32[4,128,128]{2,1,0:T(8,128)S(1)} collective-permute-done((f32[4,128,128]{2,1,0:T(8,128)S(1)}, f32[4,128,128]{2,1,0:T(8,128)S(1)}, u32[]{:S(2)}, u32[]{:S(2)}) %collective-permute-start.11) | collective-permute-done | bytes 262176 | tf_op jit(solution)/shard_map/ppermute | solution.py:53
  71.2 4.6 %collective-permute-start.10 = (f32[4,128,128]{2,1,0:T(8,128)S(1)}, f32[4,128,128]{2,1,0:T(8,128)S(1)}, u32[]{:S(2)}, u32[]{:S(2)}) collective-permute-start(f32[4,128,128]{2,1,0:T(8,128)S(1)} %get-tuple-element.38), channel_id=1, source_target_pairs={{0,28},{4,8},{8,4},{12,16},{16,12},{20,24},{24,20},{28,0},{1,29},{... | collective-permute-start | bytes 786440 | tf_op jit(solution)/shard_map/ppermute | solution.py:53
  75.9 2.1 %collective-permute-start.14 = (f32[4,128,128]{2,1,0:T(8,128)S(1)}, f32[4,128,128]{2,1,0:T(8,128)S(1)}, u32[]{:S(2)}, u32[]{:S(2)}) collective-permute-start(f32[4,128,128]{2,1,0:T(8,128)S(1)} %get-tuple-element.40), channel_id=1, source_target_pairs={{0,28},{4,8},{8,4},{12,16},{16,12},{20,24},{24,20},{28,0},{1,29},{... | collective-permute-start | bytes 786440 | tf_op jit(solution)/shard_map/ppermute | solution.py:53
  77.9 2.5 %collective-permute-start.13 = (f32[4,128,128]{2,1,0:T(8,128)S(1)}, f32[4,128,128]{2,1,0:T(8,128)S(1)}, u32[]{:S(2)}, u32[]{:S(2)}) collective-permute-start(f32[4,128,128]{2,1,0:T(8,128)S(1)} %get-tuple-element.41), channel_id=1, source_target_pairs={{0,4},{4,0},{8,12},{12,8},{16,20},{20,16},{24,28},{28,24},{1,5},{5... | collective-permute-start | bytes 786440 | tf_op jit(solution)/shard_map/ppermute | solution.py:53
  80.5 3.8 %collective-permute-done.14 = f32[4,128,128]{2,1,0:T(8,128)S(1)} collective-permute-done((f32[4,128,128]{2,1,0:T(8,128)S(1)}, f32[4,128,128]{2,1,0:T(8,128)S(1)}, u32[]{:S(2)}, u32[]{:S(2)}) %collective-permute-start.14) | collective-permute-done | bytes 262176 | tf_op jit(solution)/shard_map/ppermute | solution.py:53
  84.3 1.0 collective-permute-done.13
  85.4 22.6 %all_to_all.26.terms_ref = f32[4,128,256]{2,1,0:T(8,128)S(1)} all-to-all(f32[4,128,256]{2,1,0:T(8,128)S(1)} %pad_maximum_fusion), channel_id=1, replica_groups=mesh['x'=4,'zl'=2,'c'=2,'yh'=4,'yl'=2,'zh'=4] {'zh'}, dimensions={0} | all-to-all | bytes 1048576 | tf_op jit(solution)/shard_map/all_to_all | solution.py:63
  108.0 1.0 shard_map.88
  109.0 18.9 %all_to_all.27 = f32[32,2,8,128]{3,2,1,0:T(8,128)S(1)} all-to-all(f32[32,2,8,128]{3,2,1,0:T(8,128)S(1)} %get-tuple-element.37), channel_id=1, replica_groups=mesh['x'=4,'zl'=2,'c'=2,'yh'=4,'yl'=2,'zh'=4] {'x','zl','c','yl'}, dimensions={0} | all-to-all | bytes 524288 | tf_op jit(solution)/shard_map/all_to_all | solution.py:63
  127.9 16.9 %all_to_all.28 = f32[16,2,8,128]{3,2,1,0:T(8,128)S(1)} all-to-all(f32[16,2,8,128]{3,2,1,0:T(8,128)S(1)} %broadcast_in_dim.12), channel_id=1, replica_groups=mesh['x'=4,'zl'=2,'c'=2,'yh'=4,'yl'=2,'zh'=4] {'yh','zh'}, dimensions={0} | all-to-all | bytes 262144 | tf_op jit(solution)/shard_map/all_to_all | solution.py:63
  144.9 13.1 %all_to_all.29 = f32[32,2,8,128]{3,2,1,0:T(8,128)S(1)} all-to-all(f32[32,2,8,128]{3,2,1,0:T(8,128)S(1)} %broadcast_in_dim.13), channel_id=1, replica_groups=mesh['x'=4,'zl'=2,'c'=2,'yh'=4,'yl'=2,'zh'=4] {'x','zl','c','yl'}, dimensions={0} | all-to-all | bytes 524288 | tf_op jit(solution)/shard_map/all_to_all | solution.py:63
  158.0 0.7 copy.11
  (34 shorter events, 0.7 us)
Async XLA Ops:
  21.0 9.2 %collective-permute-start = (f32[8,128,256]{2,1,0:T(8,128)S(1)}, f32[8,128,256]{2,1,0:T(8,128)S(1)}, u32[]{:S(2)}, u32[]{:S(2)}) collective-permute-start(f32[8,128,256]{2,1,0:T(8,128)S(1)} %all_to_all.25.own_ref), channel_id=1, source_target_pairs={{0,32},{32,0},{1,33},{33,1},{2,34},{34,2},{3,35},{35,3},{4,36},{36... | collective-permute-start | bytes 3145736 | tf_op jit(solution)/shard_map/ppermute | solution.py:188
  27.3 2.2 %copy-start = (f32[64,128,128]{2,1,0:T(8,128)S(1)}, f32[64,128,128]{2,1,0:T(8,128)}, u32[]{:S(2)}) copy-start(f32[64,128,128]{2,1,0:T(8,128)} %tiles_ref.1) | copy-start | bytes 12582916
  29.5 0.7 copy-start.3
  29.5 0.7 copy-start.4
  32.3 11.9 %collective-permute-start.1 = (f32[4,128,128]{2,1,0:T(8,128)S(1)}, f32[4,128,128]{2,1,0:T(8,128)S(1)}, u32[]{:S(2)}, u32[]{:S(2)}) collective-permute-start(f32[4,128,128]{2,1,0:T(8,128)S(1)} %get-tuple-element.47), channel_id=1, source_target_pairs={{0,28},{4,8},{8,4},{12,16},{16,12},{20,24},{24,20},{28,0},{1,29},{... | collective-permute-start | bytes 786440 | tf_op jit(solution)/shard_map/ppermute | solution.py:53
  37.5 10.6 %collective-permute-start.7 = (f32[4,128,128]{2,1,0:T(8,128)S(1)}, f32[4,128,128]{2,1,0:T(8,128)S(1)}, u32[]{:S(2)}, u32[]{:S(2)}) collective-permute-start(f32[4,128,128]{2,1,0:T(8,128)S(1)} %slice.53), channel_id=1, source_target_pairs={{0,4},{4,0},{8,12},{12,8},{16,20},{20,16},{24,28},{28,24},{1,5},{5... | collective-permute-start | bytes 786440 | tf_op jit(solution)/shard_map/ppermute | solution.py:53
  39.5 13.1 %collective-permute-start.3 = (f32[4,128,128]{2,1,0:T(8,128)S(1)}, f32[4,128,128]{2,1,0:T(8,128)S(1)}, u32[]{:S(2)}, u32[]{:S(2)}) collective-permute-start(f32[4,128,128]{2,1,0:T(8,128)S(1)} %get-tuple-element.46), channel_id=1, source_target_pairs={{0,28},{4,8},{8,4},{12,16},{16,12},{20,24},{24,20},{28,0},{1,29},{... | collective-permute-start | bytes 786440 | tf_op jit(solution)/shard_map/ppermute | solution.py:53
  44.2 8.3 %collective-permute-start.2 = (f32[4,128,128]{2,1,0:T(8,128)S(1)}, f32[4,128,128]{2,1,0:T(8,128)S(1)}, u32[]{:S(2)}, u32[]{:S(2)}) collective-permute-start(f32[4,128,128]{2,1,0:T(8,128)S(1)} %slice_add_fusion.7), channel_id=1, source_target_pairs={{0,4},{4,0},{8,12},{12,8},{16,20},{20,16},{24,28},{28,24},{1,5},{5... | collective-permute-start | bytes 786440 | tf_op jit(solution)/shard_map/ppermute | solution.py:53
  48.2 11.3 %collective-permute-start.8 = (f32[4,128,128]{2,1,0:T(8,128)S(1)}, f32[4,128,128]{2,1,0:T(8,128)S(1)}, u32[]{:S(2)}, u32[]{:S(2)}) collective-permute-start(f32[4,128,128]{2,1,0:T(8,128)S(1)} %get-tuple-element.48), channel_id=1, source_target_pairs={{0,28},{4,8},{8,4},{12,16},{16,12},{20,24},{24,20},{28,0},{1,29},{... | collective-permute-start | bytes 786440 | tf_op jit(solution)/shard_map/ppermute | solution.py:53
  50.6 8.9 %collective-permute-start.6 = (f32[4,128,128]{2,1,0:T(8,128)S(1)}, f32[4,128,128]{2,1,0:T(8,128)S(1)}, u32[]{:S(2)}, u32[]{:S(2)}) collective-permute-start(f32[4,128,128]{2,1,0:T(8,128)S(1)} %get-tuple-element.49), channel_id=1, source_target_pairs={{0,4},{4,0},{8,12},{12,8},{16,20},{20,16},{24,28},{28,24},{1,5},{5... | collective-permute-start | bytes 786440 | tf_op jit(solution)/shard_map/ppermute | solution.py:53
  52.6 12.3 %collective-permute-start.5 = (f32[4,128,128]{2,1,0:T(8,128)S(1)}, f32[4,128,128]{2,1,0:T(8,128)S(1)}, u32[]{:S(2)}, u32[]{:S(2)}) collective-permute-start(f32[4,128,128]{2,1,0:T(8,128)S(1)} %get-tuple-element.42), channel_id=1, source_target_pairs={{0,28},{4,8},{8,4},{12,16},{16,12},{20,24},{24,20},{28,0},{1,29},{... | collective-permute-start | bytes 786440 | tf_op jit(solution)/shard_map/ppermute | solution.py:53
  57.6 7.4 %collective-permute-start.4 = (f32[4,128,128]{2,1,0:T(8,128)S(1)}, f32[4,128,128]{2,1,0:T(8,128)S(1)}, u32[]{:S(2)}, u32[]{:S(2)}) collective-permute-start(f32[4,128,128]{2,1,0:T(8,128)S(1)} %get-tuple-element.43), channel_id=1, source_target_pairs={{0,4},{4,0},{8,12},{12,8},{16,20},{20,16},{24,28},{28,24},{1,5},{5... | collective-permute-start | bytes 786440 | tf_op jit(solution)/shard_map/ppermute | solution.py:53
  59.6 9.8 %collective-permute-start.12 = (f32[4,128,128]{2,1,0:T(8,128)S(1)}, f32[4,128,128]{2,1,0:T(8,128)S(1)}, u32[]{:S(2)}, u32[]{:S(2)}) collective-permute-start(f32[4,128,128]{2,1,0:T(8,128)S(1)} %get-tuple-element.44), channel_id=1, source_target_pairs={{0,28},{4,8},{8,4},{12,16},{16,12},{20,24},{24,20},{28,0},{1,29},{... | collective-permute-start | bytes 786440 | tf_op jit(solution)/shard_map/ppermute | solution.py:53
  62.2 9.0 %collective-permute-start.11 = (f32[4,128,128]{2,1,0:T(8,128)S(1)}, f32[4,128,128]{2,1,0:T(8,128)S(1)}, u32[]{:S(2)}, u32[]{:S(2)}) collective-permute-start(f32[4,128,128]{2,1,0:T(8,128)S(1)} %get-tuple-element.45), channel_id=1, source_target_pairs={{0,4},{4,0},{8,12},{12,8},{16,20},{20,16},{24,28},{28,24},{1,5},{5... | collective-permute-start | bytes 786440 | tf_op jit(solution)/shard_map/ppermute | solution.py:53
  65.0 15.4 %collective-permute-start.9 = (f32[4,128,128]{2,1,0:T(8,128)S(1)}, f32[4,128,128]{2,1,0:T(8,128)S(1)}, u32[]{:S(2)}, u32[]{:S(2)}) collective-permute-start(f32[4,128,128]{2,1,0:T(8,128)S(1)} %get-tuple-element.39), channel_id=1, source_target_pairs={{0,4},{4,0},{8,12},{12,8},{16,20},{20,16},{24,28},{28,24},{1,5},{5... | collective-permute-start | bytes 786440 | tf_op jit(solution)/shard_map/ppermute | solution.py:53
  71.2 9.3 %collective-permute-start.10 = (f32[4,128,128]{2,1,0:T(8,128)S(1)}, f32[4,128,128]{2,1,0:T(8,128)S(1)}, u32[]{:S(2)}, u32[]{:S(2)}) collective-permute-start(f32[4,128,128]{2,1,0:T(8,128)S(1)} %get-tuple-element.38), channel_id=1, source_target_pairs={{0,28},{4,8},{8,4},{12,16},{16,12},{20,24},{24,20},{28,0},{1,29},{... | collective-permute-start | bytes 786440 | tf_op jit(solution)/shard_map/ppermute | solution.py:53
  75.9 32.2 %copy-start.1 = (f32[256,256]{1,0:T(8,128)S(1)}, f32[256,256]{1,0:T(8,128)}, u32[]{:S(2)}) copy-start(f32[256,256]{1,0:T(8,128)} %weight_ref.1) | copy-start | bytes 786436
  75.9 32.1 %copy-start.2 = (f32[128,256]{1,0:T(8,128)S(1)}, f32[128,256]{1,0:T(8,128)}, u32[]{:S(2)}) copy-start(f32[128,256]{1,0:T(8,128)} %cot_ref.1) | copy-start | bytes 393220
  75.9 8.5 %collective-permute-start.14 = (f32[4,128,128]{2,1,0:T(8,128)S(1)}, f32[4,128,128]{2,1,0:T(8,128)S(1)}, u32[]{:S(2)}, u32[]{:S(2)}) collective-permute-start(f32[4,128,128]{2,1,0:T(8,128)S(1)} %get-tuple-element.40), channel_id=1, source_target_pairs={{0,28},{4,8},{8,4},{12,16},{16,12},{20,24},{24,20},{28,0},{1,29},{... | collective-permute-start | bytes 786440 | tf_op jit(solution)/shard_map/ppermute | solution.py:53
  77.9 7.4 %collective-permute-start.13 = (f32[4,128,128]{2,1,0:T(8,128)S(1)}, f32[4,128,128]{2,1,0:T(8,128)S(1)}, u32[]{:S(2)}, u32[]{:S(2)}) collective-permute-start(f32[4,128,128]{2,1,0:T(8,128)S(1)} %get-tuple-element.41), channel_id=1, source_target_pairs={{0,4},{4,0},{8,12},{12,8},{16,20},{20,16},{24,28},{28,24},{1,5},{5... | collective-permute-start | bytes 786440 | tf_op jit(solution)/shard_map/ppermute | solution.py:53

commit v3 on v2

--- a/solution.py
+++ b/solution.py
@@ -94,7 +94,16 @@
     )(tiles)
 
 
-def product_kernel(count_ref, plan_ref, left_ref, own_ref, other_ref, out_a_ref, out_b_ref, high, low):
+def slot_product(left, high, low):
+    tile = left.shape[0]
+    return jnp.dot(
+        jnp.concatenate([left, left[:, :tile]], axis=1),
+        jnp.concatenate([high, high, low], axis=0),
+        preferred_element_type=jnp.float32,
+    )
+
+
+def far_kernel(count_ref, plan_ref, left_ref, own_ref, other_ref, out_a_ref, out_b_ref, high, low):
     blocks = own_ref.shape[0]
     for k, source in enumerate((own_ref, other_ref)):
         for b in range(blocks):
@@ -102,25 +111,49 @@
     out_a_ref[...] = jnp.zeros_like(out_a_ref)
     out_b_ref[...] = jnp.zeros_like(out_b_ref)
 
+    @pl.loop(0, count_ref[0])
+    def _(slot):
+        plan = plan_ref[slot]
+        place = plan // 16 - ROUNDS * NZH
+
+        @pl.when((place >= 0) & (place < NZH))
+        def _():
+            value = slot_product(left_ref[slot], high[plan % 16], low[plan % 16])
+            out_a_ref[place] += value[:, :LANES]
+            out_b_ref[place] += value[:, LANES:]
+
+
+def far_products(count, plan, left, own, other):
+    tile = left.shape[1]
+    blocks = jax.ShapeDtypeStruct((2 * own.shape[0], tile, 2 * LANES), jnp.bfloat16)
+    smem = pl.BlockSpec(memory_space=pltpu.SMEM)
+    vmem = pl.BlockSpec(memory_space=pltpu.VMEM)
+    return pl.pallas_call(
+        far_kernel,
+        out_shape=[jax.ShapeDtypeStruct((NZH, tile, LANES), jnp.float32)] * 2 + [blocks] * 2,
+        in_specs=[smem, smem, vmem, vmem, vmem],
+        out_specs=[vmem] * 4,
+        compiler_params=pltpu.CompilerParams(vmem_limit_bytes=16 * 1024 * 1024),
+        cost_estimate=pl.CostEstimate(flops=10**9, bytes_accessed=8 * 2**20, transcendentals=0),
+    )(count, plan, left, own, other)
+
+
+def product_kernel(count_ref, plan_ref, left_ref, high_ref, low_ref, out_a_ref, out_b_ref):
+    out_a_ref[...] = jnp.zeros_like(out_a_ref)
+    out_b_ref[...] = jnp.zeros_like(out_b_ref)
+
     @pl.loop(0, (count_ref[0] + GROUP - 1) // GROUP)
     def _(step):
         for k in range(GROUP):
             slot = step * GROUP + k
             plan = plan_ref[slot]
-            left = left_ref[slot]
-            right = high[plan % 16]
-            value = jnp.dot(
-                jnp.concatenate([left, left[:, : left.shape[0]]], axis=1),
-                jnp.concatenate([right, right, low[plan % 16]], axis=0),
-                preferred_element_type=jnp.float32,
-            )
+            value = slot_product(left_ref[slot], high_ref[plan % 16], low_ref[plan % 16])
             out_a_ref[plan // 16] += value[:, :LANES]
             out_b_ref[plan // 16] += value[:, LANES:]
 
 
-def products(count, plan, left, own, other):
+def products(count, plan, left, high, low):
     slots, tile, _ = left.shape
-    blocks = (2 * own.shape[0], tile, 2 * LANES)
     smem = pl.BlockSpec(memory_space=pltpu.SMEM)
     vmem = pl.BlockSpec(memory_space=pltpu.VMEM)
     return pl.pallas_call(
@@ -128,12 +161,11 @@
         out_shape=[jax.ShapeDtypeStruct((NY * NZH + 1, tile, LANES), jnp.float32)] * 2,
         in_specs=[smem, smem, vmem, vmem, vmem],
         out_specs=[vmem, vmem],
-        scratch_shapes=[pltpu.VMEM(blocks, jnp.bfloat16)] * 2,
         compiler_params=pltpu.CompilerParams(vmem_limit_bytes=20 * 1024 * 1024),
         cost_estimate=pl.CostEstimate(
             flops=12 * slots * tile * tile * LANES, bytes_accessed=8 * 2**20, transcendentals=0
         ),
-    )(count, plan, left, own, other)
+    )(count, plan, left, high, low)
 
 
 def node_kernel(terms_ref, weight_ref, cot_ref, act_ref, grad_ref):
@@ -186,11 +218,12 @@
     plan = slot_plan(tile_rows, tile_cols, tile_count)
     own = share(features, ("x", "zl"))
     other = lax.ppermute(own, "c", [(0, 1), (1, 0)])
-    arrays = (tile_count, plan, split_tiles(adjacency_tiles), own, other)
-    sums_a, sums_b = products(*arrays)
-    got_a = (None, trade(chunk(sums_a, ROUNDS), RING, 1))
-    out_b = [chunk(sums_b, ROUNDS)]
-    got_b = (trade(out_b[0], RING, 0), None)
+    left = split_tiles(adjacency_tiles)
+    far_a, far_b, high, low = far_products(tile_count, plan, left, own, other)
+    got_a = (None, trade(far_a, RING, 1))
+    got_b = (trade(far_b, RING, 0), None)
+    sums_a, sums_b = products(tile_count, plan, left, high, low)
+    out_b = [far_b]
     for step in range(1, ROUNDS):
         out_a = advance(sums_a, step, after(got_a, out_b[0]))
         got_a = send(out_a)

time: 160 us -> 159 us (level)
  Pallas kernels: 3.62 us -> 7.49 us
  blocking collectives: 90.8 us -> 87.8 us
  starting transfers between devices: 49 us -> 47.1 us
    all_to_all x5, blocking collectives: 90.8 us -> 87.8 us  [swap(): return lax.all_to_all(v, axes, split_axis=0, concat_axis=0, tiled=True)]
    pallas_call x0 -> x1, Pallas kernels: none -> 2.84 us  [far_products(): pl.pallas_call(far_kernel, out_shape=[jax.ShapeDtypeStruct((NZH, tile, LA...]
    ppermute x14, starting transfers between devices: 43.3 us -> 41.4 us  [trade(): lax.ppermute(v, axis, [(k, (k + 1 - 2 * ((k + way) % 2)) % n) for k in ra...]
  transfers between devices with their start and end apart: 15 -> 15, of which waited for: 6 -> 5; matrix products, arithmetic and copies ran while one was open for 0% -> 0% of each run, Pallas kernels for 0% -> 2%
where the time goes in v3:
time: 159 us; the launch traced here: 158 us
  blocking collectives  87.8 us (55%)
  starting transfers between devices  47.1 us (30%)
  waiting for transfers between devices  9.55 us (6%)
  Pallas kernels  7.49 us (5%)
  local copies, waits for them, and re-layouts  3.96 us (2%)
  between operations  1.63 us (1%)
    all_to_all x5, blocking collectives, swap(): return lax.all_to_all(v, axes, split_axis=0, concat_axis=0, tiled=True)  87.8 us
    ppermute x14, starting transfers between devices, trade(): lax.ppermute(v, axis, [(k, (k + 1 - 2 * ((k + way) % 2)) % n) for k in ra...  41.4 us
    ppermute x14, waiting for transfers between devices, trade(): lax.ppermute(v, axis, [(k, (k + 1 - 2 * ((k + way) % 2)) % n) for k in ra...  9.55 us
    ppermute x1, starting transfers between devices, body(): other = lax.ppermute(own, 'c', [(0, 1), (1, 0)])  5.67 us
  transfers between devices with their start and end apart: 15, of which 5 were waited for; matrix products, arithmetic and copies ran while one was open for 0% of the time, Pallas kernels for 2%

profile of v3, /device:TPU:1, one launch (start us, length us, event | category | flops | bytes accessed | tf_op | source)
XLA Modules:
  0.0 158.1 jit_solution(6672184525976858594)
XLA Ops:
  0.6 1.0 broadcast_in_dim.11
  1.6 19.3 %all_to_all.25.own_ref = f32[8,128,256]{2,1,0:T(8,128)S(1)} all-to-all(f32[8,128,256]{2,1,0:T(8,128)S(1)} %broadcast_in_dim.11), channel_id=1, replica_groups=mesh['x'=4,'zl'=2,'c'=2,'yh'=4,'yl'=2,'zh'=4] {'x','zl'}, dimensions={0} | all-to-all | bytes 2097152 | tf_op jit(solution)/shard_map/all_to_all | solution.py:63
  21.0 5.7 %collective-permute-start = (f32[8,128,256]{2,1,0:T(8,128)S(1)}, f32[8,128,256]{2,1,0:T(8,128)S(1)}, u32[]{:S(2)}, u32[]{:S(2)}) collective-permute-start(f32[8,128,256]{2,1,0:T(8,128)S(1)} %all_to_all.25.own_ref), channel_id=1, source_target_pairs={{0,32},{32,0},{1,33},{33,1},{2,34},{34,2},{3,35},{35,3},{4,36},{36... | collective-permute-start | bytes 3145736 | tf_op jit(solution)/shard_map/ppermute | solution.py:220
  27.3 2.2 %copy-done = f32[64,128,128]{2,1,0:T(8,128)S(1)} copy-done((f32[64,128,128]{2,1,0:T(8,128)S(1)}, f32[64,128,128]{2,1,0:T(8,128)}, u32[]{:S(2)}) %copy-start) | copy-done | bytes 4194328
  29.5 0.6 shard_map.86.left_ref
  30.2 2.8 %shard_map.87 = (f32[4,128,128]{2,1,0:T(8,128)S(1)}, f32[4,128,128]{2,1,0:T(8,128)S(1)}, bf16[16,128,256]{2,1,0:T(8,128)(2,1)S(1)}, bf16[16,128,256]{2,1,0:T(8,128)(2,1)S(1)}) custom-call(s32[1]{0:T(128)} %copy.10.count_ref, s32[64]{0:T(128)S(1)} %fusion.7.plan_ref, bf16[64,128,256]{2,1,0:T(8,128)(2,1)S(1)} %shard_map.86.left_ref, ...), custom_call_target="tpu_custom_call" | custom-call | flops 1000000000 | bytes 8388608 | tf_op jit(solution)/shard_map/pallas_call | solution.py:131
  33.0 5.3 %collective-permute-start.1 = (f32[4,128,128]{2,1,0:T(8,128)S(1)}, f32[4,128,128]{2,1,0:T(8,128)S(1)}, u32[]{:S(2)}, u32[]{:S(2)}) collective-permute-start(f32[4,128,128]{2,1,0:T(8,128)S(1)} %get-tuple-element.27), channel_id=1, source_target_pairs={{0,28},{4,8},{8,4},{12,16},{16,12},{20,24},{24,20},{28,0},{1,29},{... | collective-permute-start | bytes 786440 | tf_op jit(solution)/shard_map/ppermute | solution.py:53
  38.4 1.9 %collective-permute-start.7 = (f32[4,128,128]{2,1,0:T(8,128)S(1)}, f32[4,128,128]{2,1,0:T(8,128)S(1)}, u32[]{:S(2)}, u32[]{:S(2)}) collective-permute-start(f32[4,128,128]{2,1,0:T(8,128)S(1)} %get-tuple-element.28), channel_id=1, source_target_pairs={{0,4},{4,0},{8,12},{12,8},{16,20},{20,16},{24,28},{28,24},{1,5},{5... | collective-permute-start | bytes 786440 | tf_op jit(solution)/shard_map/ppermute | solution.py:53
  40.3 3.1 %shard_map.88 = (f32[33,128,128]{2,1,0:T(8,128)S(1)}, f32[33,128,128]{2,1,0:T(8,128)S(1)}) custom-call(s32[1]{0:T(128)} %copy.10.count_ref, s32[64]{0:T(128)S(1)} %fusion.7.plan_ref, bf16[64,128,256]{2,1,0:T(8,128)(2,1)S(1)} %shard_map.86.left_ref, bf16[16,128,256]{2,1,0:T(8,128)(2,1)S(1)} %get-tuple-element.24.high_ref, ...), custom_call_target="tpu_custom_call" | custom-call | flops 1610612736 | bytes 8388608 | tf_op jit(solution)/shard_map/pallas_call | solution.py:159
  43.4 1.4 collective-permute-done.1
  44.9 3.8 %collective-permute-start.3 = (f32[4,128,128]{2,1,0:T(8,128)S(1)}, f32[4,128,128]{2,1,0:T(8,128)S(1)}, u32[]{:S(2)}, u32[]{:S(2)}) collective-permute-start(f32[4,128,128]{2,1,0:T(8,128)S(1)} %get-tuple-element.54), channel_id=1, source_target_pairs={{0,28},{4,8},{8,4},{12,16},{16,12},{20,24},{24,20},{28,0},{1,29},{... | collective-permute-start | bytes 786440 | tf_op jit(solution)/shard_map/ppermute | solution.py:53
  48.7 1.9 %collective-permute-start.2 = (f32[4,128,128]{2,1,0:T(8,128)S(1)}, f32[4,128,128]{2,1,0:T(8,128)S(1)}, u32[]{:S(2)}, u32[]{:S(2)}) collective-permute-start(f32[4,128,128]{2,1,0:T(8,128)S(1)} %get-tuple-element.55), channel_id=1, source_target_pairs={{0,4},{4,0},{8,12},{12,8},{16,20},{20,16},{24,28},{28,24},{1,5},{5... | collective-permute-start | bytes 786440 | tf_op jit(solution)/shard_map/ppermute | solution.py:53
  50.7 2.7 %collective-permute-start.8 = (f32[4,128,128]{2,1,0:T(8,128)S(1)}, f32[4,128,128]{2,1,0:T(8,128)S(1)}, u32[]{:S(2)}, u32[]{:S(2)}) collective-permute-start(f32[4,128,128]{2,1,0:T(8,128)S(1)} %get-tuple-element.56), channel_id=1, source_target_pairs={{0,28},{4,8},{8,4},{12,16},{16,12},{20,24},{24,20},{28,0},{1,29},{... | collective-permute-start | bytes 786440 | tf_op jit(solution)/shard_map/ppermute | solution.py:53
  53.4 3.8 %collective-permute-start.6 = (f32[4,128,128]{2,1,0:T(8,128)S(1)}, f32[4,128,128]{2,1,0:T(8,128)S(1)}, u32[]{:S(2)}, u32[]{:S(2)}) collective-permute-start(f32[4,128,128]{2,1,0:T(8,128)S(1)} %get-tuple-element.57), channel_id=1, source_target_pairs={{0,4},{4,0},{8,12},{12,8},{16,20},{20,16},{24,28},{28,24},{1,5},{5... | collective-permute-start | bytes 786440 | tf_op jit(solution)/shard_map/ppermute | solution.py:53
  57.2 1.2 collective-permute-done.2
  58.4 1.9 %collective-permute-start.5 = (f32[4,128,128]{2,1,0:T(8,128)S(1)}, f32[4,128,128]{2,1,0:T(8,128)S(1)}, u32[]{:S(2)}, u32[]{:S(2)}) collective-permute-start(f32[4,128,128]{2,1,0:T(8,128)S(1)} %get-tuple-element.50), channel_id=1, source_target_pairs={{0,28},{4,8},{8,4},{12,16},{16,12},{20,24},{24,20},{28,0},{1,29},{... | collective-permute-start | bytes 786440 | tf_op jit(solution)/shard_map/ppermute | solution.py:53
  60.3 2.4 %collective-permute-start.4 = (f32[4,128,128]{2,1,0:T(8,128)S(1)}, f32[4,128,128]{2,1,0:T(8,128)S(1)}, u32[]{:S(2)}, u32[]{:S(2)}) collective-permute-start(f32[4,128,128]{2,1,0:T(8,128)S(1)} %get-tuple-element.51), channel_id=1, source_target_pairs={{0,4},{4,0},{8,12},{12,8},{16,20},{20,16},{24,28},{28,24},{1,5},{5... | collective-permute-start | bytes 786440 | tf_op jit(solution)/shard_map/ppermute | solution.py:53
  62.7 0.5 collective-permute-done.6
  63.3 3.7 %collective-permute-start.12 = (f32[4,128,128]{2,1,0:T(8,128)S(1)}, f32[4,128,128]{2,1,0:T(8,128)S(1)}, u32[]{:S(2)}, u32[]{:S(2)}) collective-permute-start(f32[4,128,128]{2,1,0:T(8,128)S(1)} %get-tuple-element.52), channel_id=1, source_target_pairs={{0,28},{4,8},{8,4},{12,16},{16,12},{20,24},{24,20},{28,0},{1,29},{... | collective-permute-start | bytes 786440 | tf_op jit(solution)/shard_map/ppermute | solution.py:53
  66.9 3.4 %collective-permute-start.11 = (f32[4,128,128]{2,1,0:T(8,128)S(1)}, f32[4,128,128]{2,1,0:T(8,128)S(1)}, u32[]{:S(2)}, u32[]{:S(2)}) collective-permute-start(f32[4,128,128]{2,1,0:T(8,128)S(1)} %get-tuple-element.53), channel_id=1, source_target_pairs={{0,4},{4,0},{8,12},{12,8},{16,20},{20,16},{24,28},{28,24},{1,5},{5... | collective-permute-start | bytes 786440 | tf_op jit(solution)/shard_map/ppermute | solution.py:53
  70.4 2.5 %collective-permute-start.10 = (f32[4,128,128]{2,1,0:T(8,128)S(1)}, f32[4,128,128]{2,1,0:T(8,128)S(1)}, u32[]{:S(2)}, u32[]{:S(2)}) collective-permute-start(f32[4,128,128]{2,1,0:T(8,128)S(1)} %get-tuple-element.46), channel_id=1, source_target_pairs={{0,28},{4,8},{8,4},{12,16},{16,12},{20,24},{24,20},{28,0},{1,29},{... | collective-permute-start | bytes 786440 | tf_op jit(solution)/shard_map/ppermute | solution.py:53
  73.0 3.0 %collective-permute-start.9 = (f32[4,128,128]{2,1,0:T(8,128)S(1)}, f32[4,128,128]{2,1,0:T(8,128)S(1)}, u32[]{:S(2)}, u32[]{:S(2)}) collective-permute-start(f32[4,128,128]{2,1,0:T(8,128)S(1)} %get-tuple-element.47), channel_id=1, source_target_pairs={{0,4},{4,0},{8,12},{12,8},{16,20},{20,16},{24,28},{28,24},{1,5},{5... | collective-permute-start | bytes 786440 | tf_op jit(solution)/shard_map/ppermute | solution.py:53
  76.1 3.1 %collective-permute-start.14 = (f32[4,128,128]{2,1,0:T(8,128)S(1)}, f32[4,128,128]{2,1,0:T(8,128)S(1)}, u32[]{:S(2)}, u32[]{:S(2)}) collective-permute-start(f32[4,128,128]{2,1,0:T(8,128)S(1)} %get-tuple-element.48), channel_id=1, source_target_pairs={{0,28},{4,8},{8,4},{12,16},{16,12},{20,24},{24,20},{28,0},{1,29},{... | collective-permute-start | bytes 786440 | tf_op jit(solution)/shard_map/ppermute | solution.py:53
  79.3 2.0 %collective-permute-start.13 = (f32[4,128,128]{2,1,0:T(8,128)S(1)}, f32[4,128,128]{2,1,0:T(8,128)S(1)}, u32[]{:S(2)}, u32[]{:S(2)}) collective-permute-start(f32[4,128,128]{2,1,0:T(8,128)S(1)} %get-tuple-element.49), channel_id=1, source_target_pairs={{0,4},{4,0},{8,12},{12,8},{16,20},{20,16},{24,28},{28,24},{1,5},{5... | collective-permute-start | bytes 786440 | tf_op jit(solution)/shard_map/ppermute | solution.py:53
  81.3 3.3 %collective-permute-done.14 = f32[4,128,128]{2,1,0:T(8,128)S(1)} collective-permute-done((f32[4,128,128]{2,1,0:T(8,128)S(1)}, f32[4,128,128]{2,1,0:T(8,128)S(1)}, u32[]{:S(2)}, u32[]{:S(2)}) %collective-permute-start.14) | collective-permute-done | bytes 262176 | tf_op jit(solution)/shard_map/ppermute | solution.py:53
  84.6 3.1 %collective-permute-done.13 = f32[4,128,128]{2,1,0:T(8,128)S(1)} collective-permute-done((f32[4,128,128]{2,1,0:T(8,128)S(1)}, f32[4,128,128]{2,1,0:T(8,128)S(1)}, u32[]{:S(2)}, u32[]{:S(2)}) %collective-permute-start.13) | collective-permute-done | bytes 262176 | tf_op jit(solution)/shard_map/ppermute | solution.py:53
  87.8 23.2 %all_to_all.26.terms_ref = f32[4,128,256]{2,1,0:T(8,128)S(1)} all-to-all(f32[4,128,256]{2,1,0:T(8,128)S(1)} %pad_maximum_fusion), channel_id=1, replica_groups=mesh['x'=4,'zl'=2,'c'=2,'yh'=4,'yl'=2,'zh'=4] {'zh'}, dimensions={0} | all-to-all | bytes 1048576 | tf_op jit(solution)/shard_map/all_to_all | solution.py:63
  111.0 1.0 shard_map.89
  112.0 16.7 %all_to_all.27 = f32[32,2,8,128]{3,2,1,0:T(8,128)S(1)} all-to-all(f32[32,2,8,128]{3,2,1,0:T(8,128)S(1)} %get-tuple-element.45), channel_id=1, replica_groups=mesh['x'=4,'zl'=2,'c'=2,'yh'=4,'yl'=2,'zh'=4] {'x','zl','c','yl'}, dimensions={0} | all-to-all | bytes 524288 | tf_op jit(solution)/shard_map/all_to_all | solution.py:63
  128.8 15.5 %all_to_all.28 = f32[16,2,8,128]{3,2,1,0:T(8,128)S(1)} all-to-all(f32[16,2,8,128]{3,2,1,0:T(8,128)S(1)} %broadcast_in_dim.12), channel_id=1, replica_groups=mesh['x'=4,'zl'=2,'c'=2,'yh'=4,'yl'=2,'zh'=4] {'yh','zh'}, dimensions={0} | all-to-all | bytes 262144 | tf_op jit(solution)/shard_map/all_to_all | solution.py:63
  144.3 13.1 %all_to_all.29 = f32[32,2,8,128]{3,2,1,0:T(8,128)S(1)} all-to-all(f32[32,2,8,128]{3,2,1,0:T(8,128)S(1)} %broadcast_in_dim.13), channel_id=1, replica_groups=mesh['x'=4,'zl'=2,'c'=2,'yh'=4,'yl'=2,'zh'=4] {'x','zl','c','yl'}, dimensions={0} | all-to-all | bytes 524288 | tf_op jit(solution)/shard_map/all_to_all | solution.py:63
  157.4 0.7 copy.11
  (33 shorter events, 0.6 us)
Async XLA Ops:
  21.0 9.2 %collective-permute-start = (f32[8,128,256]{2,1,0:T(8,128)S(1)}, f32[8,128,256]{2,1,0:T(8,128)S(1)}, u32[]{:S(2)}, u32[]{:S(2)}) collective-permute-start(f32[8,128,256]{2,1,0:T(8,128)S(1)} %all_to_all.25.own_ref), channel_id=1, source_target_pairs={{0,32},{32,0},{1,33},{33,1},{2,34},{34,2},{3,35},{35,3},{4,36},{36... | collective-permute-start | bytes 3145736 | tf_op jit(solution)/shard_map/ppermute | solution.py:220
  27.3 2.2 %copy-start = (f32[64,128,128]{2,1,0:T(8,128)S(1)}, f32[64,128,128]{2,1,0:T(8,128)}, u32[]{:S(2)}) copy-start(f32[64,128,128]{2,1,0:T(8,128)} %tiles_ref.1) | copy-start | bytes 12582916
  29.5 0.7 copy-start.3
  29.5 0.7 copy-start.4
  33.0 11.8 %collective-permute-start.1 = (f32[4,128,128]{2,1,0:T(8,128)S(1)}, f32[4,128,128]{2,1,0:T(8,128)S(1)}, u32[]{:S(2)}, u32[]{:S(2)}) collective-permute-start(f32[4,128,128]{2,1,0:T(8,128)S(1)} %get-tuple-element.27), channel_id=1, source_target_pairs={{0,28},{4,8},{8,4},{12,16},{16,12},{20,24},{24,20},{28,0},{1,29},{... | collective-permute-start | bytes 786440 | tf_op jit(solution)/shard_map/ppermute | solution.py:53
  38.4 12.2 %collective-permute-start.7 = (f32[4,128,128]{2,1,0:T(8,128)S(1)}, f32[4,128,128]{2,1,0:T(8,128)S(1)}, u32[]{:S(2)}, u32[]{:S(2)}) collective-permute-start(f32[4,128,128]{2,1,0:T(8,128)S(1)} %get-tuple-element.28), channel_id=1, source_target_pairs={{0,4},{4,0},{8,12},{12,8},{16,20},{20,16},{24,28},{28,24},{1,5},{5... | collective-permute-start | bytes 786440 | tf_op jit(solution)/shard_map/ppermute | solution.py:53
  44.9 12.3 %collective-permute-start.3 = (f32[4,128,128]{2,1,0:T(8,128)S(1)}, f32[4,128,128]{2,1,0:T(8,128)S(1)}, u32[]{:S(2)}, u32[]{:S(2)}) collective-permute-start(f32[4,128,128]{2,1,0:T(8,128)S(1)} %get-tuple-element.54), channel_id=1, source_target_pairs={{0,28},{4,8},{8,4},{12,16},{16,12},{20,24},{24,20},{28,0},{1,29},{... | collective-permute-start | bytes 786440 | tf_op jit(solution)/shard_map/ppermute | solution.py:53
  48.7 9.7 %collective-permute-start.2 = (f32[4,128,128]{2,1,0:T(8,128)S(1)}, f32[4,128,128]{2,1,0:T(8,128)S(1)}, u32[]{:S(2)}, u32[]{:S(2)}) collective-permute-start(f32[4,128,128]{2,1,0:T(8,128)S(1)} %get-tuple-element.55), channel_id=1, source_target_pairs={{0,4},{4,0},{8,12},{12,8},{16,20},{20,16},{24,28},{28,24},{1,5},{5... | collective-permute-start | bytes 786440 | tf_op jit(solution)/shard_map/ppermute | solution.py:53
  50.7 12.0 %collective-permute-start.8 = (f32[4,128,128]{2,1,0:T(8,128)S(1)}, f32[4,128,128]{2,1,0:T(8,128)S(1)}, u32[]{:S(2)}, u32[]{:S(2)}) collective-permute-start(f32[4,128,128]{2,1,0:T(8,128)S(1)} %get-tuple-element.56), channel_id=1, source_target_pairs={{0,28},{4,8},{8,4},{12,16},{16,12},{20,24},{24,20},{28,0},{1,29},{... | collective-permute-start | bytes 786440 | tf_op jit(solution)/shard_map/ppermute | solution.py:53
  53.4 9.8 %collective-permute-start.6 = (f32[4,128,128]{2,1,0:T(8,128)S(1)}, f32[4,128,128]{2,1,0:T(8,128)S(1)}, u32[]{:S(2)}, u32[]{:S(2)}) collective-permute-start(f32[4,128,128]{2,1,0:T(8,128)S(1)} %get-tuple-element.57), channel_id=1, source_target_pairs={{0,4},{4,0},{8,12},{12,8},{16,20},{20,16},{24,28},{28,24},{1,5},{5... | collective-permute-start | bytes 786440 | tf_op jit(solution)/shard_map/ppermute | solution.py:53
  58.4 11.9 %collective-permute-start.5 = (f32[4,128,128]{2,1,0:T(8,128)S(1)}, f32[4,128,128]{2,1,0:T(8,128)S(1)}, u32[]{:S(2)}, u32[]{:S(2)}) collective-permute-start(f32[4,128,128]{2,1,0:T(8,128)S(1)} %get-tuple-element.50), channel_id=1, source_target_pairs={{0,28},{4,8},{8,4},{12,16},{16,12},{20,24},{24,20},{28,0},{1,29},{... | collective-permute-start | bytes 786440 | tf_op jit(solution)/shard_map/ppermute | solution.py:53
  60.3 10.0 %collective-permute-start.4 = (f32[4,128,128]{2,1,0:T(8,128)S(1)}, f32[4,128,128]{2,1,0:T(8,128)S(1)}, u32[]{:S(2)}, u32[]{:S(2)}) collective-permute-start(f32[4,128,128]{2,1,0:T(8,128)S(1)} %get-tuple-element.51), channel_id=1, source_target_pairs={{0,4},{4,0},{8,12},{12,8},{16,20},{20,16},{24,28},{28,24},{1,5},{5... | collective-permute-start | bytes 786440 | tf_op jit(solution)/shard_map/ppermute | solution.py:53
  63.3 12.7 %collective-permute-start.12 = (f32[4,128,128]{2,1,0:T(8,128)S(1)}, f32[4,128,128]{2,1,0:T(8,128)S(1)}, u32[]{:S(2)}, u32[]{:S(2)}) collective-permute-start(f32[4,128,128]{2,1,0:T(8,128)S(1)} %get-tuple-element.52), channel_id=1, source_target_pairs={{0,28},{4,8},{8,4},{12,16},{16,12},{20,24},{24,20},{28,0},{1,29},{... | collective-permute-start | bytes 786440 | tf_op jit(solution)/shard_map/ppermute | solution.py:53
  66.9 9.1 %collective-permute-start.11 = (f32[4,128,128]{2,1,0:T(8,128)S(1)}, f32[4,128,128]{2,1,0:T(8,128)S(1)}, u32[]{:S(2)}, u32[]{:S(2)}) collective-permute-start(f32[4,128,128]{2,1,0:T(8,128)S(1)} %get-tuple-element.53), channel_id=1, source_target_pairs={{0,4},{4,0},{8,12},{12,8},{16,20},{20,16},{24,28},{28,24},{1,5},{5... | collective-permute-start | bytes 786440 | tf_op jit(solution)/shard_map/ppermute | solution.py:53
  70.4 10.8 %collective-permute-start.10 = (f32[4,128,128]{2,1,0:T(8,128)S(1)}, f32[4,128,128]{2,1,0:T(8,128)S(1)}, u32[]{:S(2)}, u32[]{:S(2)}) collective-permute-start(f32[4,128,128]{2,1,0:T(8,128)S(1)} %get-tuple-element.46), channel_id=1, source_target_pairs={{0,28},{4,8},{8,4},{12,16},{16,12},{20,24},{24,20},{28,0},{1,29},{... | collective-permute-start | bytes 786440 | tf_op jit(solution)/shard_map/ppermute | solution.py:53
  73.0 8.3 %collective-permute-start.9 = (f32[4,128,128]{2,1,0:T(8,128)S(1)}, f32[4,128,128]{2,1,0:T(8,128)S(1)}, u32[]{:S(2)}, u32[]{:S(2)}) collective-permute-start(f32[4,128,128]{2,1,0:T(8,128)S(1)} %get-tuple-element.47), channel_id=1, source_target_pairs={{0,4},{4,0},{8,12},{12,8},{16,20},{20,16},{24,28},{28,24},{1,5},{5... | collective-permute-start | bytes 786440 | tf_op jit(solution)/shard_map/ppermute | solution.py:53
  76.1 34.9 %copy-start.1 = (f32[256,256]{1,0:T(8,128)S(1)}, f32[256,256]{1,0:T(8,128)}, u32[]{:S(2)}) copy-start(f32[256,256]{1,0:T(8,128)} %weight_ref.1) | copy-start | bytes 786436
  76.1 34.9 %copy-start.2 = (f32[128,256]{1,0:T(8,128)S(1)}, f32[128,256]{1,0:T(8,128)}, u32[]{:S(2)}) copy-start(f32[128,256]{1,0:T(8,128)} %cot_ref.1) | copy-start | bytes 393220
  76.1 8.5 %collective-permute-start.14 = (f32[4,128,128]{2,1,0:T(8,128)S(1)}, f32[4,128,128]{2,1,0:T(8,128)S(1)}, u32[]{:S(2)}, u32[]{:S(2)}) collective-permute-start(f32[4,128,128]{2,1,0:T(8,128)S(1)} %get-tuple-element.48), channel_id=1, source_target_pairs={{0,28},{4,8},{8,4},{12,16},{16,12},{20,24},{24,20},{28,0},{1,29},{... | collective-permute-start | bytes 786440 | tf_op jit(solution)/shard_map/ppermute | solution.py:53
  79.3 8.4 %collective-permute-start.13 = (f32[4,128,128]{2,1,0:T(8,128)S(1)}, f32[4,128,128]{2,1,0:T(8,128)S(1)}, u32[]{:S(2)}, u32[]{:S(2)}) collective-permute-start(f32[4,128,128]{2,1,0:T(8,128)S(1)} %get-tuple-element.49), channel_id=1, source_target_pairs={{0,4},{4,0},{8,12},{12,8},{16,20},{20,16},{24,28},{28,24},{1,5},{5... | collective-permute-start | bytes 786440 | tf_op jit(solution)/shard_map/ppermute | solution.py:53

commit v4 on v3

--- a/solution.py
+++ b/solution.py
@@ -103,13 +103,12 @@
     )
 
 
-def far_kernel(count_ref, plan_ref, left_ref, own_ref, other_ref, out_a_ref, out_b_ref, high, low):
+def far_kernel(count_ref, plan_ref, left_ref, own_ref, other_ref, out_ref, high, low):
     blocks = own_ref.shape[0]
     for k, source in enumerate((own_ref, other_ref)):
         for b in range(blocks):
             high[k * blocks + b], low[k * blocks + b] = halves(source[b])
-    out_a_ref[...] = jnp.zeros_like(out_a_ref)
-    out_b_ref[...] = jnp.zeros_like(out_b_ref)
+    out_ref[...] = jnp.zeros_like(out_ref)
 
     @pl.loop(0, count_ref[0])
     def _(slot):
@@ -118,9 +117,7 @@
 
         @pl.when((place >= 0) & (place < NZH))
         def _():
-            value = slot_product(left_ref[slot], high[plan % 16], low[plan % 16])
-            out_a_ref[place] += value[:, :LANES]
-            out_b_ref[place] += value[:, LANES:]
+            out_ref[place] += slot_product(left_ref[slot], high[plan % 16], low[plan % 16])
 
 
 def far_products(count, plan, left, own, other):
@@ -130,26 +127,25 @@
     vmem = pl.BlockSpec(memory_space=pltpu.VMEM)
     return pl.pallas_call(
         far_kernel,
-        out_shape=[jax.ShapeDtypeStruct((NZH, tile, LANES), jnp.float32)] * 2 + [blocks] * 2,
+        out_shape=[jax.ShapeDtypeStruct((NZH, tile, 2 * LANES), jnp.float32)] + [blocks] * 2,
         in_specs=[smem, smem, vmem, vmem, vmem],
-        out_specs=[vmem] * 4,
+        out_specs=[vmem] * 3,
         compiler_params=pltpu.CompilerParams(vmem_limit_bytes=16 * 1024 * 1024),
         cost_estimate=pl.CostEstimate(flops=10**9, bytes_accessed=8 * 2**20, transcendentals=0),
     )(count, plan, left, own, other)
 
 
-def product_kernel(count_ref, plan_ref, left_ref, high_ref, low_ref, out_a_ref, out_b_ref):
-    out_a_ref[...] = jnp.zeros_like(out_a_ref)
-    out_b_ref[...] = jnp.zeros_like(out_b_ref)
+def product_kernel(count_ref, plan_ref, left_ref, high_ref, low_ref, out_ref):
+    out_ref[...] = jnp.zeros_like(out_ref)
 
     @pl.loop(0, (count_ref[0] + GROUP - 1) // GROUP)
     def _(step):
         for k in range(GROUP):
             slot = step * GROUP + k
             plan = plan_ref[slot]
-            value = slot_product(left_ref[slot], high_ref[plan % 16], low_ref[plan % 16])
-            out_a_ref[plan // 16] += value[:, :LANES]
-            out_b_ref[plan // 16] += value[:, LANES:]
+            out_ref[plan // 16] += slot_product(
+                left_ref[slot], high_ref[plan % 16], low_ref[plan % 16]
+            )
 
 
 def products(count, plan, left, high, low):
@@ -158,13 +154,11 @@
     vmem = pl.BlockSpec(memory_space=pltpu.VMEM)
     return pl.pallas_call(
         product_kernel,
-        out_shape=[jax.ShapeDtypeStruct((NY * NZH + 1, tile, LANES), jnp.float32)] * 2,
+        out_shape=jax.ShapeDtypeStruct((NY * NZH + 1, tile, 2 * LANES), jnp.float32),
         in_specs=[smem, smem, vmem, vmem, vmem],
-        out_specs=[vmem, vmem],
+        out_specs=vmem,
         compiler_params=pltpu.CompilerParams(vmem_limit_bytes=20 * 1024 * 1024),
-        cost_estimate=pl.CostEstimate(
-            flops=12 * slots * tile * tile * LANES, bytes_accessed=8 * 2**20, transcendentals=0
-        ),
+        cost_estimate=pl.CostEstimate(flops=10**6, bytes_accessed=2**16, transcendentals=0),
     )(count, plan, left, high, low)
 
 
@@ -194,24 +188,20 @@
     )(terms, weight, cotangent)
 
 
-def after(values, witness):
-    here = lax.optimization_barrier((*(v for v in values if v is not None), witness))
-    return [None if v is None else here[sum(u is not None for u in values[:k])] for k, v in enumerate(values)]
+def after(value, witness):
+    return lax.optimization_barrier((value, witness))[0]
 
 
 def chunk(sums, ahead):
     return sums[ahead * NZH : (ahead + 1) * NZH]
 
 
-def advance(sums, step, got):
-    pair = [chunk(sums, ROUNDS - step), chunk(sums, (ROUNDS + step) % NY)]
-    if step == ROUNDS:
-        return pair[0] + (got[0] + got[1])
-    return [v if g is None else v + g for v, g in zip(pair, got[::-1])]
-
-
-def send(pair):
-    return trade(pair[0], RING, 0), trade(pair[1], RING, 1)
+def advance(sums, step, way, got):
+    part = chunk(sums, (ROUNDS + (2 * way - 1) * step) % NY)
+    if step == 1:
+        rest = ((0, 0), (0, 0))
+        got = jnp.pad(got, ((NZH // 2 * (1 - way), NZH // 2 * way), *rest))
+    return part + got
 
 
 def body(features, adjacency_tiles, tile_rows, tile_cols, tile_count, weight, cotangent):
@@ -219,19 +209,21 @@
     own = share(features, ("x", "zl"))
     other = lax.ppermute(own, "c", [(0, 1), (1, 0)])
     left = split_tiles(adjacency_tiles)
-    far_a, far_b, high, low = far_products(tile_count, plan, left, own, other)
-    got_a = (None, trade(far_a, RING, 1))
-    got_b = (trade(far_b, RING, 0), None)
-    sums_a, sums_b = products(tile_count, plan, left, high, low)
-    out_b = [far_b]
+    far, high, low = far_products(tile_count, plan, left, own, other)
+    got = [trade(far[: NZH // 2], RING, 0), trade(far[NZH // 2 :], RING, 1)]
+    sums = products(tile_count, plan, left, high, low)
+    made = sums
+    got = lax.optimization_barrier(got)
+    first = 1
     for step in range(1, ROUNDS):
-        out_a = advance(sums_a, step, after(got_a, out_b[0]))
-        got_a = send(out_a)
-        out_b = advance(sums_b, step, after(got_b, out_a[0]))
-        got_b = send(out_b)
-    last_a = advance(sums_a, ROUNDS, after(got_a, out_b[0]))
-    last_b = advance(sums_b, ROUNDS, after(got_b, last_a))
-    terms = swap(jnp.concatenate([last_a, last_b], axis=2), "zh")
+        came = got
+        got = [None, None]
+        for way in (first, 1 - first):
+            made = advance(sums, step, way, after(came[1 - way], made))
+            got[way] = trade(made, RING, way)
+        first = 1 - first
+    whole = lax.optimization_barrier(chunk(sums, 0) + after(got[1 - first], made))
+    terms = swap(whole + got[first], "zh")
     activated, grad = node_step(terms, weight, cotangent)
     grad = jnp.sum(swap(grad, NEAR), axis=0)
     grad = jnp.sum(share(grad, FAR), axis=0)

time: 159 us -> 167 us (1.050)
  waiting for transfers between devices: 9.55 us -> 31.5 us
  starting transfers between devices: 47.1 us -> 34.6 us
  Pallas kernels: 7.49 us -> 4.58 us
  blocking collectives: 87.8 us -> 89.7 us
    ppermute x14 -> x8, waiting for transfers between devices: 9.55 us -> 31.5 us  [trade(): lax.ppermute(v, axis, [(k, (k + 1 - 2 * ((k + way) % 2)) % n) for k in ra...]
    ppermute x14 -> x8, starting transfers between devices: 41.4 us -> 28.8 us  [trade(): lax.ppermute(v, axis, [(k, (k + 1 - 2 * ((k + way) % 2)) % n) for k in ra...]
    pallas_call x2, Pallas kernels: 5.9 us -> 2.98 us  [the longest x1 1.79 us: products(): pl.pallas_call(product_kernel, out_shape=jax.ShapeDtypeStruct((NY * NZH +...]
    all_to_all x5, blocking collectives: 87.8 us -> 89.7 us  [swap(): return lax.all_to_all(v, axes, split_axis=0, concat_axis=0, tiled=True)]
  transfers between devices with their start and end apart: 15 -> 9, of which waited for: 5 -> 7; matrix products, arithmetic and copies ran while one was open for 0% -> 0% of each run, Pallas kernels for 2% -> 1%
where the time goes in v4:
time: 167 us
  blocking collectives  89.7 us (54%)
  starting transfers between devices  34.6 us (21%)
  waiting for transfers between devices  31.5 us (19%)
  Pallas kernels  4.58 us (3%)
  local copies, waits for them, and re-layouts  3.96 us (2%)
    all_to_all x5, blocking collectives, swap(): return lax.all_to_all(v, axes, split_axis=0, concat_axis=0, tiled=True)  89.7 us
    ppermute x8, waiting for transfers between devices, trade(): lax.ppermute(v, axis, [(k, (k + 1 - 2 * ((k + way) % 2)) % n) for k in ra...  31.5 us
    ppermute x8, starting transfers between devices, trade(): lax.ppermute(v, axis, [(k, (k + 1 - 2 * ((k + way) % 2)) % n) for k in ra...  28.8 us
    ppermute x1, starting transfers between devices, body(): other = lax.ppermute(own, 'c', [(0, 1), (1, 0)])  5.8 us
  transfers between devices with their start and end apart: 9, of which 7 were waited for; matrix products, arithmetic and copies ran while one was open for 0% of the time, Pallas kernels for 1%

profile of v4, /device:TPU:1, one launch (start us, length us, event | category | flops | bytes accessed | tf_op | source)
XLA Modules:
  0.0 166.6 jit_solution(13772100313501813823)
XLA Ops:
  0.6 1.0 broadcast_in_dim.11
  1.6 19.3 %all_to_all.25.own_ref = f32[8,128,256]{2,1,0:T(8,128)S(1)} all-to-all(f32[8,128,256]{2,1,0:T(8,128)S(1)} %broadcast_in_dim.11), channel_id=1, replica_groups=mesh['x'=4,'zl'=2,'c'=2,'yh'=4,'yl'=2,'zh'=4] {'x','zl'}, dimensions={0} | all-to-all | bytes 2097152 | tf_op jit(solution)/shard_map/all_to_all | solution.py:63
  21.0 5.8 %collective-permute-start = (f32[8,128,256]{2,1,0:T(8,128)S(1)}, f32[8,128,256]{2,1,0:T(8,128)S(1)}, u32[]{:S(2)}, u32[]{:S(2)}) collective-permute-start(f32[8,128,256]{2,1,0:T(8,128)S(1)} %all_to_all.25.own_ref), channel_id=1, source_target_pairs={{0,32},{32,0},{1,33},{33,1},{2,34},{34,2},{3,35},{35,3},{4,36},{36... | collective-permute-start | bytes 3145736 | tf_op jit(solution)/shard_map/ppermute | solution.py:210
  27.4 2.2 %copy-done = f32[64,128,128]{2,1,0:T(8,128)S(1)} copy-done((f32[64,128,128]{2,1,0:T(8,128)S(1)}, f32[64,128,128]{2,1,0:T(8,128)}, u32[]{:S(2)}) %copy-start) | copy-done | bytes 4194328
  29.6 0.6 shard_map.86.left_ref
  30.3 1.2 shard_map.87
  31.6 5.3 %collective-permute-start.2 = (f32[2,128,256]{2,1,0:T(8,128)S(1)}, f32[2,128,256]{2,1,0:T(8,128)S(1)}, u32[]{:S(2)}, u32[]{:S(2)}) collective-permute-start(f32[2,128,256]{2,1,0:T(8,128)S(1)} %get-tuple-element.30), channel_id=1, source_target_pairs={{0,28},{4,8},{8,4},{12,16},{16,12},{20,24},{24,20},{28,0},{1,29},{... | collective-permute-start | bytes 786440 | tf_op jit(solution)/shard_map/ppermute | solution.py:53
  36.9 2.6 %collective-permute-start.1 = (f32[2,128,256]{2,1,0:T(8,128)S(1)}, f32[2,128,256]{2,1,0:T(8,128)S(1)}, u32[]{:S(2)}, u32[]{:S(2)}) collective-permute-start(f32[2,128,256]{2,1,0:T(8,128)S(1)} %get-tuple-element.31), channel_id=1, source_target_pairs={{0,4},{4,0},{8,12},{12,8},{16,20},{20,16},{24,28},{28,24},{1,5},{5... | collective-permute-start | bytes 786440 | tf_op jit(solution)/shard_map/ppermute | solution.py:53
  39.4 1.8 %shard_map.88 = f32[33,128,256]{2,1,0:T(8,128)S(1)} custom-call(s32[1]{0:T(128)} %copy.10.count_ref, s32[64]{0:T(128)S(1)} %fusion.7.plan_ref, bf16[64,128,256]{2,1,0:T(8,128)(2,1)S(1)} %shard_map.86.left_ref, bf16[16,128,256]{2,1,0:T(8,128)(2,1)S(1)} %get-tuple-element.16.high_ref, bf16[16,128,256]{2,1,0:T(8,128)(2,1)S(1)} %get-tuple-element.17.low_ref), custom_call_target="tpu_custom_call" | custom-call | flops 1000000 | bytes 65536 | tf_op jit(solution)/shard_map/pallas_call | solution.py:155
  41.3 0.9 collective-permute-done.2
  42.1 2.8 %collective-permute-done.1 = f32[2,128,256]{2,1,0:T(8,128)S(1)} collective-permute-done((f32[2,128,256]{2,1,0:T(8,128)S(1)}, f32[2,128,256]{2,1,0:T(8,128)S(1)}, u32[]{:S(2)}, u32[]{:S(2)}) %collective-permute-start.1) | collective-permute-done | bytes 262176 | tf_op jit(solution)/shard_map/ppermute | solution.py:53
  45.0 5.7 %collective-permute-start.3 = (f32[4,128,256]{2,1,0:T(8,128)S(1)}, f32[4,128,256]{2,1,0:T(8,128)S(1)}, u32[]{:S(2)}, u32[]{:S(2)}) collective-permute-start(f32[4,128,256]{2,1,0:T(8,128)S(1)} %slice_add_fusion.3), channel_id=1, source_target_pairs={{0,28},{4,8},{8,4},{12,16},{16,12},{20,24},{24,20},{28,0},{1,29},{... | collective-permute-start | bytes 1572872 | tf_op jit(solution)/shard_map/ppermute | solution.py:53
  50.8 1.9 %collective-permute-start.5 = (f32[4,128,256]{2,1,0:T(8,128)S(1)}, f32[4,128,256]{2,1,0:T(8,128)S(1)}, u32[]{:S(2)}, u32[]{:S(2)}) collective-permute-start(f32[4,128,256]{2,1,0:T(8,128)S(1)} %slice_add_fusion.2), channel_id=1, source_target_pairs={{0,4},{4,0},{8,12},{12,8},{16,20},{20,16},{24,28},{28,24},{1,5},{5... | collective-permute-start | bytes 1572872 | tf_op jit(solution)/shard_map/ppermute | solution.py:53
  52.7 8.9 %collective-permute-done.3 = f32[4,128,256]{2,1,0:T(8,128)S(1)} collective-permute-done((f32[4,128,256]{2,1,0:T(8,128)S(1)}, f32[4,128,256]{2,1,0:T(8,128)S(1)}, u32[]{:S(2)}, u32[]{:S(2)}) %collective-permute-start.3) | collective-permute-done | bytes 524320 | tf_op jit(solution)/shard_map/ppermute | solution.py:53
  61.7 2.1 %collective-permute-start.4 = (f32[4,128,256]{2,1,0:T(8,128)S(1)}, f32[4,128,256]{2,1,0:T(8,128)S(1)}, u32[]{:S(2)}, u32[]{:S(2)}) collective-permute-start(f32[4,128,256]{2,1,0:T(8,128)S(1)} %slice_add_fusion.4), channel_id=1, source_target_pairs={{0,4},{4,0},{8,12},{12,8},{16,20},{20,16},{24,28},{28,24},{1,5},{5... | collective-permute-start | bytes 1572872 | tf_op jit(solution)/shard_map/ppermute | solution.py:53
  63.8 1.7 %collective-permute-done.5 = f32[4,128,256]{2,1,0:T(8,128)S(1)} collective-permute-done((f32[4,128,256]{2,1,0:T(8,128)S(1)}, f32[4,128,256]{2,1,0:T(8,128)S(1)}, u32[]{:S(2)}, u32[]{:S(2)}) %collective-permute-start.5) | collective-permute-done | bytes 524320 | tf_op jit(solution)/shard_map/ppermute | solution.py:53
  65.5 0.1 slice_add_fusion.1
  65.5 3.6 %collective-permute-start.7 = (f32[4,128,256]{2,1,0:T(8,128)S(1)}, f32[4,128,256]{2,1,0:T(8,128)S(1)}, u32[]{:S(2)}, u32[]{:S(2)}) collective-permute-start(f32[4,128,256]{2,1,0:T(8,128)S(1)} %slice_add_fusion.1), channel_id=1, source_target_pairs={{0,28},{4,8},{8,4},{12,16},{16,12},{20,24},{24,20},{28,0},{1,29},{... | collective-permute-start | bytes 1572872 | tf_op jit(solution)/shard_map/ppermute | solution.py:53
  69.2 6.4 %collective-permute-done.4 = f32[4,128,256]{2,1,0:T(8,128)S(1)} collective-permute-done((f32[4,128,256]{2,1,0:T(8,128)S(1)}, f32[4,128,256]{2,1,0:T(8,128)S(1)}, u32[]{:S(2)}, u32[]{:S(2)}) %collective-permute-start.4) | collective-permute-done | bytes 524320 | tf_op jit(solution)/shard_map/ppermute | solution.py:53
  75.5 0.1 slice_add_fusion.5
  75.6 5.7 %collective-permute-start.6 = (f32[4,128,256]{2,1,0:T(8,128)S(1)}, f32[4,128,256]{2,1,0:T(8,128)S(1)}, u32[]{:S(2)}, u32[]{:S(2)}) collective-permute-start(f32[4,128,256]{2,1,0:T(8,128)S(1)} %slice_add_fusion.5), channel_id=1, source_target_pairs={{0,28},{4,8},{8,4},{12,16},{16,12},{20,24},{24,20},{28,0},{1,29},{... | collective-permute-start | bytes 1572872 | tf_op jit(solution)/shard_map/ppermute | solution.py:53
  81.3 0.1 slice_add_fusion
  81.4 1.9 %collective-permute-start.8 = (f32[4,128,256]{2,1,0:T(8,128)S(1)}, f32[4,128,256]{2,1,0:T(8,128)S(1)}, u32[]{:S(2)}, u32[]{:S(2)}) collective-permute-start(f32[4,128,256]{2,1,0:T(8,128)S(1)} %slice_add_fusion), channel_id=1, source_target_pairs={{0,4},{4,0},{8,12},{12,8},{16,20},{20,16},{24,28},{28,24},{1,5},{5... | collective-permute-start | bytes 1572872 | tf_op jit(solution)/shard_map/ppermute | solution.py:53
  83.3 8.1 %collective-permute-done.6 = f32[4,128,256]{2,1,0:T(8,128)S(1)} collective-permute-done((f32[4,128,256]{2,1,0:T(8,128)S(1)}, f32[4,128,256]{2,1,0:T(8,128)S(1)}, u32[]{:S(2)}, u32[]{:S(2)}) %collective-permute-start.6) | collective-permute-done | bytes 524320 | tf_op jit(solution)/shard_map/ppermute | solution.py:53
  91.5 2.7 %collective-permute-done.8 = f32[4,128,256]{2,1,0:T(8,128)S(1)} collective-permute-done((f32[4,128,256]{2,1,0:T(8,128)S(1)}, f32[4,128,256]{2,1,0:T(8,128)S(1)}, u32[]{:S(2)}, u32[]{:S(2)}) %collective-permute-start.8) | collective-permute-done | bytes 524320 | tf_op jit(solution)/shard_map/ppermute | solution.py:53
  94.3 0.1 add.82
  94.3 23.2 %all_to_all.26.terms_ref = f32[4,128,256]{2,1,0:T(8,128)S(1)} all-to-all(f32[4,128,256]{2,1,0:T(8,128)S(1)} %add.82), channel_id=1, replica_groups=mesh['x'=4,'zl'=2,'c'=2,'yh'=4,'yl'=2,'zh'=4] {'zh'}, dimensions={0} | all-to-all | bytes 1048576 | tf_op jit(solution)/shard_map/all_to_all | solution.py:63
  117.5 1.0 shard_map.89
  118.5 15.7 %all_to_all.27 = f32[32,2,8,128]{3,2,1,0:T(8,128)S(1)} all-to-all(f32[32,2,8,128]{3,2,1,0:T(8,128)S(1)} %get-tuple-element.29), channel_id=1, replica_groups=mesh['x'=4,'zl'=2,'c'=2,'yh'=4,'yl'=2,'zh'=4] {'x','zl','c','yl'}, dimensions={0} | all-to-all | bytes 524288 | tf_op jit(solution)/shard_map/all_to_all | solution.py:63
  134.3 18.4 %all_to_all.28 = f32[16,2,8,128]{3,2,1,0:T(8,128)S(1)} all-to-all(f32[16,2,8,128]{3,2,1,0:T(8,128)S(1)} %broadcast_in_dim.12), channel_id=1, replica_groups=mesh['x'=4,'zl'=2,'c'=2,'yh'=4,'yl'=2,'zh'=4] {'yh','zh'}, dimensions={0} | all-to-all | bytes 262144 | tf_op jit(solution)/shard_map/all_to_all | solution.py:63
  152.7 13.1 %all_to_all.29 = f32[32,2,8,128]{3,2,1,0:T(8,128)S(1)} all-to-all(f32[32,2,8,128]{3,2,1,0:T(8,128)S(1)} %broadcast_in_dim.13), channel_id=1, replica_groups=mesh['x'=4,'zl'=2,'c'=2,'yh'=4,'yl'=2,'zh'=4] {'x','zl','c','yl'}, dimensions={0} | all-to-all | bytes 524288 | tf_op jit(solution)/shard_map/all_to_all | solution.py:63
  165.8 0.7 copy.11
  (21 shorter events, 0.4 us)
Async XLA Ops:
  21.0 9.3 %copy-start.3 = (s32[64]{0:T(128)S(1)}, s32[64]{0:T(128)}, u32[]{:S(2)}) copy-start(s32[64]{0:T(128)} %param.10) | copy-start | bytes 772
  21.0 9.3 %copy-start.4 = (s32[64]{0:T(128)S(1)}, s32[64]{0:T(128)}, u32[]{:S(2)}) copy-start(s32[64]{0:T(128)} %param.9) | copy-start | bytes 772
  21.0 9.3 %collective-permute-start = (f32[8,128,256]{2,1,0:T(8,128)S(1)}, f32[8,128,256]{2,1,0:T(8,128)S(1)}, u32[]{:S(2)}, u32[]{:S(2)}) collective-permute-start(f32[8,128,256]{2,1,0:T(8,128)S(1)} %all_to_all.25.own_ref), channel_id=1, source_target_pairs={{0,32},{32,0},{1,33},{33,1},{2,34},{34,2},{3,35},{35,3},{4,36},{36... | collective-permute-start | bytes 3145736 | tf_op jit(solution)/shard_map/ppermute | solution.py:210
  27.4 2.2 %copy-start = (f32[64,128,128]{2,1,0:T(8,128)S(1)}, f32[64,128,128]{2,1,0:T(8,128)}, u32[]{:S(2)}) copy-start(f32[64,128,128]{2,1,0:T(8,128)} %tiles_ref.1) | copy-start | bytes 12582916
  31.6 10.6 %collective-permute-start.2 = (f32[2,128,256]{2,1,0:T(8,128)S(1)}, f32[2,128,256]{2,1,0:T(8,128)S(1)}, u32[]{:S(2)}, u32[]{:S(2)}) collective-permute-start(f32[2,128,256]{2,1,0:T(8,128)S(1)} %get-tuple-element.30), channel_id=1, source_target_pairs={{0,28},{4,8},{8,4},{12,16},{16,12},{20,24},{24,20},{28,0},{1,29},{... | collective-permute-start | bytes 786440 | tf_op jit(solution)/shard_map/ppermute | solution.py:53
  36.9 8.1 %collective-permute-start.1 = (f32[2,128,256]{2,1,0:T(8,128)S(1)}, f32[2,128,256]{2,1,0:T(8,128)S(1)}, u32[]{:S(2)}, u32[]{:S(2)}) collective-permute-start(f32[2,128,256]{2,1,0:T(8,128)S(1)} %get-tuple-element.31), channel_id=1, source_target_pairs={{0,4},{4,0},{8,12},{12,8},{16,20},{20,16},{24,28},{28,24},{1,5},{5... | collective-permute-start | bytes 786440 | tf_op jit(solution)/shard_map/ppermute | solution.py:53
  45.0 16.6 %collective-permute-start.3 = (f32[4,128,256]{2,1,0:T(8,128)S(1)}, f32[4,128,256]{2,1,0:T(8,128)S(1)}, u32[]{:S(2)}, u32[]{:S(2)}) collective-permute-start(f32[4,128,256]{2,1,0:T(8,128)S(1)} %slice_add_fusion.3), channel_id=1, source_target_pairs={{0,28},{4,8},{8,4},{12,16},{16,12},{20,24},{24,20},{28,0},{1,29},{... | collective-permute-start | bytes 1572872 | tf_op jit(solution)/shard_map/ppermute | solution.py:53
  50.8 14.7 %collective-permute-start.5 = (f32[4,128,256]{2,1,0:T(8,128)S(1)}, f32[4,128,256]{2,1,0:T(8,128)S(1)}, u32[]{:S(2)}, u32[]{:S(2)}) collective-permute-start(f32[4,128,256]{2,1,0:T(8,128)S(1)} %slice_add_fusion.2), channel_id=1, source_target_pairs={{0,4},{4,0},{8,12},{12,8},{16,20},{20,16},{24,28},{28,24},{1,5},{5... | collective-permute-start | bytes 1572872 | tf_op jit(solution)/shard_map/ppermute | solution.py:53
  61.7 55.9 %copy-start.1 = (f32[256,256]{1,0:T(8,128)S(1)}, f32[256,256]{1,0:T(8,128)}, u32[]{:S(2)}) copy-start(f32[256,256]{1,0:T(8,128)} %weight_ref.1) | copy-start | bytes 786436
  61.7 55.8 %copy-start.2 = (f32[128,256]{1,0:T(8,128)S(1)}, f32[128,256]{1,0:T(8,128)}, u32[]{:S(2)}) copy-start(f32[128,256]{1,0:T(8,128)} %cot_ref.1) | copy-start | bytes 393220
  61.7 13.8 %collective-permute-start.4 = (f32[4,128,256]{2,1,0:T(8,128)S(1)}, f32[4,128,256]{2,1,0:T(8,128)S(1)}, u32[]{:S(2)}, u32[]{:S(2)}) collective-permute-start(f32[4,128,256]{2,1,0:T(8,128)S(1)} %slice_add_fusion.4), channel_id=1, source_target_pairs={{0,4},{4,0},{8,12},{12,8},{16,20},{20,16},{24,28},{28,24},{1,5},{5... | collective-permute-start | bytes 1572872 | tf_op jit(solution)/shard_map/ppermute | solution.py:53
  65.5 15.8 %collective-permute-start.7 = (f32[4,128,256]{2,1,0:T(8,128)S(1)}, f32[4,128,256]{2,1,0:T(8,128)S(1)}, u32[]{:S(2)}, u32[]{:S(2)}) collective-permute-start(f32[4,128,256]{2,1,0:T(8,128)S(1)} %slice_add_fusion.1), channel_id=1, source_target_pairs={{0,28},{4,8},{8,4},{12,16},{16,12},{20,24},{24,20},{28,0},{1,29},{... | collective-permute-start | bytes 1572872 | tf_op jit(solution)/shard_map/ppermute | solution.py:53
  75.6 15.9 %collective-permute-start.6 = (f32[4,128,256]{2,1,0:T(8,128)S(1)}, f32[4,128,256]{2,1,0:T(8,128)S(1)}, u32[]{:S(2)}, u32[]{:S(2)}) collective-permute-start(f32[4,128,256]{2,1,0:T(8,128)S(1)} %slice_add_fusion.5), channel_id=1, source_target_pairs={{0,28},{4,8},{8,4},{12,16},{16,12},{20,24},{24,20},{28,0},{1,29},{... | collective-permute-start | bytes 1572872 | tf_op jit(solution)/shard_map/ppermute | solution.py:53
  81.4 12.9 %collective-permute-start.8 = (f32[4,128,256]{2,1,0:T(8,128)S(1)}, f32[4,128,256]{2,1,0:T(8,128)S(1)}, u32[]{:S(2)}, u32[]{:S(2)}) collective-permute-start(f32[4,128,256]{2,1,0:T(8,128)S(1)} %slice_add_fusion), channel_id=1, source_target_pairs={{0,4},{4,0},{8,12},{12,8},{16,20},{20,16},{24,28},{28,24},{1,5},{5... | collective-permute-start | bytes 1572872 | tf_op jit(solution)/shard_map/ppermute | solution.py:53

commit v5 on v3

--- a/solution.py
+++ b/solution.py
@@ -69,10 +69,22 @@
 
 def slot_plan(tile_rows, tile_cols, tile_count):
     ids = jnp.arange(tile_rows.shape[0], dtype=jnp.int32)
-    place = ahead(tile_rows // NZH, RING) * NZH + tile_rows % NZH
-    place = jnp.where(ids < tile_count[0], place, NY * NZH)
+    far = ahead(tile_rows // NZH, RING)
+    away = jnp.minimum(far, NY - far)
+    key = jnp.where(ids < tile_count[0], jnp.minimum(ROUNDS - away, 2), 3)
+    row = tile_rows % NZH + NZH * (
+        jnp.where(far > ROUNDS, 1, 0) + jnp.where(away == 1, 3, jnp.where(away == 0, 2, 0))
+    )
     core = lax.rem(tile_cols % NC + lax.axis_index("c"), NC)
-    return place * 16 + core * (NX * NZL) + tile_cols // NC
+    packed = (ids * 32 + row) * 16 + core * (NX * NZL) + tile_cols // NC
+    before = (key[None, :] < key[:, None]) | (
+        (key[None, :] == key[:, None]) & (ids[None, :] < ids[:, None])
+    )
+    place = jnp.sum(before.astype(jnp.int32), axis=1)
+    ordered = jnp.sum(jnp.where(place[None, :] == ids[:, None], packed[None, :], 0), axis=1)
+    marks = jnp.arange(8, dtype=jnp.int32)
+    starts = jnp.sum((key[None, :] < marks[:, None]).astype(jnp.int32), axis=1)
+    return ordered, starts
 
 
 def split_kernel(tiles_ref, out_ref):
@@ -103,69 +115,47 @@
     )
 
 
-def far_kernel(count_ref, plan_ref, left_ref, own_ref, other_ref, out_a_ref, out_b_ref, high, low):
+def add_products(step, starts_ref, order_ref, left_ref, high, low, out_a_ref, out_b_ref):
+    first, last = starts_ref[step], starts_ref[step + 1]
+    slots, spare = order_ref.shape[0], out_a_ref.shape[0] - 1
+    out_a_ref[...] = jnp.zeros_like(out_a_ref)
+    out_b_ref[...] = jnp.zeros_like(out_b_ref)
+
+    @pl.loop(0, (last - first + GROUP - 1) // GROUP)
+    def _(group):
+        for k in range(GROUP):
+            index = first + group * GROUP + k
+            packed = order_ref[jnp.minimum(index, slots - 1)]
+            row = jnp.where(index < last, packed // 16 % 32, spare)
+            value = slot_product(left_ref[packed // 512], high[packed % 16], low[packed % 16])
+            out_a_ref[row] += value[:, :LANES]
+            out_b_ref[row] += value[:, LANES:]
+
+
+def first_kernel(starts_ref, order_ref, left_ref, own_ref, other_ref, out_a_ref, out_b_ref, high, low):
     blocks = own_ref.shape[0]
     for k, source in enumerate((own_ref, other_ref)):
         for b in range(blocks):
             high[k * blocks + b], low[k * blocks + b] = halves(source[b])
-    out_a_ref[...] = jnp.zeros_like(out_a_ref)
-    out_b_ref[...] = jnp.zeros_like(out_b_ref)
-
-    @pl.loop(0, count_ref[0])
-    def _(slot):
-        plan = plan_ref[slot]
-        place = plan // 16 - ROUNDS * NZH
-
-        @pl.when((place >= 0) & (place < NZH))
-        def _():
-            value = slot_product(left_ref[slot], high[plan % 16], low[plan % 16])
-            out_a_ref[place] += value[:, :LANES]
-            out_b_ref[place] += value[:, LANES:]
-
-
-def far_products(count, plan, left, own, other):
+    add_products(0, starts_ref, order_ref, left_ref, high, low, out_a_ref, out_b_ref)
+
+
+def sums_of(step, starts, ordered, left, sources):
     tile = left.shape[1]
-    blocks = jax.ShapeDtypeStruct((2 * own.shape[0], tile, 2 * LANES), jnp.bfloat16)
+    rows = NZH * (1, 2, 5)[step] + 1
+    shapes = [jax.ShapeDtypeStruct((rows, tile, LANES), jnp.float32)] * 2
+    if step == 0:
+        shapes += [jax.ShapeDtypeStruct((2 * sources[0].shape[0], tile, 2 * LANES), jnp.bfloat16)] * 2
     smem = pl.BlockSpec(memory_space=pltpu.SMEM)
     vmem = pl.BlockSpec(memory_space=pltpu.VMEM)
     return pl.pallas_call(
-        far_kernel,
-        out_shape=[jax.ShapeDtypeStruct((NZH, tile, LANES), jnp.float32)] * 2 + [blocks] * 2,
+        functools.partial(add_products, step) if step else first_kernel,
+        out_shape=shapes,
         in_specs=[smem, smem, vmem, vmem, vmem],
-        out_specs=[vmem] * 4,
+        out_specs=[vmem] * len(shapes),
         compiler_params=pltpu.CompilerParams(vmem_limit_bytes=16 * 1024 * 1024),
-        cost_estimate=pl.CostEstimate(flops=10**9, bytes_accessed=8 * 2**20, transcendentals=0),
-    )(count, plan, left, own, other)
-
-
-def product_kernel(count_ref, plan_ref, left_ref, high_ref, low_ref, out_a_ref, out_b_ref):
-    out_a_ref[...] = jnp.zeros_like(out_a_ref)
-    out_b_ref[...] = jnp.zeros_like(out_b_ref)
-
-    @pl.loop(0, (count_ref[0] + GROUP - 1) // GROUP)
-    def _(step):
-        for k in range(GROUP):
-            slot = step * GROUP + k
-            plan = plan_ref[slot]
-            value = slot_product(left_ref[slot], high_ref[plan % 16], low_ref[plan % 16])
-            out_a_ref[plan // 16] += value[:, :LANES]
-            out_b_ref[plan // 16] += value[:, LANES:]
-
-
-def products(count, plan, left, high, low):
-    slots, tile, _ = left.shape
-    smem = pl.BlockSpec(memory_space=pltpu.SMEM)
-    vmem = pl.BlockSpec(memory_space=pltpu.VMEM)
-    return pl.pallas_call(
-        product_kernel,
-        out_shape=[jax.ShapeDtypeStruct((NY * NZH + 1, tile, LANES), jnp.float32)] * 2,
-        in_specs=[smem, smem, vmem, vmem, vmem],
-        out_specs=[vmem, vmem],
-        compiler_params=pltpu.CompilerParams(vmem_limit_bytes=20 * 1024 * 1024),
-        cost_estimate=pl.CostEstimate(
-            flops=12 * slots * tile * tile * LANES, bytes_accessed=8 * 2**20, transcendentals=0
-        ),
-    )(count, plan, left, high, low)
+        cost_estimate=pl.CostEstimate(flops=10**6, bytes_accessed=2**14, transcendentals=0),
+    )(starts, ordered, left, *sources)
 
 
 def node_kernel(terms_ref, weight_ref, cot_ref, act_ref, grad_ref):
@@ -199,15 +189,13 @@
     return [None if v is None else here[sum(u is not None for u in values[:k])] for k, v in enumerate(values)]
 
 
-def chunk(sums, ahead):
-    return sums[ahead * NZH : (ahead + 1) * NZH]
-
-
-def advance(sums, step, got):
-    pair = [chunk(sums, ROUNDS - step), chunk(sums, (ROUNDS + step) % NY)]
-    if step == ROUNDS:
-        return pair[0] + (got[0] + got[1])
+def advance(sums, first, got):
+    pair = [sums[first : first + NZH], sums[first + NZH : first + 2 * NZH]]
     return [v if g is None else v + g for v, g in zip(pair, got[::-1])]
+
+
+def finish(sums, got):
+    return sums[2 * NZH : 3 * NZH] + (got[0] + got[1])
 
 
 def send(pair):
@@ -215,22 +203,25 @@
 
 
 def body(features, adjacency_tiles, tile_rows, tile_cols, tile_count, weight, cotangent):
-    plan = slot_plan(tile_rows, tile_cols, tile_count)
+    ordered, starts = slot_plan(tile_rows, tile_cols, tile_count)
     own = share(features, ("x", "zl"))
     other = lax.ppermute(own, "c", [(0, 1), (1, 0)])
     left = split_tiles(adjacency_tiles)
-    far_a, far_b, high, low = far_products(tile_count, plan, left, own, other)
+    far_a, far_b, high, low = sums_of(0, starts, ordered, left, (own, other))
+    far_a, far_b = far_a[:NZH], far_b[:NZH]
     got_a = (None, trade(far_a, RING, 1))
     got_b = (trade(far_b, RING, 0), None)
-    sums_a, sums_b = products(tile_count, plan, left, high, low)
     out_b = [far_b]
     for step in range(1, ROUNDS):
-        out_a = advance(sums_a, step, after(got_a, out_b[0]))
+        if step < 3:
+            sums_a, sums_b = sums_of(step, after((starts,), out_b[0])[0], ordered, left, (high, low))
+        first = 0 if step < 3 else 3 * NZH
+        out_a = advance(sums_a, first, after(got_a, out_b[0]))
         got_a = send(out_a)
-        out_b = advance(sums_b, step, after(got_b, out_a[0]))
+        out_b = advance(sums_b, first, after(got_b, out_a[0]))
         got_b = send(out_b)
-    last_a = advance(sums_a, ROUNDS, after(got_a, out_b[0]))
-    last_b = advance(sums_b, ROUNDS, after(got_b, last_a))
+    last_a = finish(sums_a, after(got_a, out_b[0]))
+    last_b = finish(sums_b, after(got_b, last_a))
     terms = swap(jnp.concatenate([last_a, last_b], axis=2), "zh")
     activated, grad = node_step(terms, weight, cotangent)
     grad = jnp.sum(swap(grad, NEAR), axis=0)

time: 159 us -> 164 us (1.031)
  starting transfers between devices: 47.1 us -> 50.5 us
  waiting for transfers between devices: 9.55 us -> 11.4 us
  Pallas kernels: 7.49 us -> 5.74 us
    ppermute x14, starting transfers between devices: 41.4 us -> 44.9 us  [trade(): lax.ppermute(v, axis, [(k, (k + 1 - 2 * ((k + way) % 2)) % n) for k in ra...]
    ppermute x14, waiting for transfers between devices: 9.55 us -> 11.4 us  [trade(): lax.ppermute(v, axis, [(k, (k + 1 - 2 * ((k + way) % 2)) % n) for k in ra...]
    pallas_call x2 -> x3, Pallas kernels: 5.9 us -> 4.15 us  [sums_of(): pl.pallas_call(functools.partial(add_products, step) if step else first_k...]
  transfers between devices with their start and end apart: 15 -> 15, of which waited for: 5 -> 4; matrix products, arithmetic and copies ran while one was open for 0% -> 1% of each run, Pallas kernels for 2% -> 2%
where the time goes in v5:
time: 164 us; the launch traced here: 163 us
  blocking collectives  88.5 us (54%)
  starting transfers between devices  50.5 us (31%)
  waiting for transfers between devices  11.4 us (7%)
  Pallas kernels  5.74 us (4%)
  local copies, waits for them, and re-layouts  4 us (2%)
  between operations  1.65 us (1%)
    all_to_all x5, blocking collectives, swap(): return lax.all_to_all(v, axes, split_axis=0, concat_axis=0, tiled=True)  88.5 us
    ppermute x14, starting transfers between devices, trade(): lax.ppermute(v, axis, [(k, (k + 1 - 2 * ((k + way) % 2)) % n) for k in ra...  44.9 us
    ppermute x14, waiting for transfers between devices, trade(): lax.ppermute(v, axis, [(k, (k + 1 - 2 * ((k + way) % 2)) % n) for k in ra...  11.4 us
    ppermute x1, starting transfers between devices, body(): other = lax.ppermute(own, 'c', [(0, 1), (1, 0)])  5.67 us
    pallas_call x3, Pallas kernels, sums_of(): pl.pallas_call(functools.partial(add_products, step) if step else first_k...  4.15 us
  transfers between devices with their start and end apart: 15, of which 4 were waited for; matrix products, arithmetic and copies ran while one was open for 1% of the time, Pallas kernels for 2%

profile of v5, /device:TPU:1, one launch (start us, length us, event | category | flops | bytes accessed | tf_op | source)
XLA Modules:
  0.0 162.8 jit_solution(14507103922151568026)
XLA Ops:
  0.6 1.0 broadcast_in_dim.30
  1.6 19.3 %all_to_all.25.own_ref = f32[8,128,256]{2,1,0:T(8,128)S(1)} all-to-all(f32[8,128,256]{2,1,0:T(8,128)S(1)} %broadcast_in_dim.30), channel_id=1, replica_groups=mesh['x'=4,'zl'=2,'c'=2,'yh'=4,'yl'=2,'zh'=4] {'x','zl'}, dimensions={0} | all-to-all | bytes 2097152 | tf_op jit(solution)/shard_map/all_to_all | solution.py:63
  21.0 5.7 %collective-permute-start = (f32[8,128,256]{2,1,0:T(8,128)S(1)}, f32[8,128,256]{2,1,0:T(8,128)S(1)}, u32[]{:S(2)}, u32[]{:S(2)}) collective-permute-start(f32[8,128,256]{2,1,0:T(8,128)S(1)} %all_to_all.25.own_ref), channel_id=1, source_target_pairs={{0,32},{32,0},{1,33},{33,1},{2,34},{34,2},{3,35},{35,3},{4,36},{36... | collective-permute-start | bytes 3145736 | tf_op jit(solution)/shard_map/ppermute | solution.py:208
  27.3 2.2 %copy-done = f32[64,128,128]{2,1,0:T(8,128)S(1)} copy-done((f32[64,128,128]{2,1,0:T(8,128)S(1)}, f32[64,128,128]{2,1,0:T(8,128)}, u32[]{:S(2)}) %copy-start) | copy-done | bytes 4194328
  29.5 0.6 shard_map.86.left_ref
  30.6 1.2 shard_map.87
  31.8 4.9 %collective-permute-start.1 = (f32[4,128,128]{2,1,0:T(8,128)S(1)}, f32[4,128,128]{2,1,0:T(8,128)S(1)}, u32[]{:S(2)}, u32[]{:S(2)}) collective-permute-start(f32[4,128,128]{2,1,0:T(8,128)S(1)} %slice.54), channel_id=1, source_target_pairs={{0,28},{4,8},{8,4},{12,16},{16,12},{20,24},{24,20},{28,0},{1,29},{... | collective-permute-start | bytes 786440 | tf_op jit(solution)/shard_map/ppermute | solution.py:53
  36.8 1.9 %collective-permute-start.7 = (f32[4,128,128]{2,1,0:T(8,128)S(1)}, f32[4,128,128]{2,1,0:T(8,128)S(1)}, u32[]{:S(2)}, u32[]{:S(2)}) collective-permute-start(f32[4,128,128]{2,1,0:T(8,128)S(1)} %slice.48), channel_id=1, source_target_pairs={{0,4},{4,0},{8,12},{12,8},{16,20},{20,16},{24,28},{28,24},{1,5},{5... | collective-permute-start | bytes 786440 | tf_op jit(solution)/shard_map/ppermute | solution.py:53
  38.7 1.3 shard_map.88
  40.0 3.4 %collective-permute-done.1 = f32[4,128,128]{2,1,0:T(8,128)S(1)} collective-permute-done((f32[4,128,128]{2,1,0:T(8,128)S(1)}, f32[4,128,128]{2,1,0:T(8,128)S(1)}, u32[]{:S(2)}, u32[]{:S(2)}) %collective-permute-start.1) | collective-permute-done | bytes 262176 | tf_op jit(solution)/shard_map/ppermute | solution.py:53
  43.4 4.4 %collective-permute-start.3 = (f32[4,128,128]{2,1,0:T(8,128)S(1)}, f32[4,128,128]{2,1,0:T(8,128)S(1)}, u32[]{:S(2)}, u32[]{:S(2)}) collective-permute-start(f32[4,128,128]{2,1,0:T(8,128)S(1)} %get-tuple-element.64), channel_id=1, source_target_pairs={{0,28},{4,8},{8,4},{12,16},{16,12},{20,24},{24,20},{28,0},{1,29},{... | collective-permute-start | bytes 786440 | tf_op jit(solution)/shard_map/ppermute | solution.py:53
  47.8 1.9 %collective-permute-start.2 = (f32[4,128,128]{2,1,0:T(8,128)S(1)}, f32[4,128,128]{2,1,0:T(8,128)S(1)}, u32[]{:S(2)}, u32[]{:S(2)}) collective-permute-start(f32[4,128,128]{2,1,0:T(8,128)S(1)} %get-tuple-element.65), channel_id=1, source_target_pairs={{0,4},{4,0},{8,12},{12,8},{16,20},{20,16},{24,28},{28,24},{1,5},{5... | collective-permute-start | bytes 786440 | tf_op jit(solution)/shard_map/ppermute | solution.py:53
  49.8 4.0 %collective-permute-start.8 = (f32[4,128,128]{2,1,0:T(8,128)S(1)}, f32[4,128,128]{2,1,0:T(8,128)S(1)}, u32[]{:S(2)}, u32[]{:S(2)}) collective-permute-start(f32[4,128,128]{2,1,0:T(8,128)S(1)} %get-tuple-element.66), channel_id=1, source_target_pairs={{0,28},{4,8},{8,4},{12,16},{16,12},{20,24},{24,20},{28,0},{1,29},{... | collective-permute-start | bytes 786440 | tf_op jit(solution)/shard_map/ppermute | solution.py:53
  53.8 3.7 %collective-permute-start.6 = (f32[4,128,128]{2,1,0:T(8,128)S(1)}, f32[4,128,128]{2,1,0:T(8,128)S(1)}, u32[]{:S(2)}, u32[]{:S(2)}) collective-permute-start(f32[4,128,128]{2,1,0:T(8,128)S(1)} %get-tuple-element.67), channel_id=1, source_target_pairs={{0,4},{4,0},{8,12},{12,8},{16,20},{20,16},{24,28},{28,24},{1,5},{5... | collective-permute-start | bytes 786440 | tf_op jit(solution)/shard_map/ppermute | solution.py:53
  57.5 1.7 %shard_map.89 = (f32[21,128,128]{2,1,0:T(8,128)S(1)}, f32[21,128,128]{2,1,0:T(8,128)S(1)}) custom-call(s32[8]{0:T(128)S(1)} %convert_reduce_fusion.1.starts_ref, s32[64]{0:T(128)S(1)} %select_reduce_fusion.order_ref, bf16[64,128,256]{2,1,0:T(8,128)(2,1)S(1)} %shard_map.86.left_ref, bf16[16,128,256]{2,1,0:T(8,128)(2,1)S(1)} %get-tuple-element.30.high, ...), custom_call_target="tpu_custom_call" | custom-call | flops 1000000 | bytes 16384 | tf_op jit(solution)/shard_map/pallas_call | solution.py:151
  59.3 1.9 %collective-permute-start.5 = (f32[4,128,128]{2,1,0:T(8,128)S(1)}, f32[4,128,128]{2,1,0:T(8,128)S(1)}, u32[]{:S(2)}, u32[]{:S(2)}) collective-permute-start(f32[4,128,128]{2,1,0:T(8,128)S(1)} %get-tuple-element.60), channel_id=1, source_target_pairs={{0,28},{4,8},{8,4},{12,16},{16,12},{20,24},{24,20},{28,0},{1,29},{... | collective-permute-start | bytes 786440 | tf_op jit(solution)/shard_map/ppermute | solution.py:53
  61.3 3.6 %collective-permute-start.4 = (f32[4,128,128]{2,1,0:T(8,128)S(1)}, f32[4,128,128]{2,1,0:T(8,128)S(1)}, u32[]{:S(2)}, u32[]{:S(2)}) collective-permute-start(f32[4,128,128]{2,1,0:T(8,128)S(1)} %get-tuple-element.61), channel_id=1, source_target_pairs={{0,4},{4,0},{8,12},{12,8},{16,20},{20,16},{24,28},{28,24},{1,5},{5... | collective-permute-start | bytes 786440 | tf_op jit(solution)/shard_map/ppermute | solution.py:53
  65.0 4.8 %collective-permute-start.12 = (f32[4,128,128]{2,1,0:T(8,128)S(1)}, f32[4,128,128]{2,1,0:T(8,128)S(1)}, u32[]{:S(2)}, u32[]{:S(2)}) collective-permute-start(f32[4,128,128]{2,1,0:T(8,128)S(1)} %get-tuple-element.62), channel_id=1, source_target_pairs={{0,28},{4,8},{8,4},{12,16},{16,12},{20,24},{24,20},{28,0},{1,29},{... | collective-permute-start | bytes 786440 | tf_op jit(solution)/shard_map/ppermute | solution.py:53
  69.8 1.9 %collective-permute-start.11 = (f32[4,128,128]{2,1,0:T(8,128)S(1)}, f32[4,128,128]{2,1,0:T(8,128)S(1)}, u32[]{:S(2)}, u32[]{:S(2)}) collective-permute-start(f32[4,128,128]{2,1,0:T(8,128)S(1)} %get-tuple-element.63), channel_id=1, source_target_pairs={{0,4},{4,0},{8,12},{12,8},{16,20},{20,16},{24,28},{28,24},{1,5},{5... | collective-permute-start | bytes 786440 | tf_op jit(solution)/shard_map/ppermute | solution.py:53
  71.9 3.4 %collective-permute-start.9 = (f32[4,128,128]{2,1,0:T(8,128)S(1)}, f32[4,128,128]{2,1,0:T(8,128)S(1)}, u32[]{:S(2)}, u32[]{:S(2)}) collective-permute-start(f32[4,128,128]{2,1,0:T(8,128)S(1)} %get-tuple-element.57), channel_id=1, source_target_pairs={{0,4},{4,0},{8,12},{12,8},{16,20},{20,16},{24,28},{28,24},{1,5},{5... | collective-permute-start | bytes 786440 | tf_op jit(solution)/shard_map/ppermute | solution.py:53
  75.2 2.5 %collective-permute-done.11 = f32[4,128,128]{2,1,0:T(8,128)S(1)} collective-permute-done((f32[4,128,128]{2,1,0:T(8,128)S(1)}, f32[4,128,128]{2,1,0:T(8,128)S(1)}, u32[]{:S(2)}, u32[]{:S(2)}) %collective-permute-start.11) | collective-permute-done | bytes 262176 | tf_op jit(solution)/shard_map/ppermute | solution.py:53
  77.8 2.6 %collective-permute-start.10 = (f32[4,128,128]{2,1,0:T(8,128)S(1)}, f32[4,128,128]{2,1,0:T(8,128)S(1)}, u32[]{:S(2)}, u32[]{:S(2)}) collective-permute-start(f32[4,128,128]{2,1,0:T(8,128)S(1)} %get-tuple-element.56), channel_id=1, source_target_pairs={{0,28},{4,8},{8,4},{12,16},{16,12},{20,24},{24,20},{28,0},{1,29},{... | collective-permute-start | bytes 786440 | tf_op jit(solution)/shard_map/ppermute | solution.py:53
  80.5 3.8 %collective-permute-start.14 = (f32[4,128,128]{2,1,0:T(8,128)S(1)}, f32[4,128,128]{2,1,0:T(8,128)S(1)}, u32[]{:S(2)}, u32[]{:S(2)}) collective-permute-start(f32[4,128,128]{2,1,0:T(8,128)S(1)} %get-tuple-element.58), channel_id=1, source_target_pairs={{0,28},{4,8},{8,4},{12,16},{16,12},{20,24},{24,20},{28,0},{1,29},{... | collective-permute-start | bytes 786440 | tf_op jit(solution)/shard_map/ppermute | solution.py:53
  84.3 1.9 %collective-permute-start.13 = (f32[4,128,128]{2,1,0:T(8,128)S(1)}, f32[4,128,128]{2,1,0:T(8,128)S(1)}, u32[]{:S(2)}, u32[]{:S(2)}) collective-permute-start(f32[4,128,128]{2,1,0:T(8,128)S(1)} %get-tuple-element.59), channel_id=1, source_target_pairs={{0,4},{4,0},{8,12},{12,8},{16,20},{20,16},{24,28},{28,24},{1,5},{5... | collective-permute-start | bytes 786440 | tf_op jit(solution)/shard_map/ppermute | solution.py:53
  86.4 3.7 %collective-permute-done.14 = f32[4,128,128]{2,1,0:T(8,128)S(1)} collective-permute-done((f32[4,128,128]{2,1,0:T(8,128)S(1)}, f32[4,128,128]{2,1,0:T(8,128)S(1)}, u32[]{:S(2)}, u32[]{:S(2)}) %collective-permute-start.14) | collective-permute-done | bytes 262176 | tf_op jit(solution)/shard_map/ppermute | solution.py:53
  90.1 1.7 %collective-permute-done.13 = f32[4,128,128]{2,1,0:T(8,128)S(1)} collective-permute-done((f32[4,128,128]{2,1,0:T(8,128)S(1)}, f32[4,128,128]{2,1,0:T(8,128)S(1)}, u32[]{:S(2)}, u32[]{:S(2)}) %collective-permute-start.13) | collective-permute-done | bytes 262176 | tf_op jit(solution)/shard_map/ppermute | solution.py:53
  91.9 20.5 %all_to_all.26.terms_ref = f32[4,128,256]{2,1,0:T(8,128)S(1)} all-to-all(f32[4,128,256]{2,1,0:T(8,128)S(1)} %pad_maximum_fusion), channel_id=1, replica_groups=mesh['x'=4,'zl'=2,'c'=2,'yh'=4,'yl'=2,'zh'=4] {'zh'}, dimensions={0} | all-to-all | bytes 1048576 | tf_op jit(solution)/shard_map/all_to_all | solution.py:63
  112.4 1.0 shard_map.90
  113.4 19.2 %all_to_all.27 = f32[32,2,8,128]{3,2,1,0:T(8,128)S(1)} all-to-all(f32[32,2,8,128]{3,2,1,0:T(8,128)S(1)} %get-tuple-element.53), channel_id=1, replica_groups=mesh['x'=4,'zl'=2,'c'=2,'yh'=4,'yl'=2,'zh'=4] {'x','zl','c','yl'}, dimensions={0} | all-to-all | bytes 524288 | tf_op jit(solution)/shard_map/all_to_all | solution.py:63
  132.6 16.3 %all_to_all.28 = f32[16,2,8,128]{3,2,1,0:T(8,128)S(1)} all-to-all(f32[16,2,8,128]{3,2,1,0:T(8,128)S(1)} %broadcast_in_dim.31), channel_id=1, replica_groups=mesh['x'=4,'zl'=2,'c'=2,'yh'=4,'yl'=2,'zh'=4] {'yh','zh'}, dimensions={0} | all-to-all | bytes 262144 | tf_op jit(solution)/shard_map/all_to_all | solution.py:63
  149.0 13.1 %all_to_all.29 = f32[32,2,8,128]{3,2,1,0:T(8,128)S(1)} all-to-all(f32[32,2,8,128]{3,2,1,0:T(8,128)S(1)} %broadcast_in_dim.32), channel_id=1, replica_groups=mesh['x'=4,'zl'=2,'c'=2,'yh'=4,'yl'=2,'zh'=4] {'x','zl','c','yl'}, dimensions={0} | all-to-all | bytes 524288 | tf_op jit(solution)/shard_map/all_to_all | solution.py:63
  162.1 0.7 copy.11
  (40 shorter events, 1.2 us)
Async XLA Ops:
  21.0 9.7 %collective-permute-start = (f32[8,128,256]{2,1,0:T(8,128)S(1)}, f32[8,128,256]{2,1,0:T(8,128)S(1)}, u32[]{:S(2)}, u32[]{:S(2)}) collective-permute-start(f32[8,128,256]{2,1,0:T(8,128)S(1)} %all_to_all.25.own_ref), channel_id=1, source_target_pairs={{0,32},{32,0},{1,33},{33,1},{2,34},{34,2},{3,35},{35,3},{4,36},{36... | collective-permute-start | bytes 3145736 | tf_op jit(solution)/shard_map/ppermute | solution.py:208
  27.3 2.2 %copy-start = (f32[64,128,128]{2,1,0:T(8,128)S(1)}, f32[64,128,128]{2,1,0:T(8,128)}, u32[]{:S(2)}) copy-start(f32[64,128,128]{2,1,0:T(8,128)} %tiles_ref.1) | copy-start | bytes 12582916
  29.5 0.7 copy-start.3
  29.5 0.7 copy-start.4
  31.8 11.6 %collective-permute-start.1 = (f32[4,128,128]{2,1,0:T(8,128)S(1)}, f32[4,128,128]{2,1,0:T(8,128)S(1)}, u32[]{:S(2)}, u32[]{:S(2)}) collective-permute-start(f32[4,128,128]{2,1,0:T(8,128)S(1)} %slice.54), channel_id=1, source_target_pairs={{0,28},{4,8},{8,4},{12,16},{16,12},{20,24},{24,20},{28,0},{1,29},{... | collective-permute-start | bytes 786440 | tf_op jit(solution)/shard_map/ppermute | solution.py:53
  36.8 13.0 %collective-permute-start.7 = (f32[4,128,128]{2,1,0:T(8,128)S(1)}, f32[4,128,128]{2,1,0:T(8,128)S(1)}, u32[]{:S(2)}, u32[]{:S(2)}) collective-permute-start(f32[4,128,128]{2,1,0:T(8,128)S(1)} %slice.48), channel_id=1, source_target_pairs={{0,4},{4,0},{8,12},{12,8},{16,20},{20,16},{24,28},{28,24},{1,5},{5... | collective-permute-start | bytes 786440 | tf_op jit(solution)/shard_map/ppermute | solution.py:53
  43.4 15.8 %collective-permute-start.3 = (f32[4,128,128]{2,1,0:T(8,128)S(1)}, f32[4,128,128]{2,1,0:T(8,128)S(1)}, u32[]{:S(2)}, u32[]{:S(2)}) collective-permute-start(f32[4,128,128]{2,1,0:T(8,128)S(1)} %get-tuple-element.64), channel_id=1, source_target_pairs={{0,28},{4,8},{8,4},{12,16},{16,12},{20,24},{24,20},{28,0},{1,29},{... | collective-permute-start | bytes 786440 | tf_op jit(solution)/shard_map/ppermute | solution.py:53
  47.8 11.4 %collective-permute-start.2 = (f32[4,128,128]{2,1,0:T(8,128)S(1)}, f32[4,128,128]{2,1,0:T(8,128)S(1)}, u32[]{:S(2)}, u32[]{:S(2)}) collective-permute-start(f32[4,128,128]{2,1,0:T(8,128)S(1)} %get-tuple-element.65), channel_id=1, source_target_pairs={{0,4},{4,0},{8,12},{12,8},{16,20},{20,16},{24,28},{28,24},{1,5},{5... | collective-permute-start | bytes 786440 | tf_op jit(solution)/shard_map/ppermute | solution.py:53
  49.8 15.1 %collective-permute-start.8 = (f32[4,128,128]{2,1,0:T(8,128)S(1)}, f32[4,128,128]{2,1,0:T(8,128)S(1)}, u32[]{:S(2)}, u32[]{:S(2)}) collective-permute-start(f32[4,128,128]{2,1,0:T(8,128)S(1)} %get-tuple-element.66), channel_id=1, source_target_pairs={{0,28},{4,8},{8,4},{12,16},{16,12},{20,24},{24,20},{28,0},{1,29},{... | collective-permute-start | bytes 786440 | tf_op jit(solution)/shard_map/ppermute | solution.py:53
  53.8 11.1 %collective-permute-start.6 = (f32[4,128,128]{2,1,0:T(8,128)S(1)}, f32[4,128,128]{2,1,0:T(8,128)S(1)}, u32[]{:S(2)}, u32[]{:S(2)}) collective-permute-start(f32[4,128,128]{2,1,0:T(8,128)S(1)} %get-tuple-element.67), channel_id=1, source_target_pairs={{0,4},{4,0},{8,12},{12,8},{16,20},{20,16},{24,28},{28,24},{1,5},{5... | collective-permute-start | bytes 786440 | tf_op jit(solution)/shard_map/ppermute | solution.py:53
  59.3 12.4 %collective-permute-start.5 = (f32[4,128,128]{2,1,0:T(8,128)S(1)}, f32[4,128,128]{2,1,0:T(8,128)S(1)}, u32[]{:S(2)}, u32[]{:S(2)}) collective-permute-start(f32[4,128,128]{2,1,0:T(8,128)S(1)} %get-tuple-element.60), channel_id=1, source_target_pairs={{0,28},{4,8},{8,4},{12,16},{16,12},{20,24},{24,20},{28,0},{1,29},{... | collective-permute-start | bytes 786440 | tf_op jit(solution)/shard_map/ppermute | solution.py:53
  61.3 10.5 %collective-permute-start.4 = (f32[4,128,128]{2,1,0:T(8,128)S(1)}, f32[4,128,128]{2,1,0:T(8,128)S(1)}, u32[]{:S(2)}, u32[]{:S(2)}) collective-permute-start(f32[4,128,128]{2,1,0:T(8,128)S(1)} %get-tuple-element.61), channel_id=1, source_target_pairs={{0,4},{4,0},{8,12},{12,8},{16,20},{20,16},{24,28},{28,24},{1,5},{5... | collective-permute-start | bytes 786440 | tf_op jit(solution)/shard_map/ppermute | solution.py:53
  65.0 10.2 %collective-permute-start.12 = (f32[4,128,128]{2,1,0:T(8,128)S(1)}, f32[4,128,128]{2,1,0:T(8,128)S(1)}, u32[]{:S(2)}, u32[]{:S(2)}) collective-permute-start(f32[4,128,128]{2,1,0:T(8,128)S(1)} %get-tuple-element.62), channel_id=1, source_target_pairs={{0,28},{4,8},{8,4},{12,16},{16,12},{20,24},{24,20},{28,0},{1,29},{... | collective-permute-start | bytes 786440 | tf_op jit(solution)/shard_map/ppermute | solution.py:53
  69.8 7.9 %collective-permute-start.11 = (f32[4,128,128]{2,1,0:T(8,128)S(1)}, f32[4,128,128]{2,1,0:T(8,128)S(1)}, u32[]{:S(2)}, u32[]{:S(2)}) collective-permute-start(f32[4,128,128]{2,1,0:T(8,128)S(1)} %get-tuple-element.63), channel_id=1, source_target_pairs={{0,4},{4,0},{8,12},{12,8},{16,20},{20,16},{24,28},{28,24},{1,5},{5... | collective-permute-start | bytes 786440 | tf_op jit(solution)/shard_map/ppermute | solution.py:53
  71.9 14.4 %collective-permute-start.9 = (f32[4,128,128]{2,1,0:T(8,128)S(1)}, f32[4,128,128]{2,1,0:T(8,128)S(1)}, u32[]{:S(2)}, u32[]{:S(2)}) collective-permute-start(f32[4,128,128]{2,1,0:T(8,128)S(1)} %get-tuple-element.57), channel_id=1, source_target_pairs={{0,4},{4,0},{8,12},{12,8},{16,20},{20,16},{24,28},{28,24},{1,5},{5... | collective-permute-start | bytes 786440 | tf_op jit(solution)/shard_map/ppermute | solution.py:53
  77.8 8.5 %collective-permute-start.10 = (f32[4,128,128]{2,1,0:T(8,128)S(1)}, f32[4,128,128]{2,1,0:T(8,128)S(1)}, u32[]{:S(2)}, u32[]{:S(2)}) collective-permute-start(f32[4,128,128]{2,1,0:T(8,128)S(1)} %get-tuple-element.56), channel_id=1, source_target_pairs={{0,28},{4,8},{8,4},{12,16},{16,12},{20,24},{24,20},{28,0},{1,29},{... | collective-permute-start | bytes 786440 | tf_op jit(solution)/shard_map/ppermute | solution.py:53
  80.5 9.6 %collective-permute-start.14 = (f32[4,128,128]{2,1,0:T(8,128)S(1)}, f32[4,128,128]{2,1,0:T(8,128)S(1)}, u32[]{:S(2)}, u32[]{:S(2)}) collective-permute-start(f32[4,128,128]{2,1,0:T(8,128)S(1)} %get-tuple-element.58), channel_id=1, source_target_pairs={{0,28},{4,8},{8,4},{12,16},{16,12},{20,24},{24,20},{28,0},{1,29},{... | collective-permute-start | bytes 786440 | tf_op jit(solution)/shard_map/ppermute | solution.py:53
  84.3 7.4 %collective-permute-start.13 = (f32[4,128,128]{2,1,0:T(8,128)S(1)}, f32[4,128,128]{2,1,0:T(8,128)S(1)}, u32[]{:S(2)}, u32[]{:S(2)}) collective-permute-start(f32[4,128,128]{2,1,0:T(8,128)S(1)} %get-tuple-element.59), channel_id=1, source_target_pairs={{0,4},{4,0},{8,12},{12,8},{16,20},{20,16},{24,28},{28,24},{1,5},{5... | collective-permute-start | bytes 786440 | tf_op jit(solution)/shard_map/ppermute | solution.py:53
  86.4 26.0 %copy-start.1 = (f32[256,256]{1,0:T(8,128)S(1)}, f32[256,256]{1,0:T(8,128)}, u32[]{:S(2)}) copy-start(f32[256,256]{1,0:T(8,128)} %weight_ref.1) | copy-start | bytes 786436
  86.4 26.0 %copy-start.2 = (f32[128,256]{1,0:T(8,128)S(1)}, f32[128,256]{1,0:T(8,128)}, u32[]{:S(2)}) copy-start(f32[128,256]{1,0:T(8,128)} %cot_ref.1) | copy-start | bytes 393220

commit v6 on v5

--- a/solution.py
+++ b/solution.py
@@ -21,6 +21,11 @@
 NEAR = ("x", "zl", "c", "yl")
 FAR = ("yh", "zh")
 NEAR_SIZE = 32
+PARTS = (10, 11, 8, 2, 1, 0, 9, 12)
+MESSAGES = (
+    (0, 0, 3), (1, 1, 5), (0, 0, 2), (1, 1, 6), (0, 1, 6),
+    (1, 0, 2), (0, 1, 7), (1, 0, 1), (0, 0, 1), (1, 1, 7),
+)
 
 
 def halves(v):
@@ -70,11 +75,9 @@
 def slot_plan(tile_rows, tile_cols, tile_count):
     ids = jnp.arange(tile_rows.shape[0], dtype=jnp.int32)
     far = ahead(tile_rows // NZH, RING)
-    away = jnp.minimum(far, NY - far)
-    key = jnp.where(ids < tile_count[0], jnp.minimum(ROUNDS - away, 2), 3)
-    row = tile_rows % NZH + NZH * (
-        jnp.where(far > ROUNDS, 1, 0) + jnp.where(away == 1, 3, jnp.where(away == 0, 2, 0))
-    )
+    part = sum(jnp.where(far == k, PARTS[k], 0) for k in range(NY))
+    key = jnp.where(ids < tile_count[0], part // 8, 2)
+    row = tile_rows % NZH + part % 8 * NZH
     core = lax.rem(tile_cols % NC + lax.axis_index("c"), NC)
     packed = (ids * 32 + row) * 16 + core * (NX * NZL) + tile_cols // NC
     before = (key[None, :] < key[:, None]) | (
@@ -142,7 +145,7 @@
 
 def sums_of(step, starts, ordered, left, sources):
     tile = left.shape[1]
-    rows = NZH * (1, 2, 5)[step] + 1
+    rows = NZH * (3, 5)[step] + 1
     shapes = [jax.ShapeDtypeStruct((rows, tile, LANES), jnp.float32)] * 2
     if step == 0:
         shapes += [jax.ShapeDtypeStruct((2 * sources[0].shape[0], tile, 2 * LANES), jnp.bfloat16)] * 2
@@ -184,22 +187,8 @@
     )(terms, weight, cotangent)
 
 
-def after(values, witness):
-    here = lax.optimization_barrier((*(v for v in values if v is not None), witness))
-    return [None if v is None else here[sum(u is not None for u in values[:k])] for k, v in enumerate(values)]
-
-
-def advance(sums, first, got):
-    pair = [sums[first : first + NZH], sums[first + NZH : first + 2 * NZH]]
-    return [v if g is None else v + g for v, g in zip(pair, got[::-1])]
-
-
-def finish(sums, got):
-    return sums[2 * NZH : 3 * NZH] + (got[0] + got[1])
-
-
-def send(pair):
-    return trade(pair[0], RING, 0), trade(pair[1], RING, 1)
+def after(value, witness):
+    return lax.optimization_barrier((value, witness))[0]
 
 
 def body(features, adjacency_tiles, tile_rows, tile_cols, tile_count, weight, cotangent):
@@ -207,21 +196,24 @@
     own = share(features, ("x", "zl"))
     other = lax.ppermute(own, "c", [(0, 1), (1, 0)])
     left = split_tiles(adjacency_tiles)
-    far_a, far_b, high, low = sums_of(0, starts, ordered, left, (own, other))
-    far_a, far_b = far_a[:NZH], far_b[:NZH]
-    got_a = (None, trade(far_a, RING, 1))
-    got_b = (trade(far_b, RING, 0), None)
-    out_b = [far_b]
-    for step in range(1, ROUNDS):
-        if step < 3:
-            sums_a, sums_b = sums_of(step, after((starts,), out_b[0])[0], ordered, left, (high, low))
-        first = 0 if step < 3 else 3 * NZH
-        out_a = advance(sums_a, first, after(got_a, out_b[0]))
-        got_a = send(out_a)
-        out_b = advance(sums_b, first, after(got_b, out_a[0]))
-        got_b = send(out_b)
-    last_a = finish(sums_a, after(got_a, out_b[0]))
-    last_b = finish(sums_b, after(got_b, last_a))
+    *early, high, low = sums_of(0, starts, ordered, left, (own, other))
+    late = sums_of(1, after(starts, early[0]), ordered, left, (high, low))
+
+    def chunk(lane, far):
+        first = PARTS[far] % 8 * NZH
+        return (early, late)[PARTS[far] // 8][lane][first : first + NZH]
+
+    first_a = trade(early[0][: 2 * NZH], RING, 1)
+    first_b = trade(early[1][NZH : 3 * NZH], RING, 0)
+    came = [first_a[NZH:], first_b[:NZH], first_a[:NZH], first_b[NZH:]]
+    made = late[0]
+    for k, (lane, way, far) in enumerate(MESSAGES):
+        made = chunk(lane, far) + after(came[k], made)
+        came.append(trade(made, RING, way))
+    part_a = chunk(0, 0) + after(came[10], made)
+    part_b = chunk(1, 0) + after(came[11], part_a)
+    last_a = part_a + after(came[12], part_b)
+    last_b = part_b + after(came[13], last_a)
     terms = swap(jnp.concatenate([last_a, last_b], axis=2), "zh")
     activated, grad = node_step(terms, weight, cotangent)
     grad = jnp.sum(swap(grad, NEAR), axis=0)

time: 164 us -> 157 us (0.957)
  starting transfers between devices: 50.5 us -> 40.8 us
  waiting for transfers between devices: 11.4 us -> 14.4 us
    ppermute x14 -> x12, starting transfers between devices: 44.9 us -> 35.1 us  [trade(): lax.ppermute(v, axis, [(k, (k + 1 - 2 * ((k + way) % 2)) % n) for k in ra...]
    ppermute x14 -> x12, waiting for transfers between devices: 11.4 us -> 14.4 us  [trade(): lax.ppermute(v, axis, [(k, (k + 1 - 2 * ((k + way) % 2)) % n) for k in ra...]
    pallas_call x3 -> x2, Pallas kernels: 4.15 us -> 4.58 us  [sums_of(): pl.pallas_call(functools.partial(add_products, step) if step else first_k...]
  transfers between devices with their start and end apart: 15 -> 13, of which waited for: 4 -> 5; matrix products, arithmetic and copies ran while one was open for 1% -> 1% of each run, Pallas kernels for 2% -> 2%
where the time goes in v6:
time: 157 us; the launch traced here: 156 us
  blocking collectives  87.7 us (56%)
  starting transfers between devices  40.8 us (26%)
  waiting for transfers between devices  14.4 us (9%)
  Pallas kernels  6.17 us (4%)
  local copies, waits for them, and re-layouts  4.11 us (3%)
  between operations  1.6 us (1%)
    all_to_all x5, blocking collectives, swap(): return lax.all_to_all(v, axes, split_axis=0, concat_axis=0, tiled=True)  87.7 us
    ppermute x12, starting transfers between devices, trade(): lax.ppermute(v, axis, [(k, (k + 1 - 2 * ((k + way) % 2)) % n) for k in ra...  35.1 us
    ppermute x12, waiting for transfers between devices, trade(): lax.ppermute(v, axis, [(k, (k + 1 - 2 * ((k + way) % 2)) % n) for k in ra...  14.4 us
    ppermute x1, starting transfers between devices, body(): other = lax.ppermute(own, 'c', [(0, 1), (1, 0)])  5.67 us
    pallas_call x2, Pallas kernels, sums_of(): pl.pallas_call(functools.partial(add_products, step) if step else first_k...  4.58 us
  transfers between devices with their start and end apart: 13, of which 5 were waited for; matrix products, arithmetic and copies ran while one was open for 1% of the time, Pallas kernels for 2%

profile of v6, /device:TPU:1, one launch (start us, length us, event | category | flops | bytes accessed | tf_op | source)
XLA Modules:
  0.0 155.9 jit_solution(578212232497076903)
XLA Ops:
  0.6 1.0 broadcast_in_dim.75
  1.6 19.3 %all_to_all.25.own_ref = f32[8,128,256]{2,1,0:T(8,128)S(1)} all-to-all(f32[8,128,256]{2,1,0:T(8,128)S(1)} %broadcast_in_dim.75), channel_id=1, replica_groups=mesh['x'=4,'zl'=2,'c'=2,'yh'=4,'yl'=2,'zh'=4] {'x','zl'}, dimensions={0} | all-to-all | bytes 2097152 | tf_op jit(solution)/shard_map/all_to_all | solution.py:68
  21.0 5.7 %collective-permute-start = (f32[8,128,256]{2,1,0:T(8,128)S(1)}, f32[8,128,256]{2,1,0:T(8,128)S(1)}, u32[]{:S(2)}, u32[]{:S(2)}) collective-permute-start(f32[8,128,256]{2,1,0:T(8,128)S(1)} %all_to_all.25.own_ref), channel_id=1, source_target_pairs={{0,32},{32,0},{1,33},{33,1},{2,34},{34,2},{3,35},{35,3},{4,36},{36... | collective-permute-start | bytes 3145736 | tf_op jit(solution)/shard_map/ppermute | solution.py:197
  27.3 2.2 %copy-done = f32[64,128,128]{2,1,0:T(8,128)S(1)} copy-done((f32[64,128,128]{2,1,0:T(8,128)S(1)}, f32[64,128,128]{2,1,0:T(8,128)}, u32[]{:S(2)}) %copy-start) | copy-done | bytes 4194328
  29.5 0.6 shard_map.86.left_ref
  30.2 0.1 convert_reduce_fusion.1.starts_ref
  30.3 0.2 convert_reduce_fusion
  30.5 0.1 select_reduce_fusion.order_ref
  30.6 2.2 %shard_map.87 = (f32[13,128,128]{2,1,0:T(8,128)S(1)}, f32[13,128,128]{2,1,0:T(8,128)S(1)}, bf16[16,128,256]{2,1,0:T(8,128)(2,1)S(1)}, bf16[16,128,256]{2,1,0:T(8,128)(2,1)S(1)}) custom-call(s32[8]{0:T(128)S(1)} %convert_reduce_fusion.1.starts_ref, s32[64]{0:T(128)S(1)} %select_reduce_fusion.order_ref, bf16[64,128,256]{2,1,0:T(8,128)(2,1)S(1)} %shard_map.86.left_ref, ...), custom_call_target="tpu_custom_call" | custom-call | flops 1000000 | bytes 16384 | tf_op jit(solution)/shard_map/pallas_call | solution.py:154
  32.9 4.2 %collective-permute-start.1 = (f32[8,128,128]{2,1,0:T(8,128)S(1)}, f32[8,128,128]{2,1,0:T(8,128)S(1)}, u32[]{:S(2)}, u32[]{:S(2)}) collective-permute-start(f32[8,128,128]{2,1,0:T(8,128)S(1)} %slice.57), channel_id=1, source_target_pairs={{0,28},{4,8},{8,4},{12,16},{16,12},{20,24},{24,20},{28,0},{1,29},{... | collective-permute-start | bytes 1572872 | tf_op jit(solution)/shard_map/ppermute | solution.py:58
  37.2 2.3 %collective-permute-start.2 = (f32[8,128,128]{2,1,0:T(8,128)S(1)}, f32[8,128,128]{2,1,0:T(8,128)S(1)}, u32[]{:S(2)}, u32[]{:S(2)}) collective-permute-start(f32[8,128,128]{2,1,0:T(8,128)S(1)} %slice.60), channel_id=1, source_target_pairs={{0,4},{4,0},{8,12},{12,8},{16,20},{20,16},{24,28},{28,24},{1,5},{5... | collective-permute-start | bytes 1572872 | tf_op jit(solution)/shard_map/ppermute | solution.py:58
  39.5 2.4 %shard_map.88 = (f32[21,128,128]{2,1,0:T(8,128)S(1)}, f32[21,128,128]{2,1,0:T(8,128)S(1)}) custom-call(s32[8]{0:T(128)S(1)} %convert_reduce_fusion.1.starts_ref, s32[64]{0:T(128)S(1)} %select_reduce_fusion.order_ref, bf16[64,128,256]{2,1,0:T(8,128)(2,1)S(1)} %shard_map.86.left_ref, bf16[16,128,256]{2,1,0:T(8,128)(2,1)S(1)} %get-tuple-element.27.high, ...), custom_call_target="tpu_custom_call" | custom-call | flops 1000000 | bytes 16384 | tf_op jit(solution)/shard_map/pallas_call | solution.py:154
  41.9 7.6 %collective-permute-done.1 = f32[8,128,128]{2,1,0:T(8,128)S(1)} collective-permute-done((f32[8,128,128]{2,1,0:T(8,128)S(1)}, f32[8,128,128]{2,1,0:T(8,128)S(1)}, u32[]{:S(2)}, u32[]{:S(2)}) %collective-permute-start.1) | collective-permute-done | bytes 524320 | tf_op jit(solution)/shard_map/ppermute | solution.py:58
  49.6 2.1 %collective-permute-start.5 = (f32[4,128,128]{2,1,0:T(8,128)S(1)}, f32[4,128,128]{2,1,0:T(8,128)S(1)}, u32[]{:S(2)}, u32[]{:S(2)}) collective-permute-start(f32[4,128,128]{2,1,0:T(8,128)S(1)} %slice_add_fusion.7), channel_id=1, source_target_pairs={{0,4},{4,0},{8,12},{12,8},{16,20},{20,16},{24,28},{28,24},{1,5},{5... | collective-permute-start | bytes 786440 | tf_op jit(solution)/shard_map/ppermute | solution.py:58
  51.8 4.8 %collective-permute-start.4 = (f32[4,128,128]{2,1,0:T(8,128)S(1)}, f32[4,128,128]{2,1,0:T(8,128)S(1)}, u32[]{:S(2)}, u32[]{:S(2)}) collective-permute-start(f32[4,128,128]{2,1,0:T(8,128)S(1)} %slice_add_fusion.8), channel_id=1, source_target_pairs={{0,28},{4,8},{8,4},{12,16},{16,12},{20,24},{24,20},{28,0},{1,29},{... | collective-permute-start | bytes 786440 | tf_op jit(solution)/shard_map/ppermute | solution.py:58
  56.6 2.9 %collective-permute-start.3 = (f32[4,128,128]{2,1,0:T(8,128)S(1)}, f32[4,128,128]{2,1,0:T(8,128)S(1)}, u32[]{:S(2)}, u32[]{:S(2)}) collective-permute-start(f32[4,128,128]{2,1,0:T(8,128)S(1)} %slice_add_fusion.9), channel_id=1, source_target_pairs={{0,4},{4,0},{8,12},{12,8},{16,20},{20,16},{24,28},{28,24},{1,5},{5... | collective-permute-start | bytes 786440 | tf_op jit(solution)/shard_map/ppermute | solution.py:58
  59.5 2.8 %collective-permute-start.9 = (f32[4,128,128]{2,1,0:T(8,128)S(1)}, f32[4,128,128]{2,1,0:T(8,128)S(1)}, u32[]{:S(2)}, u32[]{:S(2)}) collective-permute-start(f32[4,128,128]{2,1,0:T(8,128)S(1)} %slice_add_fusion.4), channel_id=1, source_target_pairs={{0,28},{4,8},{8,4},{12,16},{16,12},{20,24},{24,20},{28,0},{1,29},{... | collective-permute-start | bytes 786440 | tf_op jit(solution)/shard_map/ppermute | solution.py:58
  62.3 3.7 %collective-permute-start.8 = (f32[4,128,128]{2,1,0:T(8,128)S(1)}, f32[4,128,128]{2,1,0:T(8,128)S(1)}, u32[]{:S(2)}, u32[]{:S(2)}) collective-permute-start(f32[4,128,128]{2,1,0:T(8,128)S(1)} %slice_add_fusion.5), channel_id=1, source_target_pairs={{0,28},{4,8},{8,4},{12,16},{16,12},{20,24},{24,20},{28,0},{1,29},{... | collective-permute-start | bytes 786440 | tf_op jit(solution)/shard_map/ppermute | solution.py:58
  66.1 1.9 %collective-permute-start.7 = (f32[4,128,128]{2,1,0:T(8,128)S(1)}, f32[4,128,128]{2,1,0:T(8,128)S(1)}, u32[]{:S(2)}, u32[]{:S(2)}) collective-permute-start(f32[4,128,128]{2,1,0:T(8,128)S(1)} %slice_add_fusion.6), channel_id=1, source_target_pairs={{0,4},{4,0},{8,12},{12,8},{16,20},{20,16},{24,28},{28,24},{1,5},{5... | collective-permute-start | bytes 786440 | tf_op jit(solution)/shard_map/ppermute | solution.py:58
  68.1 2.8 %collective-permute-start.6 = (f32[4,128,128]{2,1,0:T(8,128)S(1)}, f32[4,128,128]{2,1,0:T(8,128)S(1)}, u32[]{:S(2)}, u32[]{:S(2)}) collective-permute-start(f32[4,128,128]{2,1,0:T(8,128)S(1)} %slice_add_fusion.10), channel_id=1, source_target_pairs={{0,28},{4,8},{8,4},{12,16},{16,12},{20,24},{24,20},{28,0},{1,29},{... | collective-permute-start | bytes 786440 | tf_op jit(solution)/shard_map/ppermute | solution.py:58
  70.9 3.1 %collective-permute-start.11 = (f32[4,128,128]{2,1,0:T(8,128)S(1)}, f32[4,128,128]{2,1,0:T(8,128)S(1)}, u32[]{:S(2)}, u32[]{:S(2)}) collective-permute-start(f32[4,128,128]{2,1,0:T(8,128)S(1)} %slice_add_fusion.1), channel_id=1, source_target_pairs={{0,4},{4,0},{8,12},{12,8},{16,20},{20,16},{24,28},{28,24},{1,5},{5... | collective-permute-start | bytes 786440 | tf_op jit(solution)/shard_map/ppermute | solution.py:58
  74.0 1.3 collective-permute-done.8
  75.4 1.9 %collective-permute-start.10 = (f32[4,128,128]{2,1,0:T(8,128)S(1)}, f32[4,128,128]{2,1,0:T(8,128)S(1)}, u32[]{:S(2)}, u32[]{:S(2)}) collective-permute-start(f32[4,128,128]{2,1,0:T(8,128)S(1)} %slice_add_fusion.2), channel_id=1, source_target_pairs={{0,4},{4,0},{8,12},{12,8},{16,20},{20,16},{24,28},{28,24},{1,5},{5... | collective-permute-start | bytes 786440 | tf_op jit(solution)/shard_map/ppermute | solution.py:58
  77.4 2.7 %collective-permute-start.12 = (f32[4,128,128]{2,1,0:T(8,128)S(1)}, f32[4,128,128]{2,1,0:T(8,128)S(1)}, u32[]{:S(2)}, u32[]{:S(2)}) collective-permute-start(f32[4,128,128]{2,1,0:T(8,128)S(1)} %slice_add_fusion.3), channel_id=1, source_target_pairs={{0,28},{4,8},{8,4},{12,16},{16,12},{20,24},{24,20},{28,0},{1,29},{... | collective-permute-start | bytes 786440 | tf_op jit(solution)/shard_map/ppermute | solution.py:58
  80.1 0.9 collective-permute-done.6
  81.1 4.5 %collective-permute-done.10 = f32[4,128,128]{2,1,0:T(8,128)S(1)} collective-permute-done((f32[4,128,128]{2,1,0:T(8,128)S(1)}, f32[4,128,128]{2,1,0:T(8,128)S(1)}, u32[]{:S(2)}, u32[]{:S(2)}) %collective-permute-start.10) | collective-permute-done | bytes 262176 | tf_op jit(solution)/shard_map/ppermute | solution.py:58
  85.8 20.5 %all_to_all.26.terms_ref = f32[4,128,256]{2,1,0:T(8,128)S(1)} all-to-all(f32[4,128,256]{2,1,0:T(8,128)S(1)} %pad_maximum_fusion), channel_id=1, replica_groups=mesh['x'=4,'zl'=2,'c'=2,'yh'=4,'yl'=2,'zh'=4] {'zh'}, dimensions={0} | all-to-all | bytes 1048576 | tf_op jit(solution)/shard_map/all_to_all | solution.py:68
  106.2 1.0 shard_map.89
  107.2 18.2 %all_to_all.27 = f32[32,2,8,128]{3,2,1,0:T(8,128)S(1)} all-to-all(f32[32,2,8,128]{3,2,1,0:T(8,128)S(1)} %get-tuple-element.47), channel_id=1, replica_groups=mesh['x'=4,'zl'=2,'c'=2,'yh'=4,'yl'=2,'zh'=4] {'x','zl','c','yl'}, dimensions={0} | all-to-all | bytes 524288 | tf_op jit(solution)/shard_map/all_to_all | solution.py:68
  125.5 16.6 %all_to_all.28 = f32[16,2,8,128]{3,2,1,0:T(8,128)S(1)} all-to-all(f32[16,2,8,128]{3,2,1,0:T(8,128)S(1)} %broadcast_in_dim.76), channel_id=1, replica_groups=mesh['x'=4,'zl'=2,'c'=2,'yh'=4,'yl'=2,'zh'=4] {'yh','zh'}, dimensions={0} | all-to-all | bytes 262144 | tf_op jit(solution)/shard_map/all_to_all | solution.py:68
  142.1 13.1 %all_to_all.29 = f32[32,2,8,128]{3,2,1,0:T(8,128)S(1)} all-to-all(f32[32,2,8,128]{3,2,1,0:T(8,128)S(1)} %broadcast_in_dim.77), channel_id=1, replica_groups=mesh['x'=4,'zl'=2,'c'=2,'yh'=4,'yl'=2,'zh'=4] {'x','zl','c','yl'}, dimensions={0} | all-to-all | bytes 524288 | tf_op jit(solution)/shard_map/all_to_all | solution.py:68
  155.2 0.7 copy.11
  (43 shorter events, 1.0 us)
Async XLA Ops:
  21.0 9.7 %collective-permute-start = (f32[8,128,256]{2,1,0:T(8,128)S(1)}, f32[8,128,256]{2,1,0:T(8,128)S(1)}, u32[]{:S(2)}, u32[]{:S(2)}) collective-permute-start(f32[8,128,256]{2,1,0:T(8,128)S(1)} %all_to_all.25.own_ref), channel_id=1, source_target_pairs={{0,32},{32,0},{1,33},{33,1},{2,34},{34,2},{3,35},{35,3},{4,36},{36... | collective-permute-start | bytes 3145736 | tf_op jit(solution)/shard_map/ppermute | solution.py:197
  27.3 2.2 %copy-start = (f32[64,128,128]{2,1,0:T(8,128)S(1)}, f32[64,128,128]{2,1,0:T(8,128)}, u32[]{:S(2)}) copy-start(f32[64,128,128]{2,1,0:T(8,128)} %tiles_ref.1) | copy-start | bytes 12582916
  29.5 0.7 copy-start.3
  29.5 0.7 copy-start.4
  32.9 16.6 %collective-permute-start.1 = (f32[8,128,128]{2,1,0:T(8,128)S(1)}, f32[8,128,128]{2,1,0:T(8,128)S(1)}, u32[]{:S(2)}, u32[]{:S(2)}) collective-permute-start(f32[8,128,128]{2,1,0:T(8,128)S(1)} %slice.57), channel_id=1, source_target_pairs={{0,28},{4,8},{8,4},{12,16},{16,12},{20,24},{24,20},{28,0},{1,29},{... | collective-permute-start | bytes 1572872 | tf_op jit(solution)/shard_map/ppermute | solution.py:58
  37.2 14.5 %collective-permute-start.2 = (f32[8,128,128]{2,1,0:T(8,128)S(1)}, f32[8,128,128]{2,1,0:T(8,128)S(1)}, u32[]{:S(2)}, u32[]{:S(2)}) collective-permute-start(f32[8,128,128]{2,1,0:T(8,128)S(1)} %slice.60), channel_id=1, source_target_pairs={{0,4},{4,0},{8,12},{12,8},{16,20},{20,16},{24,28},{28,24},{1,5},{5... | collective-permute-start | bytes 1572872 | tf_op jit(solution)/shard_map/ppermute | solution.py:58
  49.6 12.7 %collective-permute-start.5 = (f32[4,128,128]{2,1,0:T(8,128)S(1)}, f32[4,128,128]{2,1,0:T(8,128)S(1)}, u32[]{:S(2)}, u32[]{:S(2)}) collective-permute-start(f32[4,128,128]{2,1,0:T(8,128)S(1)} %slice_add_fusion.7), channel_id=1, source_target_pairs={{0,4},{4,0},{8,12},{12,8},{16,20},{20,16},{24,28},{28,24},{1,5},{5... | collective-permute-start | bytes 786440 | tf_op jit(solution)/shard_map/ppermute | solution.py:58
  51.8 14.3 %collective-permute-start.4 = (f32[4,128,128]{2,1,0:T(8,128)S(1)}, f32[4,128,128]{2,1,0:T(8,128)S(1)}, u32[]{:S(2)}, u32[]{:S(2)}) collective-permute-start(f32[4,128,128]{2,1,0:T(8,128)S(1)} %slice_add_fusion.8), channel_id=1, source_target_pairs={{0,28},{4,8},{8,4},{12,16},{16,12},{20,24},{24,20},{28,0},{1,29},{... | collective-permute-start | bytes 786440 | tf_op jit(solution)/shard_map/ppermute | solution.py:58
  56.6 11.5 %collective-permute-start.3 = (f32[4,128,128]{2,1,0:T(8,128)S(1)}, f32[4,128,128]{2,1,0:T(8,128)S(1)}, u32[]{:S(2)}, u32[]{:S(2)}) collective-permute-start(f32[4,128,128]{2,1,0:T(8,128)S(1)} %slice_add_fusion.9), channel_id=1, source_target_pairs={{0,4},{4,0},{8,12},{12,8},{16,20},{20,16},{24,28},{28,24},{1,5},{5... | collective-permute-start | bytes 786440 | tf_op jit(solution)/shard_map/ppermute | solution.py:58
  59.5 11.4 %collective-permute-start.9 = (f32[4,128,128]{2,1,0:T(8,128)S(1)}, f32[4,128,128]{2,1,0:T(8,128)S(1)}, u32[]{:S(2)}, u32[]{:S(2)}) collective-permute-start(f32[4,128,128]{2,1,0:T(8,128)S(1)} %slice_add_fusion.4), channel_id=1, source_target_pairs={{0,28},{4,8},{8,4},{12,16},{16,12},{20,24},{24,20},{28,0},{1,29},{... | collective-permute-start | bytes 786440 | tf_op jit(solution)/shard_map/ppermute | solution.py:58
  62.3 13.0 %collective-permute-start.8 = (f32[4,128,128]{2,1,0:T(8,128)S(1)}, f32[4,128,128]{2,1,0:T(8,128)S(1)}, u32[]{:S(2)}, u32[]{:S(2)}) collective-permute-start(f32[4,128,128]{2,1,0:T(8,128)S(1)} %slice_add_fusion.5), channel_id=1, source_target_pairs={{0,28},{4,8},{8,4},{12,16},{16,12},{20,24},{24,20},{28,0},{1,29},{... | collective-permute-start | bytes 786440 | tf_op jit(solution)/shard_map/ppermute | solution.py:58
  66.1 11.2 %collective-permute-start.7 = (f32[4,128,128]{2,1,0:T(8,128)S(1)}, f32[4,128,128]{2,1,0:T(8,128)S(1)}, u32[]{:S(2)}, u32[]{:S(2)}) collective-permute-start(f32[4,128,128]{2,1,0:T(8,128)S(1)} %slice_add_fusion.6), channel_id=1, source_target_pairs={{0,4},{4,0},{8,12},{12,8},{16,20},{20,16},{24,28},{28,24},{1,5},{5... | collective-permute-start | bytes 786440 | tf_op jit(solution)/shard_map/ppermute | solution.py:58
  68.1 12.9 %collective-permute-start.6 = (f32[4,128,128]{2,1,0:T(8,128)S(1)}, f32[4,128,128]{2,1,0:T(8,128)S(1)}, u32[]{:S(2)}, u32[]{:S(2)}) collective-permute-start(f32[4,128,128]{2,1,0:T(8,128)S(1)} %slice_add_fusion.10), channel_id=1, source_target_pairs={{0,28},{4,8},{8,4},{12,16},{16,12},{20,24},{24,20},{28,0},{1,29},{... | collective-permute-start | bytes 786440 | tf_op jit(solution)/shard_map/ppermute | solution.py:58
  70.9 10.1 %collective-permute-start.11 = (f32[4,128,128]{2,1,0:T(8,128)S(1)}, f32[4,128,128]{2,1,0:T(8,128)S(1)}, u32[]{:S(2)}, u32[]{:S(2)}) collective-permute-start(f32[4,128,128]{2,1,0:T(8,128)S(1)} %slice_add_fusion.1), channel_id=1, source_target_pairs={{0,4},{4,0},{8,12},{12,8},{16,20},{20,16},{24,28},{28,24},{1,5},{5... | collective-permute-start | bytes 786440 | tf_op jit(solution)/shard_map/ppermute | solution.py:58
  75.4 10.2 %collective-permute-start.10 = (f32[4,128,128]{2,1,0:T(8,128)S(1)}, f32[4,128,128]{2,1,0:T(8,128)S(1)}, u32[]{:S(2)}, u32[]{:S(2)}) collective-permute-start(f32[4,128,128]{2,1,0:T(8,128)S(1)} %slice_add_fusion.2), channel_id=1, source_target_pairs={{0,4},{4,0},{8,12},{12,8},{16,20},{20,16},{24,28},{28,24},{1,5},{5... | collective-permute-start | bytes 786440 | tf_op jit(solution)/shard_map/ppermute | solution.py:58
  77.4 8.3 %collective-permute-start.12 = (f32[4,128,128]{2,1,0:T(8,128)S(1)}, f32[4,128,128]{2,1,0:T(8,128)S(1)}, u32[]{:S(2)}, u32[]{:S(2)}) collective-permute-start(f32[4,128,128]{2,1,0:T(8,128)S(1)} %slice_add_fusion.3), channel_id=1, source_target_pairs={{0,28},{4,8},{8,4},{12,16},{16,12},{20,24},{24,20},{28,0},{1,29},{... | collective-permute-start | bytes 786440 | tf_op jit(solution)/shard_map/ppermute | solution.py:58
  85.6 20.6 %copy-start.1 = (f32[256,256]{1,0:T(8,128)S(1)}, f32[256,256]{1,0:T(8,128)}, u32[]{:S(2)}) copy-start(f32[256,256]{1,0:T(8,128)} %weight_ref.1) | copy-start | bytes 786436
  85.6 20.6 %copy-start.2 = (f32[128,256]{1,0:T(8,128)S(1)}, f32[128,256]{1,0:T(8,128)}, u32[]{:S(2)}) copy-start(f32[128,256]{1,0:T(8,128)} %cot_ref.1) | copy-start | bytes 393220

commit v7 on v6

--- a/solution.py
+++ b/solution.py
@@ -203,9 +203,9 @@
         first = PARTS[far] % 8 * NZH
         return (early, late)[PARTS[far] // 8][lane][first : first + NZH]
 
-    first_a = trade(early[0][: 2 * NZH], RING, 1)
+    far_a = trade(chunk(0, 4), RING, 1)
     first_b = trade(early[1][NZH : 3 * NZH], RING, 0)
-    came = [first_a[NZH:], first_b[:NZH], first_a[:NZH], first_b[NZH:]]
+    came = [far_a, first_b[:NZH], trade(chunk(0, 5), RING, 1), first_b[NZH:]]
     made = late[0]
     for k, (lane, way, far) in enumerate(MESSAGES):
         made = chunk(lane, far) + after(came[k], made)

time: 157 us -> 160 us (1.019)
  starting transfers between devices: 40.8 us -> 48.3 us
  waiting for transfers between devices: 14.4 us -> 10.6 us
  Pallas kernels: 6.17 us -> 4.2 us
    ppermute x12 -> x13, starting transfers between devices: 35.1 us -> 42.7 us  [trade(): lax.ppermute(v, axis, [(k, (k + 1 - 2 * ((k + way) % 2)) % n) for k in ra...]
    ppermute x12 -> x13, waiting for transfers between devices: 14.4 us -> 10.6 us  [trade(): lax.ppermute(v, axis, [(k, (k + 1 - 2 * ((k + way) % 2)) % n) for k in ra...]
    pallas_call x2, Pallas kernels: 4.58 us -> 2.61 us  [sums_of(): pl.pallas_call(functools.partial(add_products, step) if step else first_k...]
  transfers between devices with their start and end apart: 13 -> 14, of which waited for: 5 -> 4; matrix products, arithmetic and copies ran while one was open for 1% -> 1% of each run, Pallas kernels for 2% -> 1%
where the time goes in v7:
time: 160 us; the launch traced here: 159 us
  blocking collectives  88.9 us (56%)
  starting transfers between devices  48.3 us (30%)
  waiting for transfers between devices  10.6 us (7%)
  Pallas kernels  4.2 us (3%)
  local copies, waits for them, and re-layouts  4.05 us (3%)
  between operations  1.62 us (1%)
    all_to_all x5, blocking collectives, swap(): return lax.all_to_all(v, axes, split_axis=0, concat_axis=0, tiled=True)  88.9 us
    ppermute x13, starting transfers between devices, trade(): lax.ppermute(v, axis, [(k, (k + 1 - 2 * ((k + way) % 2)) % n) for k in ra...  42.7 us
    ppermute x13, waiting for transfers between devices, trade(): lax.ppermute(v, axis, [(k, (k + 1 - 2 * ((k + way) % 2)) % n) for k in ra...  10.6 us
    ppermute x1, starting transfers between devices, body(): other = lax.ppermute(own, 'c', [(0, 1), (1, 0)])  5.67 us
  transfers between devices with their start and end apart: 14, of which 4 were waited for; matrix products, arithmetic and copies ran while one was open for 1% of the time, Pallas kernels for 1%

profile of v7, /device:TPU:1, one launch (start us, length us, event | category | flops | bytes accessed | tf_op | source)
XLA Modules:
  0.0 158.9 jit_solution(775703259497684028)
XLA Ops:
  0.6 1.0 broadcast_in_dim.75
  1.6 19.3 %all_to_all.25.own_ref = f32[8,128,256]{2,1,0:T(8,128)S(1)} all-to-all(f32[8,128,256]{2,1,0:T(8,128)S(1)} %broadcast_in_dim.75), channel_id=1, replica_groups=mesh['x'=4,'zl'=2,'c'=2,'yh'=4,'yl'=2,'zh'=4] {'x','zl'}, dimensions={0} | all-to-all | bytes 2097152 | tf_op jit(solution)/shard_map/all_to_all | solution.py:68
  21.0 5.7 %collective-permute-start = (f32[8,128,256]{2,1,0:T(8,128)S(1)}, f32[8,128,256]{2,1,0:T(8,128)S(1)}, u32[]{:S(2)}, u32[]{:S(2)}) collective-permute-start(f32[8,128,256]{2,1,0:T(8,128)S(1)} %all_to_all.25.own_ref), channel_id=1, source_target_pairs={{0,32},{32,0},{1,33},{33,1},{2,34},{34,2},{3,35},{35,3},{4,36},{36... | collective-permute-start | bytes 3145736 | tf_op jit(solution)/shard_map/ppermute | solution.py:197
  27.3 2.2 %copy-done = f32[64,128,128]{2,1,0:T(8,128)S(1)} copy-done((f32[64,128,128]{2,1,0:T(8,128)S(1)}, f32[64,128,128]{2,1,0:T(8,128)}, u32[]{:S(2)}) %copy-start) | copy-done | bytes 4194328
  29.5 0.6 shard_map.86.left_ref
  30.2 0.1 convert_reduce_fusion.1.starts_ref
  30.3 0.2 convert_reduce_fusion
  30.6 1.2 shard_map.87
  31.9 3.3 %collective-permute-start.2 = (f32[8,128,128]{2,1,0:T(8,128)S(1)}, f32[8,128,128]{2,1,0:T(8,128)S(1)}, u32[]{:S(2)}, u32[]{:S(2)}) collective-permute-start(f32[8,128,128]{2,1,0:T(8,128)S(1)} %slice.56), channel_id=1, source_target_pairs={{0,4},{4,0},{8,12},{12,8},{16,20},{20,16},{24,28},{28,24},{1,5},{5... | collective-permute-start | bytes 1572872 | tf_op jit(solution)/shard_map/ppermute | solution.py:58
  35.3 5.5 %collective-permute-start.3 = (f32[4,128,128]{2,1,0:T(8,128)S(1)}, f32[4,128,128]{2,1,0:T(8,128)S(1)}, u32[]{:S(2)}, u32[]{:S(2)}) collective-permute-start(f32[4,128,128]{2,1,0:T(8,128)S(1)} %slice.59), channel_id=1, source_target_pairs={{0,28},{4,8},{8,4},{12,16},{16,12},{20,24},{24,20},{28,0},{1,29},{... | collective-permute-start | bytes 786440 | tf_op jit(solution)/shard_map/ppermute | solution.py:58
  40.8 1.4 shard_map.88
  42.2 5.1 %collective-permute-done.3 = f32[4,128,128]{2,1,0:T(8,128)S(1)} collective-permute-done((f32[4,128,128]{2,1,0:T(8,128)S(1)}, f32[4,128,128]{2,1,0:T(8,128)S(1)}, u32[]{:S(2)}, u32[]{:S(2)}) %collective-permute-start.3) | collective-permute-done | bytes 262176 | tf_op jit(solution)/shard_map/ppermute | solution.py:58
  47.3 4.6 %collective-permute-start.1 = (f32[4,128,128]{2,1,0:T(8,128)S(1)}, f32[4,128,128]{2,1,0:T(8,128)S(1)}, u32[]{:S(2)}, u32[]{:S(2)}) collective-permute-start(f32[4,128,128]{2,1,0:T(8,128)S(1)} %get-tuple-element.51), channel_id=1, source_target_pairs={{0,28},{4,8},{8,4},{12,16},{16,12},{20,24},{24,20},{28,0},{1,29},{... | collective-permute-start | bytes 786440 | tf_op jit(solution)/shard_map/ppermute | solution.py:58
  52.0 1.9 %collective-permute-start.6 = (f32[4,128,128]{2,1,0:T(8,128)S(1)}, f32[4,128,128]{2,1,0:T(8,128)S(1)}, u32[]{:S(2)}, u32[]{:S(2)}) collective-permute-start(f32[4,128,128]{2,1,0:T(8,128)S(1)} %get-tuple-element.50), channel_id=1, source_target_pairs={{0,4},{4,0},{8,12},{12,8},{16,20},{20,16},{24,28},{28,24},{1,5},{5... | collective-permute-start | bytes 786440 | tf_op jit(solution)/shard_map/ppermute | solution.py:58
  54.0 3.9 %collective-permute-start.5 = (f32[4,128,128]{2,1,0:T(8,128)S(1)}, f32[4,128,128]{2,1,0:T(8,128)S(1)}, u32[]{:S(2)}, u32[]{:S(2)}) collective-permute-start(f32[4,128,128]{2,1,0:T(8,128)S(1)} %slice_add_fusion.8), channel_id=1, source_target_pairs={{0,28},{4,8},{8,4},{12,16},{16,12},{20,24},{24,20},{28,0},{1,29},{... | collective-permute-start | bytes 786440 | tf_op jit(solution)/shard_map/ppermute | solution.py:58
  58.0 3.2 %collective-permute-start.4 = (f32[4,128,128]{2,1,0:T(8,128)S(1)}, f32[4,128,128]{2,1,0:T(8,128)S(1)}, u32[]{:S(2)}, u32[]{:S(2)}) collective-permute-start(f32[4,128,128]{2,1,0:T(8,128)S(1)} %slice_add_fusion.9), channel_id=1, source_target_pairs={{0,4},{4,0},{8,12},{12,8},{16,20},{20,16},{24,28},{28,24},{1,5},{5... | collective-permute-start | bytes 786440 | tf_op jit(solution)/shard_map/ppermute | solution.py:58
  61.2 2.9 %collective-permute-start.10 = (f32[4,128,128]{2,1,0:T(8,128)S(1)}, f32[4,128,128]{2,1,0:T(8,128)S(1)}, u32[]{:S(2)}, u32[]{:S(2)}) collective-permute-start(f32[4,128,128]{2,1,0:T(8,128)S(1)} %slice_add_fusion.4), channel_id=1, source_target_pairs={{0,28},{4,8},{8,4},{12,16},{16,12},{20,24},{24,20},{28,0},{1,29},{... | collective-permute-start | bytes 786440 | tf_op jit(solution)/shard_map/ppermute | solution.py:58
  64.2 3.5 %collective-permute-start.9 = (f32[4,128,128]{2,1,0:T(8,128)S(1)}, f32[4,128,128]{2,1,0:T(8,128)S(1)}, u32[]{:S(2)}, u32[]{:S(2)}) collective-permute-start(f32[4,128,128]{2,1,0:T(8,128)S(1)} %slice_add_fusion.5), channel_id=1, source_target_pairs={{0,28},{4,8},{8,4},{12,16},{16,12},{20,24},{24,20},{28,0},{1,29},{... | collective-permute-start | bytes 786440 | tf_op jit(solution)/shard_map/ppermute | solution.py:58
  67.8 1.9 %collective-permute-start.8 = (f32[4,128,128]{2,1,0:T(8,128)S(1)}, f32[4,128,128]{2,1,0:T(8,128)S(1)}, u32[]{:S(2)}, u32[]{:S(2)}) collective-permute-start(f32[4,128,128]{2,1,0:T(8,128)S(1)} %slice_add_fusion.6), channel_id=1, source_target_pairs={{0,4},{4,0},{8,12},{12,8},{16,20},{20,16},{24,28},{28,24},{1,5},{5... | collective-permute-start | bytes 786440 | tf_op jit(solution)/shard_map/ppermute | solution.py:58
  69.8 3.8 %collective-permute-start.7 = (f32[4,128,128]{2,1,0:T(8,128)S(1)}, f32[4,128,128]{2,1,0:T(8,128)S(1)}, u32[]{:S(2)}, u32[]{:S(2)}) collective-permute-start(f32[4,128,128]{2,1,0:T(8,128)S(1)} %slice_add_fusion.10), channel_id=1, source_target_pairs={{0,28},{4,8},{8,4},{12,16},{16,12},{20,24},{24,20},{28,0},{1,29},{... | collective-permute-start | bytes 786440 | tf_op jit(solution)/shard_map/ppermute | solution.py:58
  73.7 1.9 %collective-permute-start.12 = (f32[4,128,128]{2,1,0:T(8,128)S(1)}, f32[4,128,128]{2,1,0:T(8,128)S(1)}, u32[]{:S(2)}, u32[]{:S(2)}) collective-permute-start(f32[4,128,128]{2,1,0:T(8,128)S(1)} %slice_add_fusion.1), channel_id=1, source_target_pairs={{0,4},{4,0},{8,12},{12,8},{16,20},{20,16},{24,28},{28,24},{1,5},{5... | collective-permute-start | bytes 786440 | tf_op jit(solution)/shard_map/ppermute | solution.py:58
  75.6 0.5 collective-permute-done.9
  76.1 2.9 %collective-permute-start.11 = (f32[4,128,128]{2,1,0:T(8,128)S(1)}, f32[4,128,128]{2,1,0:T(8,128)S(1)}, u32[]{:S(2)}, u32[]{:S(2)}) collective-permute-start(f32[4,128,128]{2,1,0:T(8,128)S(1)} %slice_add_fusion.2), channel_id=1, source_target_pairs={{0,4},{4,0},{8,12},{12,8},{16,20},{20,16},{24,28},{28,24},{1,5},{5... | collective-permute-start | bytes 786440 | tf_op jit(solution)/shard_map/ppermute | solution.py:58
  79.1 3.1 %collective-permute-start.13 = (f32[4,128,128]{2,1,0:T(8,128)S(1)}, f32[4,128,128]{2,1,0:T(8,128)S(1)}, u32[]{:S(2)}, u32[]{:S(2)}) collective-permute-start(f32[4,128,128]{2,1,0:T(8,128)S(1)} %slice_add_fusion.3), channel_id=1, source_target_pairs={{0,28},{4,8},{8,4},{12,16},{16,12},{20,24},{24,20},{28,0},{1,29},{... | collective-permute-start | bytes 786440 | tf_op jit(solution)/shard_map/ppermute | solution.py:58
  82.3 3.1 %collective-permute-done.11 = f32[4,128,128]{2,1,0:T(8,128)S(1)} collective-permute-done((f32[4,128,128]{2,1,0:T(8,128)S(1)}, f32[4,128,128]{2,1,0:T(8,128)S(1)}, u32[]{:S(2)}, u32[]{:S(2)}) %collective-permute-start.11) | collective-permute-done | bytes 262176 | tf_op jit(solution)/shard_map/ppermute | solution.py:58
  85.5 1.9 %collective-permute-done.13 = f32[4,128,128]{2,1,0:T(8,128)S(1)} collective-permute-done((f32[4,128,128]{2,1,0:T(8,128)S(1)}, f32[4,128,128]{2,1,0:T(8,128)S(1)}, u32[]{:S(2)}, u32[]{:S(2)}) %collective-permute-start.13) | collective-permute-done | bytes 262176 | tf_op jit(solution)/shard_map/ppermute | solution.py:58
  87.5 20.0 %all_to_all.26.terms_ref = f32[4,128,256]{2,1,0:T(8,128)S(1)} all-to-all(f32[4,128,256]{2,1,0:T(8,128)S(1)} %pad_maximum_fusion), channel_id=1, replica_groups=mesh['x'=4,'zl'=2,'c'=2,'yh'=4,'yl'=2,'zh'=4] {'zh'}, dimensions={0} | all-to-all | bytes 1048576 | tf_op jit(solution)/shard_map/all_to_all | solution.py:68
  107.4 1.0 shard_map.89
  108.4 18.4 %all_to_all.27 = f32[32,2,8,128]{3,2,1,0:T(8,128)S(1)} all-to-all(f32[32,2,8,128]{3,2,1,0:T(8,128)S(1)} %get-tuple-element.47), channel_id=1, replica_groups=mesh['x'=4,'zl'=2,'c'=2,'yh'=4,'yl'=2,'zh'=4] {'x','zl','c','yl'}, dimensions={0} | all-to-all | bytes 524288 | tf_op jit(solution)/shard_map/all_to_all | solution.py:68
  126.8 18.2 %all_to_all.28 = f32[16,2,8,128]{3,2,1,0:T(8,128)S(1)} all-to-all(f32[16,2,8,128]{3,2,1,0:T(8,128)S(1)} %broadcast_in_dim.76), channel_id=1, replica_groups=mesh['x'=4,'zl'=2,'c'=2,'yh'=4,'yl'=2,'zh'=4] {'yh','zh'}, dimensions={0} | all-to-all | bytes 262144 | tf_op jit(solution)/shard_map/all_to_all | solution.py:68
  145.0 13.1 %all_to_all.29 = f32[32,2,8,128]{3,2,1,0:T(8,128)S(1)} all-to-all(f32[32,2,8,128]{3,2,1,0:T(8,128)S(1)} %broadcast_in_dim.77), channel_id=1, replica_groups=mesh['x'=4,'zl'=2,'c'=2,'yh'=4,'yl'=2,'zh'=4] {'x','zl','c','yl'}, dimensions={0} | all-to-all | bytes 524288 | tf_op jit(solution)/shard_map/all_to_all | solution.py:68
  158.2 0.7 copy.11
  (44 shorter events, 1.0 us)
Async XLA Ops:
  21.0 9.7 %collective-permute-start = (f32[8,128,256]{2,1,0:T(8,128)S(1)}, f32[8,128,256]{2,1,0:T(8,128)S(1)}, u32[]{:S(2)}, u32[]{:S(2)}) collective-permute-start(f32[8,128,256]{2,1,0:T(8,128)S(1)} %all_to_all.25.own_ref), channel_id=1, source_target_pairs={{0,32},{32,0},{1,33},{33,1},{2,34},{34,2},{3,35},{35,3},{4,36},{36... | collective-permute-start | bytes 3145736 | tf_op jit(solution)/shard_map/ppermute | solution.py:197
  27.3 2.2 %copy-start = (f32[64,128,128]{2,1,0:T(8,128)S(1)}, f32[64,128,128]{2,1,0:T(8,128)}, u32[]{:S(2)}) copy-start(f32[64,128,128]{2,1,0:T(8,128)} %tiles_ref.1) | copy-start | bytes 12582916
  29.5 0.7 copy-start.3
  29.5 0.7 copy-start.4
  31.9 22.0 %collective-permute-start.2 = (f32[8,128,128]{2,1,0:T(8,128)S(1)}, f32[8,128,128]{2,1,0:T(8,128)S(1)}, u32[]{:S(2)}, u32[]{:S(2)}) collective-permute-start(f32[8,128,128]{2,1,0:T(8,128)S(1)} %slice.56), channel_id=1, source_target_pairs={{0,4},{4,0},{8,12},{12,8},{16,20},{20,16},{24,28},{28,24},{1,5},{5... | collective-permute-start | bytes 1572872 | tf_op jit(solution)/shard_map/ppermute | solution.py:58
  35.3 12.0 %collective-permute-start.3 = (f32[4,128,128]{2,1,0:T(8,128)S(1)}, f32[4,128,128]{2,1,0:T(8,128)S(1)}, u32[]{:S(2)}, u32[]{:S(2)}) collective-permute-start(f32[4,128,128]{2,1,0:T(8,128)S(1)} %slice.59), channel_id=1, source_target_pairs={{0,28},{4,8},{8,4},{12,16},{16,12},{20,24},{24,20},{28,0},{1,29},{... | collective-permute-start | bytes 786440 | tf_op jit(solution)/shard_map/ppermute | solution.py:58
  47.3 10.6 %collective-permute-start.1 = (f32[4,128,128]{2,1,0:T(8,128)S(1)}, f32[4,128,128]{2,1,0:T(8,128)S(1)}, u32[]{:S(2)}, u32[]{:S(2)}) collective-permute-start(f32[4,128,128]{2,1,0:T(8,128)S(1)} %get-tuple-element.51), channel_id=1, source_target_pairs={{0,28},{4,8},{8,4},{12,16},{16,12},{20,24},{24,20},{28,0},{1,29},{... | collective-permute-start | bytes 786440 | tf_op jit(solution)/shard_map/ppermute | solution.py:58
  52.0 12.2 %collective-permute-start.6 = (f32[4,128,128]{2,1,0:T(8,128)S(1)}, f32[4,128,128]{2,1,0:T(8,128)S(1)}, u32[]{:S(2)}, u32[]{:S(2)}) collective-permute-start(f32[4,128,128]{2,1,0:T(8,128)S(1)} %get-tuple-element.50), channel_id=1, source_target_pairs={{0,4},{4,0},{8,12},{12,8},{16,20},{20,16},{24,28},{28,24},{1,5},{5... | collective-permute-start | bytes 786440 | tf_op jit(solution)/shard_map/ppermute | solution.py:58
  54.0 13.8 %collective-permute-start.5 = (f32[4,128,128]{2,1,0:T(8,128)S(1)}, f32[4,128,128]{2,1,0:T(8,128)S(1)}, u32[]{:S(2)}, u32[]{:S(2)}) collective-permute-start(f32[4,128,128]{2,1,0:T(8,128)S(1)} %slice_add_fusion.8), channel_id=1, source_target_pairs={{0,28},{4,8},{8,4},{12,16},{16,12},{20,24},{24,20},{28,0},{1,29},{... | collective-permute-start | bytes 786440 | tf_op jit(solution)/shard_map/ppermute | solution.py:58
  58.0 11.8 %collective-permute-start.4 = (f32[4,128,128]{2,1,0:T(8,128)S(1)}, f32[4,128,128]{2,1,0:T(8,128)S(1)}, u32[]{:S(2)}, u32[]{:S(2)}) collective-permute-start(f32[4,128,128]{2,1,0:T(8,128)S(1)} %slice_add_fusion.9), channel_id=1, source_target_pairs={{0,4},{4,0},{8,12},{12,8},{16,20},{20,16},{24,28},{28,24},{1,5},{5... | collective-permute-start | bytes 786440 | tf_op jit(solution)/shard_map/ppermute | solution.py:58
  61.2 12.4 %collective-permute-start.10 = (f32[4,128,128]{2,1,0:T(8,128)S(1)}, f32[4,128,128]{2,1,0:T(8,128)S(1)}, u32[]{:S(2)}, u32[]{:S(2)}) collective-permute-start(f32[4,128,128]{2,1,0:T(8,128)S(1)} %slice_add_fusion.4), channel_id=1, source_target_pairs={{0,28},{4,8},{8,4},{12,16},{16,12},{20,24},{24,20},{28,0},{1,29},{... | collective-permute-start | bytes 786440 | tf_op jit(solution)/shard_map/ppermute | solution.py:58
  64.2 11.8 %collective-permute-start.9 = (f32[4,128,128]{2,1,0:T(8,128)S(1)}, f32[4,128,128]{2,1,0:T(8,128)S(1)}, u32[]{:S(2)}, u32[]{:S(2)}) collective-permute-start(f32[4,128,128]{2,1,0:T(8,128)S(1)} %slice_add_fusion.5), channel_id=1, source_target_pairs={{0,28},{4,8},{8,4},{12,16},{16,12},{20,24},{24,20},{28,0},{1,29},{... | collective-permute-start | bytes 786440 | tf_op jit(solution)/shard_map/ppermute | solution.py:58
  67.8 11.2 %collective-permute-start.8 = (f32[4,128,128]{2,1,0:T(8,128)S(1)}, f32[4,128,128]{2,1,0:T(8,128)S(1)}, u32[]{:S(2)}, u32[]{:S(2)}) collective-permute-start(f32[4,128,128]{2,1,0:T(8,128)S(1)} %slice_add_fusion.6), channel_id=1, source_target_pairs={{0,4},{4,0},{8,12},{12,8},{16,20},{20,16},{24,28},{28,24},{1,5},{5... | collective-permute-start | bytes 786440 | tf_op jit(solution)/shard_map/ppermute | solution.py:58
  69.8 12.4 %collective-permute-start.7 = (f32[4,128,128]{2,1,0:T(8,128)S(1)}, f32[4,128,128]{2,1,0:T(8,128)S(1)}, u32[]{:S(2)}, u32[]{:S(2)}) collective-permute-start(f32[4,128,128]{2,1,0:T(8,128)S(1)} %slice_add_fusion.10), channel_id=1, source_target_pairs={{0,28},{4,8},{8,4},{12,16},{16,12},{20,24},{24,20},{28,0},{1,29},{... | collective-permute-start | bytes 786440 | tf_op jit(solution)/shard_map/ppermute | solution.py:58
  73.7 8.6 %collective-permute-start.12 = (f32[4,128,128]{2,1,0:T(8,128)S(1)}, f32[4,128,128]{2,1,0:T(8,128)S(1)}, u32[]{:S(2)}, u32[]{:S(2)}) collective-permute-start(f32[4,128,128]{2,1,0:T(8,128)S(1)} %slice_add_fusion.1), channel_id=1, source_target_pairs={{0,4},{4,0},{8,12},{12,8},{16,20},{20,16},{24,28},{28,24},{1,5},{5... | collective-permute-start | bytes 786440 | tf_op jit(solution)/shard_map/ppermute | solution.py:58
  76.1 9.3 %collective-permute-start.11 = (f32[4,128,128]{2,1,0:T(8,128)S(1)}, f32[4,128,128]{2,1,0:T(8,128)S(1)}, u32[]{:S(2)}, u32[]{:S(2)}) collective-permute-start(f32[4,128,128]{2,1,0:T(8,128)S(1)} %slice_add_fusion.2), channel_id=1, source_target_pairs={{0,4},{4,0},{8,12},{12,8},{16,20},{20,16},{24,28},{28,24},{1,5},{5... | collective-permute-start | bytes 786440 | tf_op jit(solution)/shard_map/ppermute | solution.py:58
  79.1 8.3 %collective-permute-start.13 = (f32[4,128,128]{2,1,0:T(8,128)S(1)}, f32[4,128,128]{2,1,0:T(8,128)S(1)}, u32[]{:S(2)}, u32[]{:S(2)}) collective-permute-start(f32[4,128,128]{2,1,0:T(8,128)S(1)} %slice_add_fusion.3), channel_id=1, source_target_pairs={{0,28},{4,8},{8,4},{12,16},{16,12},{20,24},{24,20},{28,0},{1,29},{... | collective-permute-start | bytes 786440 | tf_op jit(solution)/shard_map/ppermute | solution.py:58
  85.5 22.0 %copy-start.1 = (f32[256,256]{1,0:T(8,128)S(1)}, f32[256,256]{1,0:T(8,128)}, u32[]{:S(2)}) copy-start(f32[256,256]{1,0:T(8,128)} %weight_ref.1) | copy-start | bytes 786436
  85.5 21.9 %copy-start.2 = (f32[128,256]{1,0:T(8,128)S(1)}, f32[128,256]{1,0:T(8,128)}, u32[]{:S(2)}) copy-start(f32[128,256]{1,0:T(8,128)} %cot_ref.1) | copy-start | bytes 393220

commit v8 on v6

--- a/solution.py
+++ b/solution.py
@@ -55,13 +55,17 @@
 
 def trade(v, axis, way):
     n = lax.axis_size(axis)
-    return lax.ppermute(v, axis, [(k, (k + 1 - 2 * ((k + way) % 2)) % n) for k in range(n)])
+    pairs = [
+        (c * n + k, c * n + (k + 1 - 2 * ((k + way + c) % 2)) % n) for c in range(NC) for k in range(n)
+    ]
+    return lax.ppermute(v, ("c", *axis), pairs)
 
 
 def ahead(place, axis):
     n = lax.axis_size(axis)
     me = lax.axis_index(axis)
-    return lax.rem((1 - 2 * (me % 2)) * (place - me) + n, n)
+    turn = (me + lax.axis_index("c")) % 2
+    return lax.rem((1 - 2 * turn) * (place - me) + n, n)
 
 
 def swap(v, axes):

time: 157 us -> 156 us (level)
  starting transfers between devices: 40.8 us -> 47.9 us
  waiting for transfers between devices: 14.4 us -> 9.14 us
  Pallas kernels: 6.17 us -> 3.87 us
    ppermute x12, starting transfers between devices: 35.1 us -> 42.3 us  [trade(): return lax.ppermute(v, ('c', *axis), pairs)]
    ppermute x12, waiting for transfers between devices: 14.4 us -> 9.14 us  [trade(): return lax.ppermute(v, ('c', *axis), pairs)]
    pallas_call x2, Pallas kernels: 4.58 us -> 2.28 us  [sums_of(): pl.pallas_call(functools.partial(add_products, step) if step else first_k...]
  transfers between devices with their start and end apart: 13 -> 13, of which waited for: 5 -> 5; matrix products, arithmetic and copies ran while one was open for 1% -> 1% of each run, Pallas kernels for 2% -> 1%
where the time goes in v8:
time: 156 us; the launch traced here: 155 us
  blocking collectives  87.5 us (56%)
  starting transfers between devices  47.9 us (31%)
  waiting for transfers between devices  9.14 us (6%)
  local copies, waits for them, and re-layouts  4.1 us (3%)
  Pallas kernels  3.87 us (2%)
  between operations  1.6 us (1%)
    all_to_all x5, blocking collectives, swap(): return lax.all_to_all(v, axes, split_axis=0, concat_axis=0, tiled=True)  87.5 us
    ppermute x12, starting transfers between devices, trade(): return lax.ppermute(v, ('c', *axis), pairs)  42.3 us
    ppermute x12, waiting for transfers between devices, trade(): return lax.ppermute(v, ('c', *axis), pairs)  9.14 us
    ppermute x1, starting transfers between devices, body(): other = lax.ppermute(own, 'c', [(0, 1), (1, 0)])  5.67 us
  transfers between devices with their start and end apart: 13, of which 5 were waited for; matrix products, arithmetic and copies ran while one was open for 1% of the time, Pallas kernels for 1%

profile of v8, /device:TPU:1, one launch (start us, length us, event | category | flops | bytes accessed | tf_op | source)
XLA Modules:
  0.0 155.3 jit_solution(14674173695443706586)
XLA Ops:
  0.6 1.0 broadcast_in_dim.75
  1.6 19.3 %all_to_all.25.own_ref = f32[8,128,256]{2,1,0:T(8,128)S(1)} all-to-all(f32[8,128,256]{2,1,0:T(8,128)S(1)} %broadcast_in_dim.75), channel_id=1, replica_groups=mesh['x'=4,'zl'=2,'c'=2,'yh'=4,'yl'=2,'zh'=4] {'x','zl'}, dimensions={0} | all-to-all | bytes 2097152 | tf_op jit(solution)/shard_map/all_to_all | solution.py:72
  21.0 5.7 %collective-permute-start = (f32[8,128,256]{2,1,0:T(8,128)S(1)}, f32[8,128,256]{2,1,0:T(8,128)S(1)}, u32[]{:S(2)}, u32[]{:S(2)}) collective-permute-start(f32[8,128,256]{2,1,0:T(8,128)S(1)} %all_to_all.25.own_ref), channel_id=1, source_target_pairs={{0,32},{32,0},{1,33},{33,1},{2,34},{34,2},{3,35},{35,3},{4,36},{36... | collective-permute-start | bytes 3145736 | tf_op jit(solution)/shard_map/ppermute | solution.py:201
  27.3 2.2 %copy-done = f32[64,128,128]{2,1,0:T(8,128)S(1)} copy-done((f32[64,128,128]{2,1,0:T(8,128)S(1)}, f32[64,128,128]{2,1,0:T(8,128)}, u32[]{:S(2)}) %copy-start) | copy-done | bytes 4194328
  29.5 0.6 shard_map.86.left_ref
  30.2 0.1 convert_reduce_fusion.1.starts_ref
  30.3 0.2 convert_reduce_fusion
  30.6 1.2 shard_map.87
  31.9 3.7 %collective-permute-start.1 = (f32[8,128,128]{2,1,0:T(8,128)S(1)}, f32[8,128,128]{2,1,0:T(8,128)S(1)}, u32[]{:S(2)}, u32[]{:S(2)}) collective-permute-start(f32[8,128,128]{2,1,0:T(8,128)S(1)} %slice.57), channel_id=1, source_target_pairs={{0,28},{4,8},{8,4},{12,16},{16,12},{20,24},{24,20},{28,0},{32,36},... | collective-permute-start | bytes 1572872 | tf_op jit(solution)/shard_map/ppermute | solution.py:61
  35.6 5.2 %collective-permute-start.2 = (f32[8,128,128]{2,1,0:T(8,128)S(1)}, f32[8,128,128]{2,1,0:T(8,128)S(1)}, u32[]{:S(2)}, u32[]{:S(2)}) collective-permute-start(f32[8,128,128]{2,1,0:T(8,128)S(1)} %slice.60), channel_id=1, source_target_pairs={{0,4},{4,0},{8,12},{12,8},{16,20},{20,16},{24,28},{28,24},{32,60},... | collective-permute-start | bytes 1572872 | tf_op jit(solution)/shard_map/ppermute | solution.py:61
  40.8 1.1 shard_map.88
  41.9 0.5 collective-permute-done.1
  42.5 7.6 %collective-permute-start.5 = (f32[4,128,128]{2,1,0:T(8,128)S(1)}, f32[4,128,128]{2,1,0:T(8,128)S(1)}, u32[]{:S(2)}, u32[]{:S(2)}) collective-permute-start(f32[4,128,128]{2,1,0:T(8,128)S(1)} %slice_add_fusion.7), channel_id=1, source_target_pairs={{0,4},{4,0},{8,12},{12,8},{16,20},{20,16},{24,28},{28,24},{32,60},... | collective-permute-start | bytes 786440 | tf_op jit(solution)/shard_map/ppermute | solution.py:61
  50.1 0.4 collective-permute-done.2
  50.6 1.9 %collective-permute-start.4 = (f32[4,128,128]{2,1,0:T(8,128)S(1)}, f32[4,128,128]{2,1,0:T(8,128)S(1)}, u32[]{:S(2)}, u32[]{:S(2)}) collective-permute-start(f32[4,128,128]{2,1,0:T(8,128)S(1)} %slice_add_fusion.8), channel_id=1, source_target_pairs={{0,28},{4,8},{8,4},{12,16},{16,12},{20,24},{24,20},{28,0},{32,36},... | collective-permute-start | bytes 786440 | tf_op jit(solution)/shard_map/ppermute | solution.py:61
  52.6 4.9 %collective-permute-start.3 = (f32[4,128,128]{2,1,0:T(8,128)S(1)}, f32[4,128,128]{2,1,0:T(8,128)S(1)}, u32[]{:S(2)}, u32[]{:S(2)}) collective-permute-start(f32[4,128,128]{2,1,0:T(8,128)S(1)} %slice_add_fusion.9), channel_id=1, source_target_pairs={{0,4},{4,0},{8,12},{12,8},{16,20},{20,16},{24,28},{28,24},{32,60},... | collective-permute-start | bytes 786440 | tf_op jit(solution)/shard_map/ppermute | solution.py:61
  57.5 3.4 %collective-permute-start.9 = (f32[4,128,128]{2,1,0:T(8,128)S(1)}, f32[4,128,128]{2,1,0:T(8,128)S(1)}, u32[]{:S(2)}, u32[]{:S(2)}) collective-permute-start(f32[4,128,128]{2,1,0:T(8,128)S(1)} %slice_add_fusion.4), channel_id=1, source_target_pairs={{0,28},{4,8},{8,4},{12,16},{16,12},{20,24},{24,20},{28,0},{32,36},... | collective-permute-start | bytes 786440 | tf_op jit(solution)/shard_map/ppermute | solution.py:61
  61.0 1.9 %collective-permute-start.8 = (f32[4,128,128]{2,1,0:T(8,128)S(1)}, f32[4,128,128]{2,1,0:T(8,128)S(1)}, u32[]{:S(2)}, u32[]{:S(2)}) collective-permute-start(f32[4,128,128]{2,1,0:T(8,128)S(1)} %slice_add_fusion.5), channel_id=1, source_target_pairs={{0,28},{4,8},{8,4},{12,16},{16,12},{20,24},{24,20},{28,0},{32,36},... | collective-permute-start | bytes 786440 | tf_op jit(solution)/shard_map/ppermute | solution.py:61
  62.9 2.6 %collective-permute-start.7 = (f32[4,128,128]{2,1,0:T(8,128)S(1)}, f32[4,128,128]{2,1,0:T(8,128)S(1)}, u32[]{:S(2)}, u32[]{:S(2)}) collective-permute-start(f32[4,128,128]{2,1,0:T(8,128)S(1)} %slice_add_fusion.6), channel_id=1, source_target_pairs={{0,4},{4,0},{8,12},{12,8},{16,20},{20,16},{24,28},{28,24},{32,60},... | collective-permute-start | bytes 786440 | tf_op jit(solution)/shard_map/ppermute | solution.py:61
  65.6 2.7 %collective-permute-start.6 = (f32[4,128,128]{2,1,0:T(8,128)S(1)}, f32[4,128,128]{2,1,0:T(8,128)S(1)}, u32[]{:S(2)}, u32[]{:S(2)}) collective-permute-start(f32[4,128,128]{2,1,0:T(8,128)S(1)} %slice_add_fusion.10), channel_id=1, source_target_pairs={{0,28},{4,8},{8,4},{12,16},{16,12},{20,24},{24,20},{28,0},{32,36},... | collective-permute-start | bytes 786440 | tf_op jit(solution)/shard_map/ppermute | solution.py:61
  68.3 3.3 %collective-permute-start.11 = (f32[4,128,128]{2,1,0:T(8,128)S(1)}, f32[4,128,128]{2,1,0:T(8,128)S(1)}, u32[]{:S(2)}, u32[]{:S(2)}) collective-permute-start(f32[4,128,128]{2,1,0:T(8,128)S(1)} %slice_add_fusion.1), channel_id=1, source_target_pairs={{0,4},{4,0},{8,12},{12,8},{16,20},{20,16},{24,28},{28,24},{32,60},... | collective-permute-start | bytes 786440 | tf_op jit(solution)/shard_map/ppermute | solution.py:61
  71.7 3.2 %collective-permute-start.10 = (f32[4,128,128]{2,1,0:T(8,128)S(1)}, f32[4,128,128]{2,1,0:T(8,128)S(1)}, u32[]{:S(2)}, u32[]{:S(2)}) collective-permute-start(f32[4,128,128]{2,1,0:T(8,128)S(1)} %slice_add_fusion.2), channel_id=1, source_target_pairs={{0,4},{4,0},{8,12},{12,8},{16,20},{20,16},{24,28},{28,24},{32,60},... | collective-permute-start | bytes 786440 | tf_op jit(solution)/shard_map/ppermute | solution.py:61
  75.0 1.9 %collective-permute-start.12 = (f32[4,128,128]{2,1,0:T(8,128)S(1)}, f32[4,128,128]{2,1,0:T(8,128)S(1)}, u32[]{:S(2)}, u32[]{:S(2)}) collective-permute-start(f32[4,128,128]{2,1,0:T(8,128)S(1)} %slice_add_fusion.3), channel_id=1, source_target_pairs={{0,28},{4,8},{8,4},{12,16},{16,12},{20,24},{24,20},{28,0},{32,36},... | collective-permute-start | bytes 786440 | tf_op jit(solution)/shard_map/ppermute | solution.py:61
  76.9 2.9 %collective-permute-done.11 = f32[4,128,128]{2,1,0:T(8,128)S(1)} collective-permute-done((f32[4,128,128]{2,1,0:T(8,128)S(1)}, f32[4,128,128]{2,1,0:T(8,128)S(1)}, u32[]{:S(2)}, u32[]{:S(2)}) %collective-permute-start.11) | collective-permute-done | bytes 262176 | tf_op jit(solution)/shard_map/ppermute | solution.py:61
  79.9 2.6 %collective-permute-done.10 = f32[4,128,128]{2,1,0:T(8,128)S(1)} collective-permute-done((f32[4,128,128]{2,1,0:T(8,128)S(1)}, f32[4,128,128]{2,1,0:T(8,128)S(1)}, u32[]{:S(2)}, u32[]{:S(2)}) %collective-permute-start.10) | collective-permute-done | bytes 262176 | tf_op jit(solution)/shard_map/ppermute | solution.py:61
  82.6 2.7 %collective-permute-done.12 = f32[4,128,128]{2,1,0:T(8,128)S(1)} collective-permute-done((f32[4,128,128]{2,1,0:T(8,128)S(1)}, f32[4,128,128]{2,1,0:T(8,128)S(1)}, u32[]{:S(2)}, u32[]{:S(2)}) %collective-permute-start.12) | collective-permute-done | bytes 262176 | tf_op jit(solution)/shard_map/ppermute | solution.py:61
  85.3 20.5 %all_to_all.26.terms_ref = f32[4,128,256]{2,1,0:T(8,128)S(1)} all-to-all(f32[4,128,256]{2,1,0:T(8,128)S(1)} %pad_maximum_fusion), channel_id=1, replica_groups=mesh['x'=4,'zl'=2,'c'=2,'yh'=4,'yl'=2,'zh'=4] {'zh'}, dimensions={0} | all-to-all | bytes 1048576 | tf_op jit(solution)/shard_map/all_to_all | solution.py:72
  105.8 1.0 shard_map.89
  106.8 18.3 %all_to_all.27 = f32[32,2,8,128]{3,2,1,0:T(8,128)S(1)} all-to-all(f32[32,2,8,128]{3,2,1,0:T(8,128)S(1)} %get-tuple-element.47), channel_id=1, replica_groups=mesh['x'=4,'zl'=2,'c'=2,'yh'=4,'yl'=2,'zh'=4] {'x','zl','c','yl'}, dimensions={0} | all-to-all | bytes 524288 | tf_op jit(solution)/shard_map/all_to_all | solution.py:72
  125.1 16.3 %all_to_all.28 = f32[16,2,8,128]{3,2,1,0:T(8,128)S(1)} all-to-all(f32[16,2,8,128]{3,2,1,0:T(8,128)S(1)} %broadcast_in_dim.76), channel_id=1, replica_groups=mesh['x'=4,'zl'=2,'c'=2,'yh'=4,'yl'=2,'zh'=4] {'yh','zh'}, dimensions={0} | all-to-all | bytes 262144 | tf_op jit(solution)/shard_map/all_to_all | solution.py:72
  141.5 13.1 %all_to_all.29 = f32[32,2,8,128]{3,2,1,0:T(8,128)S(1)} all-to-all(f32[32,2,8,128]{3,2,1,0:T(8,128)S(1)} %broadcast_in_dim.77), channel_id=1, replica_groups=mesh['x'=4,'zl'=2,'c'=2,'yh'=4,'yl'=2,'zh'=4] {'x','zl','c','yl'}, dimensions={0} | all-to-all | bytes 524288 | tf_op jit(solution)/shard_map/all_to_all | solution.py:72
  154.6 0.7 copy.11
  (43 shorter events, 1.1 us)
Async XLA Ops:
  21.0 9.7 %collective-permute-start = (f32[8,128,256]{2,1,0:T(8,128)S(1)}, f32[8,128,256]{2,1,0:T(8,128)S(1)}, u32[]{:S(2)}, u32[]{:S(2)}) collective-permute-start(f32[8,128,256]{2,1,0:T(8,128)S(1)} %all_to_all.25.own_ref), channel_id=1, source_target_pairs={{0,32},{32,0},{1,33},{33,1},{2,34},{34,2},{3,35},{35,3},{4,36},{36... | collective-permute-start | bytes 3145736 | tf_op jit(solution)/shard_map/ppermute | solution.py:201
  27.3 2.2 %copy-start = (f32[64,128,128]{2,1,0:T(8,128)S(1)}, f32[64,128,128]{2,1,0:T(8,128)}, u32[]{:S(2)}) copy-start(f32[64,128,128]{2,1,0:T(8,128)} %tiles_ref.1) | copy-start | bytes 12582916
  29.5 0.7 copy-start.3
  29.5 0.7 copy-start.4
  31.9 10.5 %collective-permute-start.1 = (f32[8,128,128]{2,1,0:T(8,128)S(1)}, f32[8,128,128]{2,1,0:T(8,128)S(1)}, u32[]{:S(2)}, u32[]{:S(2)}) collective-permute-start(f32[8,128,128]{2,1,0:T(8,128)S(1)} %slice.57), channel_id=1, source_target_pairs={{0,28},{4,8},{8,4},{12,16},{16,12},{20,24},{24,20},{28,0},{32,36},... | collective-permute-start | bytes 1572872 | tf_op jit(solution)/shard_map/ppermute | solution.py:61
  35.6 14.9 %collective-permute-start.2 = (f32[8,128,128]{2,1,0:T(8,128)S(1)}, f32[8,128,128]{2,1,0:T(8,128)S(1)}, u32[]{:S(2)}, u32[]{:S(2)}) collective-permute-start(f32[8,128,128]{2,1,0:T(8,128)S(1)} %slice.60), channel_id=1, source_target_pairs={{0,4},{4,0},{8,12},{12,8},{16,20},{20,16},{24,28},{28,24},{32,60},... | collective-permute-start | bytes 1572872 | tf_op jit(solution)/shard_map/ppermute | solution.py:61
  42.5 18.4 %collective-permute-start.5 = (f32[4,128,128]{2,1,0:T(8,128)S(1)}, f32[4,128,128]{2,1,0:T(8,128)S(1)}, u32[]{:S(2)}, u32[]{:S(2)}) collective-permute-start(f32[4,128,128]{2,1,0:T(8,128)S(1)} %slice_add_fusion.7), channel_id=1, source_target_pairs={{0,4},{4,0},{8,12},{12,8},{16,20},{20,16},{24,28},{28,24},{32,60},... | collective-permute-start | bytes 786440 | tf_op jit(solution)/shard_map/ppermute | solution.py:61
  50.6 12.3 %collective-permute-start.4 = (f32[4,128,128]{2,1,0:T(8,128)S(1)}, f32[4,128,128]{2,1,0:T(8,128)S(1)}, u32[]{:S(2)}, u32[]{:S(2)}) collective-permute-start(f32[4,128,128]{2,1,0:T(8,128)S(1)} %slice_add_fusion.8), channel_id=1, source_target_pairs={{0,28},{4,8},{8,4},{12,16},{16,12},{20,24},{24,20},{28,0},{32,36},... | collective-permute-start | bytes 786440 | tf_op jit(solution)/shard_map/ppermute | solution.py:61
  52.6 13.0 %collective-permute-start.3 = (f32[4,128,128]{2,1,0:T(8,128)S(1)}, f32[4,128,128]{2,1,0:T(8,128)S(1)}, u32[]{:S(2)}, u32[]{:S(2)}) collective-permute-start(f32[4,128,128]{2,1,0:T(8,128)S(1)} %slice_add_fusion.9), channel_id=1, source_target_pairs={{0,4},{4,0},{8,12},{12,8},{16,20},{20,16},{24,28},{28,24},{32,60},... | collective-permute-start | bytes 786440 | tf_op jit(solution)/shard_map/ppermute | solution.py:61
  57.5 10.8 %collective-permute-start.9 = (f32[4,128,128]{2,1,0:T(8,128)S(1)}, f32[4,128,128]{2,1,0:T(8,128)S(1)}, u32[]{:S(2)}, u32[]{:S(2)}) collective-permute-start(f32[4,128,128]{2,1,0:T(8,128)S(1)} %slice_add_fusion.4), channel_id=1, source_target_pairs={{0,28},{4,8},{8,4},{12,16},{16,12},{20,24},{24,20},{28,0},{32,36},... | collective-permute-start | bytes 786440 | tf_op jit(solution)/shard_map/ppermute | solution.py:61
  61.0 10.7 %collective-permute-start.8 = (f32[4,128,128]{2,1,0:T(8,128)S(1)}, f32[4,128,128]{2,1,0:T(8,128)S(1)}, u32[]{:S(2)}, u32[]{:S(2)}) collective-permute-start(f32[4,128,128]{2,1,0:T(8,128)S(1)} %slice_add_fusion.5), channel_id=1, source_target_pairs={{0,28},{4,8},{8,4},{12,16},{16,12},{20,24},{24,20},{28,0},{32,36},... | collective-permute-start | bytes 786440 | tf_op jit(solution)/shard_map/ppermute | solution.py:61
  62.9 12.0 %collective-permute-start.7 = (f32[4,128,128]{2,1,0:T(8,128)S(1)}, f32[4,128,128]{2,1,0:T(8,128)S(1)}, u32[]{:S(2)}, u32[]{:S(2)}) collective-permute-start(f32[4,128,128]{2,1,0:T(8,128)S(1)} %slice_add_fusion.6), channel_id=1, source_target_pairs={{0,4},{4,0},{8,12},{12,8},{16,20},{20,16},{24,28},{28,24},{32,60},... | collective-permute-start | bytes 786440 | tf_op jit(solution)/shard_map/ppermute | solution.py:61
  65.6 11.3 %collective-permute-start.6 = (f32[4,128,128]{2,1,0:T(8,128)S(1)}, f32[4,128,128]{2,1,0:T(8,128)S(1)}, u32[]{:S(2)}, u32[]{:S(2)}) collective-permute-start(f32[4,128,128]{2,1,0:T(8,128)S(1)} %slice_add_fusion.10), channel_id=1, source_target_pairs={{0,28},{4,8},{8,4},{12,16},{16,12},{20,24},{24,20},{28,0},{32,36},... | collective-permute-start | bytes 786440 | tf_op jit(solution)/shard_map/ppermute | solution.py:61
  68.3 11.5 %collective-permute-start.11 = (f32[4,128,128]{2,1,0:T(8,128)S(1)}, f32[4,128,128]{2,1,0:T(8,128)S(1)}, u32[]{:S(2)}, u32[]{:S(2)}) collective-permute-start(f32[4,128,128]{2,1,0:T(8,128)S(1)} %slice_add_fusion.1), channel_id=1, source_target_pairs={{0,4},{4,0},{8,12},{12,8},{16,20},{20,16},{24,28},{28,24},{32,60},... | collective-permute-start | bytes 786440 | tf_op jit(solution)/shard_map/ppermute | solution.py:61
  71.7 10.8 %collective-permute-start.10 = (f32[4,128,128]{2,1,0:T(8,128)S(1)}, f32[4,128,128]{2,1,0:T(8,128)S(1)}, u32[]{:S(2)}, u32[]{:S(2)}) collective-permute-start(f32[4,128,128]{2,1,0:T(8,128)S(1)} %slice_add_fusion.2), channel_id=1, source_target_pairs={{0,4},{4,0},{8,12},{12,8},{16,20},{20,16},{24,28},{28,24},{32,60},... | collective-permute-start | bytes 786440 | tf_op jit(solution)/shard_map/ppermute | solution.py:61
  75.0 10.3 %collective-permute-start.12 = (f32[4,128,128]{2,1,0:T(8,128)S(1)}, f32[4,128,128]{2,1,0:T(8,128)S(1)}, u32[]{:S(2)}, u32[]{:S(2)}) collective-permute-start(f32[4,128,128]{2,1,0:T(8,128)S(1)} %slice_add_fusion.3), channel_id=1, source_target_pairs={{0,28},{4,8},{8,4},{12,16},{16,12},{20,24},{24,20},{28,0},{32,36},... | collective-permute-start | bytes 786440 | tf_op jit(solution)/shard_map/ppermute | solution.py:61
  82.5 23.3 %copy-start.1 = (f32[256,256]{1,0:T(8,128)S(1)}, f32[256,256]{1,0:T(8,128)}, u32[]{:S(2)}) copy-start(f32[256,256]{1,0:T(8,128)} %weight_ref.1) | copy-start | bytes 786436
  82.5 23.3 %copy-start.2 = (f32[128,256]{1,0:T(8,128)S(1)}, f32[128,256]{1,0:T(8,128)}, u32[]{:S(2)}) copy-start(f32[128,256]{1,0:T(8,128)} %cot_ref.1) | copy-start | bytes 393220

commit v9 on v6

--- a/solution.py
+++ b/solution.py
@@ -90,35 +90,20 @@
     return ordered, starts
 
 
-def split_kernel(tiles_ref, out_ref):
-    for k in range(tiles_ref.shape[0]):
-        out_ref[k] = jnp.concatenate(halves(tiles_ref[k]), axis=1)
-
-
 def split_tiles(tiles):
-    slots, tile, _ = tiles.shape
-    step = 8
-    return pl.pallas_call(
-        split_kernel,
-        grid=(slots // step,),
-        out_shape=jax.ShapeDtypeStruct((slots, tile, 2 * tile), jnp.bfloat16),
-        in_specs=[pl.BlockSpec((step, tile, tile), lambda k: (k, 0, 0))],
-        out_specs=pl.BlockSpec((step, tile, 2 * tile), lambda k: (k, 0, 0)),
-        compiler_params=pltpu.CompilerParams(vmem_limit_bytes=8 * 1024 * 1024),
-        cost_estimate=pl.CostEstimate(flops=4 * 10**6, bytes_accessed=8 * 2**20, transcendentals=0),
-    )(tiles)
-
-
-def slot_product(left, high, low):
-    tile = left.shape[0]
+    high = lax.reduce_precision(tiles, exponent_bits=8, mantissa_bits=7)
+    return high.astype(jnp.bfloat16), (tiles - high).astype(jnp.bfloat16)
+
+
+def slot_product(tile_high, tile_low, high, low):
     return jnp.dot(
-        jnp.concatenate([left, left[:, :tile]], axis=1),
+        jnp.concatenate([tile_high, tile_low, tile_high], axis=1),
         jnp.concatenate([high, high, low], axis=0),
         preferred_element_type=jnp.float32,
     )
 
 
-def add_products(step, starts_ref, order_ref, left_ref, high, low, out_a_ref, out_b_ref):
+def add_products(step, starts_ref, order_ref, left_high, left_low, high, low, out_a_ref, out_b_ref):
     first, last = starts_ref[step], starts_ref[step + 1]
     slots, spare = order_ref.shape[0], out_a_ref.shape[0] - 1
     out_a_ref[...] = jnp.zeros_like(out_a_ref)
@@ -130,21 +115,22 @@
             index = first + group * GROUP + k
             packed = order_ref[jnp.minimum(index, slots - 1)]
             row = jnp.where(index < last, packed // 16 % 32, spare)
-            value = slot_product(left_ref[packed // 512], high[packed % 16], low[packed % 16])
+            slot, block = packed // 512, packed % 16
+            value = slot_product(left_high[slot], left_low[slot], high[block], low[block])
             out_a_ref[row] += value[:, :LANES]
             out_b_ref[row] += value[:, LANES:]
 
 
-def first_kernel(starts_ref, order_ref, left_ref, own_ref, other_ref, out_a_ref, out_b_ref, high, low):
+def first_kernel(starts_ref, order_ref, left_high, left_low, own_ref, other_ref, out_a_ref, out_b_ref, high, low):
     blocks = own_ref.shape[0]
     for k, source in enumerate((own_ref, other_ref)):
         for b in range(blocks):
             high[k * blocks + b], low[k * blocks + b] = halves(source[b])
-    add_products(0, starts_ref, order_ref, left_ref, high, low, out_a_ref, out_b_ref)
+    add_products(0, starts_ref, order_ref, left_high, left_low, high, low, out_a_ref, out_b_ref)
 
 
 def sums_of(step, starts, ordered, left, sources):
-    tile = left.shape[1]
+    tile = left[0].shape[1]
     rows = NZH * (3, 5)[step] + 1
     shapes = [jax.ShapeDtypeStruct((rows, tile, LANES), jnp.float32)] * 2
     if step == 0:
@@ -154,11 +140,11 @@
     return pl.pallas_call(
         functools.partial(add_products, step) if step else first_kernel,
         out_shape=shapes,
-        in_specs=[smem, smem, vmem, vmem, vmem],
+        in_specs=[smem, smem, vmem, vmem, vmem, vmem],
         out_specs=[vmem] * len(shapes),
         compiler_params=pltpu.CompilerParams(vmem_limit_bytes=16 * 1024 * 1024),
         cost_estimate=pl.CostEstimate(flops=10**6, bytes_accessed=2**14, transcendentals=0),
-    )(starts, ordered, left, *sources)
+    )(starts, ordered, *left, *sources)
 
 
 def node_kernel(terms_ref, weight_ref, cot_ref, act_ref, grad_ref):

time: 157 us -> 158 us (level)
  blocking collectives: 87.7 us -> 67.5 us
  waiting for transfers between devices: 14.4 us -> 26.7 us
  starting transfers between devices: 40.8 us -> 49.4 us
  other arithmetic: 1.11 us -> 4.44 us
    all_to_all x5 -> x4, blocking collectives: 87.7 us -> 67.5 us  [swap(): return lax.all_to_all(v, axes, split_axis=0, concat_axis=0, tiled=True)]
    all_to_all x0 -> x1, waiting for transfers between devices: none -> 12.1 us  [swap(): return lax.all_to_all(v, axes, split_axis=0, concat_axis=0, tiled=True)]
    all_to_all x0 -> x1, starting transfers between devices: none -> 6.66 us  [swap(): return lax.all_to_all(v, axes, split_axis=0, concat_axis=0, tiled=True)]
    convert_element_type x0 -> x1, other arithmetic: none -> 3.37 us  [split_tiles(): return (high.astype(jnp.bfloat16), (tiles - high).astype(jnp.bfloat16))]
    unnamed x11 -> x9, local copies, waits for them, and re-layouts: 2.95 us -> 0.72 us
  transfers between devices with their start and end apart: 13 -> 14, of which waited for: 5 -> 6; matrix products, arithmetic and copies ran while one was open for 1% -> 3% of each run, Pallas kernels for 2% -> 2%
where the time goes in v9:
time: 158 us; the launch traced here: 157 us
  blocking collectives  67.5 us (43%)
  starting transfers between devices  49.4 us (31%)
  waiting for transfers between devices  26.7 us (17%)
  Pallas kernels  4.9 us (3%)
  other arithmetic  4.44 us (3%)
  local copies, waits for them, and re-layouts  2.87 us (2%)
  between operations  1.64 us (1%)
    all_to_all x4, blocking collectives, swap(): return lax.all_to_all(v, axes, split_axis=0, concat_axis=0, tiled=True)  67.5 us
    ppermute x12, starting transfers between devices, trade(): lax.ppermute(v, axis, [(k, (k + 1 - 2 * ((k + way) % 2)) % n) for k in ra...  36.2 us
    ppermute x12, waiting for transfers between devices, trade(): lax.ppermute(v, axis, [(k, (k + 1 - 2 * ((k + way) % 2)) % n) for k in ra...  14.6 us
    all_to_all x1, waiting for transfers between devices, swap(): return lax.all_to_all(v, axes, split_axis=0, concat_axis=0, tiled=True)  12.1 us
    all_to_all x1, starting transfers between devices, swap(): return lax.all_to_all(v, axes, split_axis=0, concat_axis=0, tiled=True)  6.66 us
    ppermute x1, starting transfers between devices, body(): other = lax.ppermute(own, 'c', [(0, 1), (1, 0)])  6.54 us
    pallas_call x2, Pallas kernels, sums_of(): pl.pallas_call(functools.partial(add_products, step) if step else first_k...  3.92 us
    convert_element_type x1, other arithmetic, split_tiles(): return (high.astype(jnp.bfloat16), (tiles - high).astype(jnp.bfloat16))  3.37 us
  transfers between devices with their start and end apart: 14, of which 6 were waited for; matrix products, arithmetic and copies ran while one was open for 3% of the time, Pallas kernels for 2%

profile of v9, /device:TPU:1, one launch (start us, length us, event | category | flops | bytes accessed | tf_op | source)
XLA Modules:
  0.0 157.4 jit_solution(4566932672624616657)
XLA Ops:
  0.6 2.0 %broadcast_in_dim.75 = f32[8,128,256]{2,1,0:T(8,128)} broadcast(f32[128,256]{1,0:T(8,128)} %param.7), dimensions={1,2} | broadcast | bytes 1179648 | tf_op jit(solution)/shard_map/broadcast_in_dim | solution.py:72
  2.6 6.7 %all-to-all-start = ((f32[8,128,256]{2,1,0:T(8,128)}), f32[8,128,256]{2,1,0:T(8,128)S(1)}, u32[]{:S(2)}, u32[]{:S(2)}) async-start(f32[8,128,256]{2,1,0:T(8,128)} %broadcast_in_dim.75), calls=%async_computation | async-start | bytes 2097152 | tf_op jit(solution)/shard_map/all_to_all | solution.py:68
  9.3 12.1 %all-to-all-done.own_ref = f32[8,128,256]{2,1,0:T(8,128)S(1)} async-done(((f32[8,128,256]{2,1,0:T(8,128)}), f32[8,128,256]{2,1,0:T(8,128)S(1)}, u32[]{:S(2)}, u32[]{:S(2)}) %all-to-all-start) | async-done | bytes 1048608 | tf_op jit(solution)/shard_map/all_to_all | solution.py:68
  21.4 6.5 %collective-permute-start = (f32[8,128,256]{2,1,0:T(8,128)S(1)}, f32[8,128,256]{2,1,0:T(8,128)S(1)}, u32[]{:S(2)}, u32[]{:S(2)}) collective-permute-start(f32[8,128,256]{2,1,0:T(8,128)S(1)} %all-to-all-done.own_ref), channel_id=1, source_target_pairs={{0,32},{32,0},{1,33},{33,1},{2,34},{34,2},{3,35},{35,3},{4,36},{36... | collective-permute-start | bytes 3145736 | tf_op jit(solution)/shard_map/ppermute | solution.py:183
  28.8 0.2 convert_reduce_fusion
  29.0 0.1 select_reduce_fusion.order_ref
  29.1 3.4 %fusion = (bf16[64,128,128]{2,1,0:T(8,128)(2,1)S(1)}, bf16[64,128,128]{2,1,0:T(8,128)(2,1)S(1)}) fusion(f32[64,128,128]{2,1,0:T(8,128)} %param.8), kind=kLoop, calls=%fused_computation.2 | loop fusion | flops 4194304 | bytes 8388608 | tf_op jit(solution)/shard_map/convert_element_type | solution.py:95
  32.5 1.6 shard_map.86
  34.1 6.0 %collective-permute-start.1 = (f32[8,128,128]{2,1,0:T(8,128)S(1)}, f32[8,128,128]{2,1,0:T(8,128)S(1)}, u32[]{:S(2)}, u32[]{:S(2)}) collective-permute-start(f32[8,128,128]{2,1,0:T(8,128)S(1)} %slice.57), channel_id=1, source_target_pairs={{0,28},{4,8},{8,4},{12,16},{16,12},{20,24},{24,20},{28,0},{1,29},{... | collective-permute-start | bytes 1572872 | tf_op jit(solution)/shard_map/ppermute | solution.py:58
  40.1 1.9 %collective-permute-start.2 = (f32[8,128,128]{2,1,0:T(8,128)S(1)}, f32[8,128,128]{2,1,0:T(8,128)S(1)}, u32[]{:S(2)}, u32[]{:S(2)}) collective-permute-start(f32[8,128,128]{2,1,0:T(8,128)S(1)} %slice.60), channel_id=1, source_target_pairs={{0,4},{4,0},{8,12},{12,8},{16,20},{20,16},{24,28},{28,24},{1,5},{5... | collective-permute-start | bytes 1572872 | tf_op jit(solution)/shard_map/ppermute | solution.py:58
  42.0 2.4 %shard_map.87 = (f32[21,128,128]{2,1,0:T(8,128)S(1)}, f32[21,128,128]{2,1,0:T(8,128)S(1)}) custom-call(s32[8]{0:T(128)S(1)} %convert_reduce_fusion.1.starts_ref, s32[64]{0:T(128)S(1)} %select_reduce_fusion.order_ref, bf16[64,128,128]{2,1,0:T(8,128)(2,1)S(1)} %get-tuple-element.51.left_high, bf16[64,128,128]{2,1,0:T(8,128)(2,1)S(1)} %get-tuple-element.50.left_low, ...), custom_call_target="tpu_custom_call" | custom-call | flops 1000000 | bytes 16384 | tf_op jit(solution)/shard_map/pallas_call | solution.py:140
  44.4 7.8 %collective-permute-done.1 = f32[8,128,128]{2,1,0:T(8,128)S(1)} collective-permute-done((f32[8,128,128]{2,1,0:T(8,128)S(1)}, f32[8,128,128]{2,1,0:T(8,128)S(1)}, u32[]{:S(2)}, u32[]{:S(2)}) %collective-permute-start.1) | collective-permute-done | bytes 524320 | tf_op jit(solution)/shard_map/ppermute | solution.py:58
  52.3 1.9 %collective-permute-start.5 = (f32[4,128,128]{2,1,0:T(8,128)S(1)}, f32[4,128,128]{2,1,0:T(8,128)S(1)}, u32[]{:S(2)}, u32[]{:S(2)}) collective-permute-start(f32[4,128,128]{2,1,0:T(8,128)S(1)} %slice_add_fusion.7), channel_id=1, source_target_pairs={{0,4},{4,0},{8,12},{12,8},{16,20},{20,16},{24,28},{28,24},{1,5},{5... | collective-permute-start | bytes 786440 | tf_op jit(solution)/shard_map/ppermute | solution.py:58
  54.3 1.0 collective-permute-done.2
  55.3 3.5 %collective-permute-start.4 = (f32[4,128,128]{2,1,0:T(8,128)S(1)}, f32[4,128,128]{2,1,0:T(8,128)S(1)}, u32[]{:S(2)}, u32[]{:S(2)}) collective-permute-start(f32[4,128,128]{2,1,0:T(8,128)S(1)} %slice_add_fusion.8), channel_id=1, source_target_pairs={{0,28},{4,8},{8,4},{12,16},{16,12},{20,24},{24,20},{28,0},{1,29},{... | collective-permute-start | bytes 786440 | tf_op jit(solution)/shard_map/ppermute | solution.py:58
  58.9 2.1 %collective-permute-start.3 = (f32[4,128,128]{2,1,0:T(8,128)S(1)}, f32[4,128,128]{2,1,0:T(8,128)S(1)}, u32[]{:S(2)}, u32[]{:S(2)}) collective-permute-start(f32[4,128,128]{2,1,0:T(8,128)S(1)} %slice_add_fusion.9), channel_id=1, source_target_pairs={{0,4},{4,0},{8,12},{12,8},{16,20},{20,16},{24,28},{28,24},{1,5},{5... | collective-permute-start | bytes 786440 | tf_op jit(solution)/shard_map/ppermute | solution.py:58
  61.0 4.6 %collective-permute-start.9 = (f32[4,128,128]{2,1,0:T(8,128)S(1)}, f32[4,128,128]{2,1,0:T(8,128)S(1)}, u32[]{:S(2)}, u32[]{:S(2)}) collective-permute-start(f32[4,128,128]{2,1,0:T(8,128)S(1)} %slice_add_fusion.4), channel_id=1, source_target_pairs={{0,28},{4,8},{8,4},{12,16},{16,12},{20,24},{24,20},{28,0},{1,29},{... | collective-permute-start | bytes 786440 | tf_op jit(solution)/shard_map/ppermute | solution.py:58
  65.7 1.9 %collective-permute-start.8 = (f32[4,128,128]{2,1,0:T(8,128)S(1)}, f32[4,128,128]{2,1,0:T(8,128)S(1)}, u32[]{:S(2)}, u32[]{:S(2)}) collective-permute-start(f32[4,128,128]{2,1,0:T(8,128)S(1)} %slice_add_fusion.5), channel_id=1, source_target_pairs={{0,28},{4,8},{8,4},{12,16},{16,12},{20,24},{24,20},{28,0},{1,29},{... | collective-permute-start | bytes 786440 | tf_op jit(solution)/shard_map/ppermute | solution.py:58
  67.7 1.9 %collective-permute-start.7 = (f32[4,128,128]{2,1,0:T(8,128)S(1)}, f32[4,128,128]{2,1,0:T(8,128)S(1)}, u32[]{:S(2)}, u32[]{:S(2)}) collective-permute-start(f32[4,128,128]{2,1,0:T(8,128)S(1)} %slice_add_fusion.6), channel_id=1, source_target_pairs={{0,4},{4,0},{8,12},{12,8},{16,20},{20,16},{24,28},{28,24},{1,5},{5... | collective-permute-start | bytes 786440 | tf_op jit(solution)/shard_map/ppermute | solution.py:58
  69.7 4.6 %collective-permute-start.6 = (f32[4,128,128]{2,1,0:T(8,128)S(1)}, f32[4,128,128]{2,1,0:T(8,128)S(1)}, u32[]{:S(2)}, u32[]{:S(2)}) collective-permute-start(f32[4,128,128]{2,1,0:T(8,128)S(1)} %slice_add_fusion.10), channel_id=1, source_target_pairs={{0,28},{4,8},{8,4},{12,16},{16,12},{20,24},{24,20},{28,0},{1,29},{... | collective-permute-start | bytes 786440 | tf_op jit(solution)/shard_map/ppermute | solution.py:58
  74.3 1.9 %collective-permute-start.11 = (f32[4,128,128]{2,1,0:T(8,128)S(1)}, f32[4,128,128]{2,1,0:T(8,128)S(1)}, u32[]{:S(2)}, u32[]{:S(2)}) collective-permute-start(f32[4,128,128]{2,1,0:T(8,128)S(1)} %slice_add_fusion.1), channel_id=1, source_target_pairs={{0,4},{4,0},{8,12},{12,8},{16,20},{20,16},{24,28},{28,24},{1,5},{5... | collective-permute-start | bytes 786440 | tf_op jit(solution)/shard_map/ppermute | solution.py:58
  76.2 0.8 collective-permute-done.8
  77.1 2.5 %collective-permute-start.10 = (f32[4,128,128]{2,1,0:T(8,128)S(1)}, f32[4,128,128]{2,1,0:T(8,128)S(1)}, u32[]{:S(2)}, u32[]{:S(2)}) collective-permute-start(f32[4,128,128]{2,1,0:T(8,128)S(1)} %slice_add_fusion.2), channel_id=1, source_target_pairs={{0,4},{4,0},{8,12},{12,8},{16,20},{20,16},{24,28},{28,24},{1,5},{5... | collective-permute-start | bytes 786440 | tf_op jit(solution)/shard_map/ppermute | solution.py:58
  79.7 3.3 %collective-permute-start.12 = (f32[4,128,128]{2,1,0:T(8,128)S(1)}, f32[4,128,128]{2,1,0:T(8,128)S(1)}, u32[]{:S(2)}, u32[]{:S(2)}) collective-permute-start(f32[4,128,128]{2,1,0:T(8,128)S(1)} %slice_add_fusion.3), channel_id=1, source_target_pairs={{0,28},{4,8},{8,4},{12,16},{16,12},{20,24},{24,20},{28,0},{1,29},{... | collective-permute-start | bytes 786440 | tf_op jit(solution)/shard_map/ppermute | solution.py:58
  83.0 4.5 %collective-permute-done.10 = f32[4,128,128]{2,1,0:T(8,128)S(1)} collective-permute-done((f32[4,128,128]{2,1,0:T(8,128)S(1)}, f32[4,128,128]{2,1,0:T(8,128)S(1)}, u32[]{:S(2)}, u32[]{:S(2)}) %collective-permute-start.10) | collective-permute-done | bytes 262176 | tf_op jit(solution)/shard_map/ppermute | solution.py:58
  87.6 0.4 collective-permute-done.12
  88.1 20.2 %all_to_all.25.terms_ref = f32[4,128,256]{2,1,0:T(8,128)S(1)} all-to-all(f32[4,128,256]{2,1,0:T(8,128)S(1)} %pad_maximum_fusion), channel_id=1, replica_groups=mesh['x'=4,'zl'=2,'c'=2,'yh'=4,'yl'=2,'zh'=4] {'zh'}, dimensions={0} | all-to-all | bytes 1048576 | tf_op jit(solution)/shard_map/all_to_all | solution.py:68
  108.3 1.0 shard_map.88
  109.3 17.9 %all_to_all.26 = f32[32,2,8,128]{3,2,1,0:T(8,128)S(1)} all-to-all(f32[32,2,8,128]{3,2,1,0:T(8,128)S(1)} %get-tuple-element.47), channel_id=1, replica_groups=mesh['x'=4,'zl'=2,'c'=2,'yh'=4,'yl'=2,'zh'=4] {'x','zl','c','yl'}, dimensions={0} | all-to-all | bytes 524288 | tf_op jit(solution)/shard_map/all_to_all | solution.py:68
  127.2 16.3 %all_to_all.27 = f32[16,2,8,128]{3,2,1,0:T(8,128)S(1)} all-to-all(f32[16,2,8,128]{3,2,1,0:T(8,128)S(1)} %broadcast_in_dim.76), channel_id=1, replica_groups=mesh['x'=4,'zl'=2,'c'=2,'yh'=4,'yl'=2,'zh'=4] {'yh','zh'}, dimensions={0} | all-to-all | bytes 262144 | tf_op jit(solution)/shard_map/all_to_all | solution.py:68
  143.6 13.1 %all_to_all.28 = f32[32,2,8,128]{3,2,1,0:T(8,128)S(1)} all-to-all(f32[32,2,8,128]{3,2,1,0:T(8,128)S(1)} %broadcast_in_dim.77), channel_id=1, replica_groups=mesh['x'=4,'zl'=2,'c'=2,'yh'=4,'yl'=2,'zh'=4] {'x','zl','c','yl'}, dimensions={0} | all-to-all | bytes 524288 | tf_op jit(solution)/shard_map/all_to_all | solution.py:68
  156.7 0.7 copy.11
  (42 shorter events, 1.0 us)
Async XLA Ops:
  0.6 27.3 %copy-start.2 = (s32[64]{0:T(128)S(1)}, s32[64]{0:T(128)}, u32[]{:S(2)}) copy-start(s32[64]{0:T(128)} %param.10) | copy-start | bytes 772
  0.6 27.3 %copy-start.3 = (s32[64]{0:T(128)S(1)}, s32[64]{0:T(128)}, u32[]{:S(2)}) copy-start(s32[64]{0:T(128)} %param.9) | copy-start | bytes 772
  2.6 18.8 %all-to-all-start = ((f32[8,128,256]{2,1,0:T(8,128)}), f32[8,128,256]{2,1,0:T(8,128)S(1)}, u32[]{:S(2)}, u32[]{:S(2)}) async-start(f32[8,128,256]{2,1,0:T(8,128)} %broadcast_in_dim.75), calls=%async_computation | async-start | bytes 2097152 | tf_op jit(solution)/shard_map/all_to_all | solution.py:68
  21.4 11.1 %collective-permute-start = (f32[8,128,256]{2,1,0:T(8,128)S(1)}, f32[8,128,256]{2,1,0:T(8,128)S(1)}, u32[]{:S(2)}, u32[]{:S(2)}) collective-permute-start(f32[8,128,256]{2,1,0:T(8,128)S(1)} %all-to-all-done.own_ref), channel_id=1, source_target_pairs={{0,32},{32,0},{1,33},{33,1},{2,34},{34,2},{3,35},{35,3},{4,36},{36... | collective-permute-start | bytes 3145736 | tf_op jit(solution)/shard_map/ppermute | solution.py:183
  34.1 18.2 %collective-permute-start.1 = (f32[8,128,128]{2,1,0:T(8,128)S(1)}, f32[8,128,128]{2,1,0:T(8,128)S(1)}, u32[]{:S(2)}, u32[]{:S(2)}) collective-permute-start(f32[8,128,128]{2,1,0:T(8,128)S(1)} %slice.57), channel_id=1, source_target_pairs={{0,28},{4,8},{8,4},{12,16},{16,12},{20,24},{24,20},{28,0},{1,29},{... | collective-permute-start | bytes 1572872 | tf_op jit(solution)/shard_map/ppermute | solution.py:58
  40.1 15.1 %collective-permute-start.2 = (f32[8,128,128]{2,1,0:T(8,128)S(1)}, f32[8,128,128]{2,1,0:T(8,128)S(1)}, u32[]{:S(2)}, u32[]{:S(2)}) collective-permute-start(f32[8,128,128]{2,1,0:T(8,128)S(1)} %slice.60), channel_id=1, source_target_pairs={{0,4},{4,0},{8,12},{12,8},{16,20},{20,16},{24,28},{28,24},{1,5},{5... | collective-permute-start | bytes 1572872 | tf_op jit(solution)/shard_map/ppermute | solution.py:58
  52.3 13.3 %collective-permute-start.5 = (f32[4,128,128]{2,1,0:T(8,128)S(1)}, f32[4,128,128]{2,1,0:T(8,128)S(1)}, u32[]{:S(2)}, u32[]{:S(2)}) collective-permute-start(f32[4,128,128]{2,1,0:T(8,128)S(1)} %slice_add_fusion.7), channel_id=1, source_target_pairs={{0,4},{4,0},{8,12},{12,8},{16,20},{20,16},{24,28},{28,24},{1,5},{5... | collective-permute-start | bytes 786440 | tf_op jit(solution)/shard_map/ppermute | solution.py:58
  55.3 12.3 %collective-permute-start.4 = (f32[4,128,128]{2,1,0:T(8,128)S(1)}, f32[4,128,128]{2,1,0:T(8,128)S(1)}, u32[]{:S(2)}, u32[]{:S(2)}) collective-permute-start(f32[4,128,128]{2,1,0:T(8,128)S(1)} %slice_add_fusion.8), channel_id=1, source_target_pairs={{0,28},{4,8},{8,4},{12,16},{16,12},{20,24},{24,20},{28,0},{1,29},{... | collective-permute-start | bytes 786440 | tf_op jit(solution)/shard_map/ppermute | solution.py:58
  58.9 10.7 %collective-permute-start.3 = (f32[4,128,128]{2,1,0:T(8,128)S(1)}, f32[4,128,128]{2,1,0:T(8,128)S(1)}, u32[]{:S(2)}, u32[]{:S(2)}) collective-permute-start(f32[4,128,128]{2,1,0:T(8,128)S(1)} %slice_add_fusion.9), channel_id=1, source_target_pairs={{0,4},{4,0},{8,12},{12,8},{16,20},{20,16},{24,28},{28,24},{1,5},{5... | collective-permute-start | bytes 786440 | tf_op jit(solution)/shard_map/ppermute | solution.py:58
  61.0 13.2 %collective-permute-start.9 = (f32[4,128,128]{2,1,0:T(8,128)S(1)}, f32[4,128,128]{2,1,0:T(8,128)S(1)}, u32[]{:S(2)}, u32[]{:S(2)}) collective-permute-start(f32[4,128,128]{2,1,0:T(8,128)S(1)} %slice_add_fusion.4), channel_id=1, source_target_pairs={{0,28},{4,8},{8,4},{12,16},{16,12},{20,24},{24,20},{28,0},{1,29},{... | collective-permute-start | bytes 786440 | tf_op jit(solution)/shard_map/ppermute | solution.py:58
  65.7 11.4 %collective-permute-start.8 = (f32[4,128,128]{2,1,0:T(8,128)S(1)}, f32[4,128,128]{2,1,0:T(8,128)S(1)}, u32[]{:S(2)}, u32[]{:S(2)}) collective-permute-start(f32[4,128,128]{2,1,0:T(8,128)S(1)} %slice_add_fusion.5), channel_id=1, source_target_pairs={{0,28},{4,8},{8,4},{12,16},{16,12},{20,24},{24,20},{28,0},{1,29},{... | collective-permute-start | bytes 786440 | tf_op jit(solution)/shard_map/ppermute | solution.py:58
  67.7 12.0 %collective-permute-start.7 = (f32[4,128,128]{2,1,0:T(8,128)S(1)}, f32[4,128,128]{2,1,0:T(8,128)S(1)}, u32[]{:S(2)}, u32[]{:S(2)}) collective-permute-start(f32[4,128,128]{2,1,0:T(8,128)S(1)} %slice_add_fusion.6), channel_id=1, source_target_pairs={{0,4},{4,0},{8,12},{12,8},{16,20},{20,16},{24,28},{28,24},{1,5},{5... | collective-permute-start | bytes 786440 | tf_op jit(solution)/shard_map/ppermute | solution.py:58
  69.7 13.3 %collective-permute-start.6 = (f32[4,128,128]{2,1,0:T(8,128)S(1)}, f32[4,128,128]{2,1,0:T(8,128)S(1)}, u32[]{:S(2)}, u32[]{:S(2)}) collective-permute-start(f32[4,128,128]{2,1,0:T(8,128)S(1)} %slice_add_fusion.10), channel_id=1, source_target_pairs={{0,28},{4,8},{8,4},{12,16},{16,12},{20,24},{24,20},{28,0},{1,29},{... | collective-permute-start | bytes 786440 | tf_op jit(solution)/shard_map/ppermute | solution.py:58
  74.3 8.7 %collective-permute-start.11 = (f32[4,128,128]{2,1,0:T(8,128)S(1)}, f32[4,128,128]{2,1,0:T(8,128)S(1)}, u32[]{:S(2)}, u32[]{:S(2)}) collective-permute-start(f32[4,128,128]{2,1,0:T(8,128)S(1)} %slice_add_fusion.1), channel_id=1, source_target_pairs={{0,4},{4,0},{8,12},{12,8},{16,20},{20,16},{24,28},{28,24},{1,5},{5... | collective-permute-start | bytes 786440 | tf_op jit(solution)/shard_map/ppermute | solution.py:58
  77.1 10.4 %collective-permute-start.10 = (f32[4,128,128]{2,1,0:T(8,128)S(1)}, f32[4,128,128]{2,1,0:T(8,128)S(1)}, u32[]{:S(2)}, u32[]{:S(2)}) collective-permute-start(f32[4,128,128]{2,1,0:T(8,128)S(1)} %slice_add_fusion.2), channel_id=1, source_target_pairs={{0,4},{4,0},{8,12},{12,8},{16,20},{20,16},{24,28},{28,24},{1,5},{5... | collective-permute-start | bytes 786440 | tf_op jit(solution)/shard_map/ppermute | solution.py:58
  79.7 8.3 %collective-permute-start.12 = (f32[4,128,128]{2,1,0:T(8,128)S(1)}, f32[4,128,128]{2,1,0:T(8,128)S(1)}, u32[]{:S(2)}, u32[]{:S(2)}) collective-permute-start(f32[4,128,128]{2,1,0:T(8,128)S(1)} %slice_add_fusion.3), channel_id=1, source_target_pairs={{0,28},{4,8},{8,4},{12,16},{16,12},{20,24},{24,20},{28,0},{1,29},{... | collective-permute-start | bytes 786440 | tf_op jit(solution)/shard_map/ppermute | solution.py:58
  87.5 20.8 %copy-start = (f32[256,256]{1,0:T(8,128)S(1)}, f32[256,256]{1,0:T(8,128)}, u32[]{:S(2)}) copy-start(f32[256,256]{1,0:T(8,128)} %weight_ref.1) | copy-start | bytes 786436
  87.5 20.8 %copy-start.1 = (f32[128,256]{1,0:T(8,128)S(1)}, f32[128,256]{1,0:T(8,128)}, u32[]{:S(2)}) copy-start(f32[128,256]{1,0:T(8,128)} %cot_ref.1) | copy-start | bytes 393220

commit v10 on v9

--- a/solution.py
+++ b/solution.py
@@ -180,8 +180,10 @@
 def body(features, adjacency_tiles, tile_rows, tile_cols, tile_count, weight, cotangent):
     ordered, starts = slot_plan(tile_rows, tile_cols, tile_count)
     own = share(features, ("x", "zl"))
-    other = lax.ppermute(own, "c", [(0, 1), (1, 0)])
     left = split_tiles(adjacency_tiles)
+    ready = lax.optimization_barrier((own, ordered, starts, *left))
+    other = lax.ppermute(ready[0], "c", [(0, 1), (1, 0)])
+    own, ordered, starts, *left = ready
     *early, high, low = sums_of(0, starts, ordered, left, (own, other))
     late = sums_of(1, after(starts, early[0]), ordered, left, (high, low))
 

time: 158 us -> 157 us (level)
  waiting for transfers between devices: 26.7 us -> 24.1 us
  Pallas kernels: 4.9 us -> 3.26 us
  local copies, waits for them, and re-layouts: 2.87 us -> 4.46 us
    all_to_all x1, waiting for transfers between devices: 12.1 us -> 6.25 us  [swap(): return lax.all_to_all(v, axes, split_axis=0, concat_axis=0, tiled=True)]
    ppermute x1, waiting for transfers between devices: 0.01 us -> 2.26 us  [body(): other = lax.ppermute(ready[0], 'c', [(0, 1), (1, 0)])]
    pallas_call x2, Pallas kernels: 3.92 us -> 2.28 us  [sums_of(): pl.pallas_call(functools.partial(add_products, step) if step else first_k...]
    unnamed x9 -> x11, local copies, waits for them, and re-layouts: 0.72 us -> 2.31 us
  transfers between devices with their start and end apart: 14 -> 14, of which waited for: 6 -> 7; matrix products, arithmetic and copies ran while one was open for 3% -> 4% of each run, Pallas kernels for 2% -> 1%
where the time goes in v10:
time: 157 us
  blocking collectives  69 us (44%)
  starting transfers between devices  48.5 us (31%)
  waiting for transfers between devices  24.1 us (15%)
  other arithmetic  5.7 us (4%)
  local copies, waits for them, and re-layouts  4.46 us (3%)
  Pallas kernels  3.26 us (2%)
  between operations  1.66 us (1%)
    all_to_all x4, blocking collectives, swap(): return lax.all_to_all(v, axes, split_axis=0, concat_axis=0, tiled=True)  69 us
    ppermute x12, starting transfers between devices, trade(): lax.ppermute(v, axis, [(k, (k + 1 - 2 * ((k + way) % 2)) % n) for k in ra...  35.3 us
    ppermute x12, waiting for transfers between devices, trade(): lax.ppermute(v, axis, [(k, (k + 1 - 2 * ((k + way) % 2)) % n) for k in ra...  15.6 us
    all_to_all x1, starting transfers between devices, swap(): return lax.all_to_all(v, axes, split_axis=0, concat_axis=0, tiled=True)  6.66 us
    ppermute x1, starting transfers between devices, body(): other = lax.ppermute(ready[0], 'c', [(0, 1), (1, 0)])  6.54 us
    all_to_all x1, waiting for transfers between devices, swap(): return lax.all_to_all(v, axes, split_axis=0, concat_axis=0, tiled=True)  6.25 us
    convert_element_type x1, other arithmetic, split_tiles(): return (high.astype(jnp.bfloat16), (tiles - high).astype(jnp.bfloat16))  4.7 us
  transfers between devices with their start and end apart: 14, of which 7 were waited for; matrix products, arithmetic and copies ran while one was open for 4% of the time, Pallas kernels for 1%

profile of v10, /device:TPU:1, one launch (start us, length us, event | category | flops | bytes accessed | tf_op | source)
XLA Modules:
  0.0 156.7 jit_solution(15031646807597946719)
XLA Ops:
  0.6 2.0 %broadcast_in_dim.69 = f32[8,128,256]{2,1,0:T(8,128)} broadcast(f32[128,256]{1,0:T(8,128)} %param.7), dimensions={1,2} | broadcast | bytes 1179648 | tf_op jit(solution)/shard_map/broadcast_in_dim | solution.py:72
  2.6 6.7 %all-to-all-start = ((f32[8,128,256]{2,1,0:T(8,128)}), f32[8,128,256]{2,1,0:T(8,128)S(1)}, u32[]{:S(2)}, u32[]{:S(2)}) async-start(f32[8,128,256]{2,1,0:T(8,128)} %broadcast_in_dim.69), calls=%async_computation | async-start | bytes 2097152 | tf_op jit(solution)/shard_map/all_to_all | solution.py:68
  10.4 4.7 %fusion = (bf16[64,128,128]{2,1,0:T(8,128)(2,1)S(1)}, bf16[64,128,128]{2,1,0:T(8,128)(2,1)}) fusion(f32[64,128,128]{2,1,0:T(8,128)} %param.8), kind=kLoop, calls=%fused_computation.2 | loop fusion | flops 4194304 | bytes 8388608 | tf_op jit(solution)/shard_map/convert_element_type | solution.py:95
  15.1 6.3 %all-to-all-done.own_ref = f32[8,128,256]{2,1,0:T(8,128)S(1)} async-done(((f32[8,128,256]{2,1,0:T(8,128)}), f32[8,128,256]{2,1,0:T(8,128)S(1)}, u32[]{:S(2)}, u32[]{:S(2)}) %all-to-all-start) | async-done | bytes 1048608 | tf_op jit(solution)/shard_map/all_to_all | solution.py:68
  21.4 6.5 %collective-permute-start = (f32[8,128,256]{2,1,0:T(8,128)S(1)}, f32[8,128,256]{2,1,0:T(8,128)S(1)}, u32[]{:S(2)}, u32[]{:S(2)}) collective-permute-start(f32[8,128,256]{2,1,0:T(8,128)S(1)} %all-to-all-done.own_ref), channel_id=1, source_target_pairs={{0,32},{32,0},{1,33},{33,1},{2,34},{34,2},{3,35},{35,3},{4,36},{36... | collective-permute-start | bytes 3145736 | tf_op jit(solution)/shard_map/ppermute | solution.py:185
  27.9 2.3 %collective-permute-done.other_ref = f32[8,128,256]{2,1,0:T(8,128)S(1)} collective-permute-done((f32[8,128,256]{2,1,0:T(8,128)S(1)}, f32[8,128,256]{2,1,0:T(8,128)S(1)}, u32[]{:S(2)}, u32[]{:S(2)}) %collective-permute-start) | collective-permute-done | bytes 1048608 | tf_op jit(solution)/shard_map/ppermute | solution.py:185
  30.2 1.6 %copy-done = bf16[64,128,128]{2,1,0:T(8,128)(2,1)S(1)} copy-done((bf16[64,128,128]{2,1,0:T(8,128)(2,1)S(1)}, bf16[64,128,128]{2,1,0:T(8,128)(2,1)}, u32[]{:S(2)}) %copy-start) | copy-done | bytes 2097176
  31.8 1.2 shard_map.86
  33.1 6.0 %collective-permute-start.1 = (f32[8,128,128]{2,1,0:T(8,128)S(1)}, f32[8,128,128]{2,1,0:T(8,128)S(1)}, u32[]{:S(2)}, u32[]{:S(2)}) collective-permute-start(f32[8,128,128]{2,1,0:T(8,128)S(1)} %slice.57), channel_id=1, source_target_pairs={{0,28},{4,8},{8,4},{12,16},{16,12},{20,24},{24,20},{28,0},{1,29},{... | collective-permute-start | bytes 1572872 | tf_op jit(solution)/shard_map/ppermute | solution.py:58
  39.1 1.9 %collective-permute-start.2 = (f32[8,128,128]{2,1,0:T(8,128)S(1)}, f32[8,128,128]{2,1,0:T(8,128)S(1)}, u32[]{:S(2)}, u32[]{:S(2)}) collective-permute-start(f32[8,128,128]{2,1,0:T(8,128)S(1)} %slice.60), channel_id=1, source_target_pairs={{0,4},{4,0},{8,12},{12,8},{16,20},{20,16},{24,28},{28,24},{1,5},{5... | collective-permute-start | bytes 1572872 | tf_op jit(solution)/shard_map/ppermute | solution.py:58
  41.0 1.1 shard_map.87
  42.1 9.2 %collective-permute-done.1 = f32[8,128,128]{2,1,0:T(8,128)S(1)} collective-permute-done((f32[8,128,128]{2,1,0:T(8,128)S(1)}, f32[8,128,128]{2,1,0:T(8,128)S(1)}, u32[]{:S(2)}, u32[]{:S(2)}) %collective-permute-start.1) | collective-permute-done | bytes 524320 | tf_op jit(solution)/shard_map/ppermute | solution.py:58
  51.4 1.9 %collective-permute-start.5 = (f32[4,128,128]{2,1,0:T(8,128)S(1)}, f32[4,128,128]{2,1,0:T(8,128)S(1)}, u32[]{:S(2)}, u32[]{:S(2)}) collective-permute-start(f32[4,128,128]{2,1,0:T(8,128)S(1)} %slice_add_fusion.7), channel_id=1, source_target_pairs={{0,4},{4,0},{8,12},{12,8},{16,20},{20,16},{24,28},{28,24},{1,5},{5... | collective-permute-start | bytes 786440 | tf_op jit(solution)/shard_map/ppermute | solution.py:58
  53.3 1.2 collective-permute-done.2
  54.7 3.4 %collective-permute-start.4 = (f32[4,128,128]{2,1,0:T(8,128)S(1)}, f32[4,128,128]{2,1,0:T(8,128)S(1)}, u32[]{:S(2)}, u32[]{:S(2)}) collective-permute-start(f32[4,128,128]{2,1,0:T(8,128)S(1)} %slice_add_fusion.8), channel_id=1, source_target_pairs={{0,28},{4,8},{8,4},{12,16},{16,12},{20,24},{24,20},{28,0},{1,29},{... | collective-permute-start | bytes 786440 | tf_op jit(solution)/shard_map/ppermute | solution.py:58
  58.1 1.9 %collective-permute-start.3 = (f32[4,128,128]{2,1,0:T(8,128)S(1)}, f32[4,128,128]{2,1,0:T(8,128)S(1)}, u32[]{:S(2)}, u32[]{:S(2)}) collective-permute-start(f32[4,128,128]{2,1,0:T(8,128)S(1)} %slice_add_fusion.9), channel_id=1, source_target_pairs={{0,4},{4,0},{8,12},{12,8},{16,20},{20,16},{24,28},{28,24},{1,5},{5... | collective-permute-start | bytes 786440 | tf_op jit(solution)/shard_map/ppermute | solution.py:58
  60.0 3.4 %collective-permute-start.9 = (f32[4,128,128]{2,1,0:T(8,128)S(1)}, f32[4,128,128]{2,1,0:T(8,128)S(1)}, u32[]{:S(2)}, u32[]{:S(2)}) collective-permute-start(f32[4,128,128]{2,1,0:T(8,128)S(1)} %slice_add_fusion.4), channel_id=1, source_target_pairs={{0,28},{4,8},{8,4},{12,16},{16,12},{20,24},{24,20},{28,0},{1,29},{... | collective-permute-start | bytes 786440 | tf_op jit(solution)/shard_map/ppermute | solution.py:58
  63.5 3.1 %collective-permute-start.8 = (f32[4,128,128]{2,1,0:T(8,128)S(1)}, f32[4,128,128]{2,1,0:T(8,128)S(1)}, u32[]{:S(2)}, u32[]{:S(2)}) collective-permute-start(f32[4,128,128]{2,1,0:T(8,128)S(1)} %slice_add_fusion.5), channel_id=1, source_target_pairs={{0,28},{4,8},{8,4},{12,16},{16,12},{20,24},{24,20},{28,0},{1,29},{... | collective-permute-start | bytes 786440 | tf_op jit(solution)/shard_map/ppermute | solution.py:58
  66.7 2.2 %collective-permute-start.7 = (f32[4,128,128]{2,1,0:T(8,128)S(1)}, f32[4,128,128]{2,1,0:T(8,128)S(1)}, u32[]{:S(2)}, u32[]{:S(2)}) collective-permute-start(f32[4,128,128]{2,1,0:T(8,128)S(1)} %slice_add_fusion.6), channel_id=1, source_target_pairs={{0,4},{4,0},{8,12},{12,8},{16,20},{20,16},{24,28},{28,24},{1,5},{5... | collective-permute-start | bytes 786440 | tf_op jit(solution)/shard_map/ppermute | solution.py:58
  68.9 3.1 %collective-permute-start.6 = (f32[4,128,128]{2,1,0:T(8,128)S(1)}, f32[4,128,128]{2,1,0:T(8,128)S(1)}, u32[]{:S(2)}, u32[]{:S(2)}) collective-permute-start(f32[4,128,128]{2,1,0:T(8,128)S(1)} %slice_add_fusion.10), channel_id=1, source_target_pairs={{0,28},{4,8},{8,4},{12,16},{16,12},{20,24},{24,20},{28,0},{1,29},{... | collective-permute-start | bytes 786440 | tf_op jit(solution)/shard_map/ppermute | solution.py:58
  72.0 2.2 %collective-permute-start.11 = (f32[4,128,128]{2,1,0:T(8,128)S(1)}, f32[4,128,128]{2,1,0:T(8,128)S(1)}, u32[]{:S(2)}, u32[]{:S(2)}) collective-permute-start(f32[4,128,128]{2,1,0:T(8,128)S(1)} %slice_add_fusion.1), channel_id=1, source_target_pairs={{0,4},{4,0},{8,12},{12,8},{16,20},{20,16},{24,28},{28,24},{1,5},{5... | collective-permute-start | bytes 786440 | tf_op jit(solution)/shard_map/ppermute | solution.py:58
  74.2 1.0 collective-permute-done.8
  75.3 2.1 %collective-permute-start.10 = (f32[4,128,128]{2,1,0:T(8,128)S(1)}, f32[4,128,128]{2,1,0:T(8,128)S(1)}, u32[]{:S(2)}, u32[]{:S(2)}) collective-permute-start(f32[4,128,128]{2,1,0:T(8,128)S(1)} %slice_add_fusion.2), channel_id=1, source_target_pairs={{0,4},{4,0},{8,12},{12,8},{16,20},{20,16},{24,28},{28,24},{1,5},{5... | collective-permute-start | bytes 786440 | tf_op jit(solution)/shard_map/ppermute | solution.py:58
  77.4 4.1 %collective-permute-start.12 = (f32[4,128,128]{2,1,0:T(8,128)S(1)}, f32[4,128,128]{2,1,0:T(8,128)S(1)}, u32[]{:S(2)}, u32[]{:S(2)}) collective-permute-start(f32[4,128,128]{2,1,0:T(8,128)S(1)} %slice_add_fusion.3), channel_id=1, source_target_pairs={{0,28},{4,8},{8,4},{12,16},{16,12},{20,24},{24,20},{28,0},{1,29},{... | collective-permute-start | bytes 786440 | tf_op jit(solution)/shard_map/ppermute | solution.py:58
  81.7 3.4 %collective-permute-done.10 = f32[4,128,128]{2,1,0:T(8,128)S(1)} collective-permute-done((f32[4,128,128]{2,1,0:T(8,128)S(1)}, f32[4,128,128]{2,1,0:T(8,128)S(1)}, u32[]{:S(2)}, u32[]{:S(2)}) %collective-permute-start.10) | collective-permute-done | bytes 262176 | tf_op jit(solution)/shard_map/ppermute | solution.py:58
  85.1 0.7 collective-permute-done.12
  85.9 22.4 %all_to_all.25.terms_ref = f32[4,128,256]{2,1,0:T(8,128)S(1)} all-to-all(f32[4,128,256]{2,1,0:T(8,128)S(1)} %pad_maximum_fusion), channel_id=1, replica_groups=mesh['x'=4,'zl'=2,'c'=2,'yh'=4,'yl'=2,'zh'=4] {'zh'}, dimensions={0} | all-to-all | bytes 1048576 | tf_op jit(solution)/shard_map/all_to_all | solution.py:68
  108.2 1.0 shard_map.88
  109.2 17.4 %all_to_all.26 = f32[32,2,8,128]{3,2,1,0:T(8,128)S(1)} all-to-all(f32[32,2,8,128]{3,2,1,0:T(8,128)S(1)} %get-tuple-element.57), channel_id=1, replica_groups=mesh['x'=4,'zl'=2,'c'=2,'yh'=4,'yl'=2,'zh'=4] {'x','zl','c','yl'}, dimensions={0} | all-to-all | bytes 524288 | tf_op jit(solution)/shard_map/all_to_all | solution.py:68
  126.7 16.1 %all_to_all.27 = f32[16,2,8,128]{3,2,1,0:T(8,128)S(1)} all-to-all(f32[16,2,8,128]{3,2,1,0:T(8,128)S(1)} %broadcast_in_dim.76), channel_id=1, replica_groups=mesh['x'=4,'zl'=2,'c'=2,'yh'=4,'yl'=2,'zh'=4] {'yh','zh'}, dimensions={0} | all-to-all | bytes 262144 | tf_op jit(solution)/shard_map/all_to_all | solution.py:68
  142.8 13.1 %all_to_all.28 = f32[32,2,8,128]{3,2,1,0:T(8,128)S(1)} all-to-all(f32[32,2,8,128]{3,2,1,0:T(8,128)S(1)} %broadcast_in_dim.77), channel_id=1, replica_groups=mesh['x'=4,'zl'=2,'c'=2,'yh'=4,'yl'=2,'zh'=4] {'x','zl','c','yl'}, dimensions={0} | all-to-all | bytes 524288 | tf_op jit(solution)/shard_map/all_to_all | solution.py:68
  156.0 0.7 copy.11
  (44 shorter events, 1.2 us)
Async XLA Ops:
  0.6 9.3 %copy-start.3 = (s32[64]{0:T(128)S(1)}, s32[64]{0:T(128)}, u32[]{:S(2)}) copy-start(s32[64]{0:T(128)} %param.9) | copy-start | bytes 772
  0.6 9.6 %copy-start.4 = (s32[64]{0:T(128)S(1)}, s32[64]{0:T(128)}, u32[]{:S(2)}) copy-start(s32[64]{0:T(128)} %param.10) | copy-start | bytes 772
  2.6 18.8 %all-to-all-start = ((f32[8,128,256]{2,1,0:T(8,128)}), f32[8,128,256]{2,1,0:T(8,128)S(1)}, u32[]{:S(2)}, u32[]{:S(2)}) async-start(f32[8,128,256]{2,1,0:T(8,128)} %broadcast_in_dim.69), calls=%async_computation | async-start | bytes 2097152 | tf_op jit(solution)/shard_map/all_to_all | solution.py:68
  21.4 8.8 %collective-permute-start = (f32[8,128,256]{2,1,0:T(8,128)S(1)}, f32[8,128,256]{2,1,0:T(8,128)S(1)}, u32[]{:S(2)}, u32[]{:S(2)}) collective-permute-start(f32[8,128,256]{2,1,0:T(8,128)S(1)} %all-to-all-done.own_ref), channel_id=1, source_target_pairs={{0,32},{32,0},{1,33},{33,1},{2,34},{34,2},{3,35},{35,3},{4,36},{36... | collective-permute-start | bytes 3145736 | tf_op jit(solution)/shard_map/ppermute | solution.py:185
  30.2 1.6 %copy-start = (bf16[64,128,128]{2,1,0:T(8,128)(2,1)S(1)}, bf16[64,128,128]{2,1,0:T(8,128)(2,1)}, u32[]{:S(2)}) copy-start(bf16[64,128,128]{2,1,0:T(8,128)(2,1)} %get-tuple-element.32.left_high) | copy-start | bytes 6291460
  33.1 18.3 %collective-permute-start.1 = (f32[8,128,128]{2,1,0:T(8,128)S(1)}, f32[8,128,128]{2,1,0:T(8,128)S(1)}, u32[]{:S(2)}, u32[]{:S(2)}) collective-permute-start(f32[8,128,128]{2,1,0:T(8,128)S(1)} %slice.57), channel_id=1, source_target_pairs={{0,28},{4,8},{8,4},{12,16},{16,12},{20,24},{24,20},{28,0},{1,29},{... | collective-permute-start | bytes 1572872 | tf_op jit(solution)/shard_map/ppermute | solution.py:58
  39.1 15.5 %collective-permute-start.2 = (f32[8,128,128]{2,1,0:T(8,128)S(1)}, f32[8,128,128]{2,1,0:T(8,128)S(1)}, u32[]{:S(2)}, u32[]{:S(2)}) collective-permute-start(f32[8,128,128]{2,1,0:T(8,128)S(1)} %slice.60), channel_id=1, source_target_pairs={{0,4},{4,0},{8,12},{12,8},{16,20},{20,16},{24,28},{28,24},{1,5},{5... | collective-permute-start | bytes 1572872 | tf_op jit(solution)/shard_map/ppermute | solution.py:58
  51.4 12.0 %collective-permute-start.5 = (f32[4,128,128]{2,1,0:T(8,128)S(1)}, f32[4,128,128]{2,1,0:T(8,128)S(1)}, u32[]{:S(2)}, u32[]{:S(2)}) collective-permute-start(f32[4,128,128]{2,1,0:T(8,128)S(1)} %slice_add_fusion.7), channel_id=1, source_target_pairs={{0,4},{4,0},{8,12},{12,8},{16,20},{20,16},{24,28},{28,24},{1,5},{5... | collective-permute-start | bytes 786440 | tf_op jit(solution)/shard_map/ppermute | solution.py:58
  54.7 12.0 %collective-permute-start.4 = (f32[4,128,128]{2,1,0:T(8,128)S(1)}, f32[4,128,128]{2,1,0:T(8,128)S(1)}, u32[]{:S(2)}, u32[]{:S(2)}) collective-permute-start(f32[4,128,128]{2,1,0:T(8,128)S(1)} %slice_add_fusion.8), channel_id=1, source_target_pairs={{0,28},{4,8},{8,4},{12,16},{16,12},{20,24},{24,20},{28,0},{1,29},{... | collective-permute-start | bytes 786440 | tf_op jit(solution)/shard_map/ppermute | solution.py:58
  58.1 10.7 %collective-permute-start.3 = (f32[4,128,128]{2,1,0:T(8,128)S(1)}, f32[4,128,128]{2,1,0:T(8,128)S(1)}, u32[]{:S(2)}, u32[]{:S(2)}) collective-permute-start(f32[4,128,128]{2,1,0:T(8,128)S(1)} %slice_add_fusion.9), channel_id=1, source_target_pairs={{0,4},{4,0},{8,12},{12,8},{16,20},{20,16},{24,28},{28,24},{1,5},{5... | collective-permute-start | bytes 786440 | tf_op jit(solution)/shard_map/ppermute | solution.py:58
  60.0 12.0 %collective-permute-start.9 = (f32[4,128,128]{2,1,0:T(8,128)S(1)}, f32[4,128,128]{2,1,0:T(8,128)S(1)}, u32[]{:S(2)}, u32[]{:S(2)}) collective-permute-start(f32[4,128,128]{2,1,0:T(8,128)S(1)} %slice_add_fusion.4), channel_id=1, source_target_pairs={{0,28},{4,8},{8,4},{12,16},{16,12},{20,24},{24,20},{28,0},{1,29},{... | collective-permute-start | bytes 786440 | tf_op jit(solution)/shard_map/ppermute | solution.py:58
  63.5 11.8 %collective-permute-start.8 = (f32[4,128,128]{2,1,0:T(8,128)S(1)}, f32[4,128,128]{2,1,0:T(8,128)S(1)}, u32[]{:S(2)}, u32[]{:S(2)}) collective-permute-start(f32[4,128,128]{2,1,0:T(8,128)S(1)} %slice_add_fusion.5), channel_id=1, source_target_pairs={{0,28},{4,8},{8,4},{12,16},{16,12},{20,24},{24,20},{28,0},{1,29},{... | collective-permute-start | bytes 786440 | tf_op jit(solution)/shard_map/ppermute | solution.py:58
  66.7 10.7 %collective-permute-start.7 = (f32[4,128,128]{2,1,0:T(8,128)S(1)}, f32[4,128,128]{2,1,0:T(8,128)S(1)}, u32[]{:S(2)}, u32[]{:S(2)}) collective-permute-start(f32[4,128,128]{2,1,0:T(8,128)S(1)} %slice_add_fusion.6), channel_id=1, source_target_pairs={{0,4},{4,0},{8,12},{12,8},{16,20},{20,16},{24,28},{28,24},{1,5},{5... | collective-permute-start | bytes 786440 | tf_op jit(solution)/shard_map/ppermute | solution.py:58
  68.9 12.7 %collective-permute-start.6 = (f32[4,128,128]{2,1,0:T(8,128)S(1)}, f32[4,128,128]{2,1,0:T(8,128)S(1)}, u32[]{:S(2)}, u32[]{:S(2)}) collective-permute-start(f32[4,128,128]{2,1,0:T(8,128)S(1)} %slice_add_fusion.10), channel_id=1, source_target_pairs={{0,28},{4,8},{8,4},{12,16},{16,12},{20,24},{24,20},{28,0},{1,29},{... | collective-permute-start | bytes 786440 | tf_op jit(solution)/shard_map/ppermute | solution.py:58
  72.0 9.6 %collective-permute-start.11 = (f32[4,128,128]{2,1,0:T(8,128)S(1)}, f32[4,128,128]{2,1,0:T(8,128)S(1)}, u32[]{:S(2)}, u32[]{:S(2)}) collective-permute-start(f32[4,128,128]{2,1,0:T(8,128)S(1)} %slice_add_fusion.1), channel_id=1, source_target_pairs={{0,4},{4,0},{8,12},{12,8},{16,20},{20,16},{24,28},{28,24},{1,5},{5... | collective-permute-start | bytes 786440 | tf_op jit(solution)/shard_map/ppermute | solution.py:58
  75.3 9.8 %collective-permute-start.10 = (f32[4,128,128]{2,1,0:T(8,128)S(1)}, f32[4,128,128]{2,1,0:T(8,128)S(1)}, u32[]{:S(2)}, u32[]{:S(2)}) collective-permute-start(f32[4,128,128]{2,1,0:T(8,128)S(1)} %slice_add_fusion.2), channel_id=1, source_target_pairs={{0,4},{4,0},{8,12},{12,8},{16,20},{20,16},{24,28},{28,24},{1,5},{5... | collective-permute-start | bytes 786440 | tf_op jit(solution)/shard_map/ppermute | solution.py:58
  77.4 8.3 %collective-permute-start.12 = (f32[4,128,128]{2,1,0:T(8,128)S(1)}, f32[4,128,128]{2,1,0:T(8,128)S(1)}, u32[]{:S(2)}, u32[]{:S(2)}) collective-permute-start(f32[4,128,128]{2,1,0:T(8,128)S(1)} %slice_add_fusion.3), channel_id=1, source_target_pairs={{0,28},{4,8},{8,4},{12,16},{16,12},{20,24},{24,20},{28,0},{1,29},{... | collective-permute-start | bytes 786440 | tf_op jit(solution)/shard_map/ppermute | solution.py:58
  85.1 23.1 %copy-start.1 = (f32[256,256]{1,0:T(8,128)S(1)}, f32[256,256]{1,0:T(8,128)}, u32[]{:S(2)}) copy-start(f32[256,256]{1,0:T(8,128)} %weight_ref.1) | copy-start | bytes 786436
  85.1 23.1 %copy-start.2 = (f32[128,256]{1,0:T(8,128)S(1)}, f32[128,256]{1,0:T(8,128)}, u32[]{:S(2)}) copy-start(f32[128,256]{1,0:T(8,128)} %cot_ref.1) | copy-start | bytes 393220

commit v11 on v9

--- a/solution.py
+++ b/solution.py
@@ -180,8 +180,8 @@
 def body(features, adjacency_tiles, tile_rows, tile_cols, tile_count, weight, cotangent):
     ordered, starts = slot_plan(tile_rows, tile_cols, tile_count)
     own = share(features, ("x", "zl"))
-    other = lax.ppermute(own, "c", [(0, 1), (1, 0)])
     left = split_tiles(adjacency_tiles)
+    other = lax.ppermute(lax.optimization_barrier((own, left[0], ordered))[0], "c", [(0, 1), (1, 0)])
     *early, high, low = sums_of(0, starts, ordered, left, (own, other))
     late = sums_of(1, after(starts, early[0]), ordered, left, (high, low))
 

time: 158 us -> 157 us (level)
  waiting for transfers between devices: 26.7 us -> 20.4 us
  Pallas kernels: 4.9 us -> 7.87 us
  starting transfers between devices: 49.4 us -> 47.7 us
  local copies, waits for them, and re-layouts: 2.87 us -> 4.46 us
    all_to_all x1, waiting for transfers between devices: 12.1 us -> 6.37 us  [swap(): return lax.all_to_all(v, axes, split_axis=0, concat_axis=0, tiled=True)]
    pallas_call x2, Pallas kernels: 3.92 us -> 6.89 us  [sums_of(): pl.pallas_call(functools.partial(add_products, step) if step else first_k...]
    ppermute x12, waiting for transfers between devices: 14.6 us -> 11.8 us  [trade(): lax.ppermute(v, axis, [(k, (k + 1 - 2 * ((k + way) % 2)) % n) for k in ra...]
    ppermute x1, waiting for transfers between devices: 0.01 us -> 2.15 us  [body(): lax.ppermute(lax.optimization_barrier((own, left[0], ordered))[0], 'c', [...]
    ppermute x12, starting transfers between devices: 36.2 us -> 34.5 us  [trade(): lax.ppermute(v, axis, [(k, (k + 1 - 2 * ((k + way) % 2)) % n) for k in ra...]
    unnamed x9 -> x11, local copies, waits for them, and re-layouts: 0.72 us -> 2.31 us
  transfers between devices with their start and end apart: 14 -> 14, of which waited for: 6 -> 7; matrix products, arithmetic and copies ran while one was open for 3% -> 4% of each run, Pallas kernels for 2% -> 3%
where the time goes in v11:
time: 157 us
  blocking collectives  69 us (44%)
  starting transfers between devices  47.7 us (30%)
  waiting for transfers between devices  20.4 us (13%)
  Pallas kernels  7.87 us (5%)
  other arithmetic  5.69 us (4%)
  local copies, waits for them, and re-layouts  4.46 us (3%)
  between operations  1.67 us (1%)
    all_to_all x4, blocking collectives, swap(): return lax.all_to_all(v, axes, split_axis=0, concat_axis=0, tiled=True)  69 us
    ppermute x12, starting transfers between devices, trade(): lax.ppermute(v, axis, [(k, (k + 1 - 2 * ((k + way) % 2)) % n) for k in ra...  34.5 us
    ppermute x12, waiting for transfers between devices, trade(): lax.ppermute(v, axis, [(k, (k + 1 - 2 * ((k + way) % 2)) % n) for k in ra...  11.8 us
    pallas_call x2, Pallas kernels, sums_of(): pl.pallas_call(functools.partial(add_products, step) if step else first_k...  6.89 us
    all_to_all x1, starting transfers between devices, swap(): return lax.all_to_all(v, axes, split_axis=0, concat_axis=0, tiled=True)  6.66 us
    ppermute x1, starting transfers between devices, body(): lax.ppermute(lax.optimization_barrier((own, left[0], ordered))[0], 'c', [...  6.54 us
    all_to_all x1, waiting for transfers between devices, swap(): return lax.all_to_all(v, axes, split_axis=0, concat_axis=0, tiled=True)  6.37 us
    convert_element_type x1, other arithmetic, split_tiles(): return (high.astype(jnp.bfloat16), (tiles - high).astype(jnp.bfloat16))  4.7 us
  transfers between devices with their start and end apart: 14, of which 7 were waited for; matrix products, arithmetic and copies ran while one was open for 4% of the time, Pallas kernels for 3%

profile of v11, /device:TPU:1, one launch (start us, length us, event | category | flops | bytes accessed | tf_op | source)
XLA Modules:
  0.0 156.8 jit_solution(6435826489023073229)
XLA Ops:
  0.6 2.0 %broadcast_in_dim.75 = f32[8,128,256]{2,1,0:T(8,128)} broadcast(f32[128,256]{1,0:T(8,128)} %param.7), dimensions={1,2} | broadcast | bytes 1179648 | tf_op jit(solution)/shard_map/broadcast_in_dim | solution.py:72
  2.6 6.7 %all-to-all-start = ((f32[8,128,256]{2,1,0:T(8,128)}), f32[8,128,256]{2,1,0:T(8,128)S(1)}, u32[]{:S(2)}, u32[]{:S(2)}) async-start(f32[8,128,256]{2,1,0:T(8,128)} %broadcast_in_dim.75), calls=%async_computation | async-start | bytes 2097152 | tf_op jit(solution)/shard_map/all_to_all | solution.py:68
  10.3 4.7 %fusion = (bf16[64,128,128]{2,1,0:T(8,128)(2,1)S(1)}, bf16[64,128,128]{2,1,0:T(8,128)(2,1)}) fusion(f32[64,128,128]{2,1,0:T(8,128)} %param.8), kind=kLoop, calls=%fused_computation.2 | loop fusion | flops 4194304 | bytes 8388608 | tf_op jit(solution)/shard_map/convert_element_type | solution.py:95
  15.0 6.4 %all-to-all-done.own_ref = f32[8,128,256]{2,1,0:T(8,128)S(1)} async-done(((f32[8,128,256]{2,1,0:T(8,128)}), f32[8,128,256]{2,1,0:T(8,128)S(1)}, u32[]{:S(2)}, u32[]{:S(2)}) %all-to-all-start) | async-done | bytes 1048608 | tf_op jit(solution)/shard_map/all_to_all | solution.py:68
  21.4 6.5 %collective-permute-start = (f32[8,128,256]{2,1,0:T(8,128)S(1)}, f32[8,128,256]{2,1,0:T(8,128)S(1)}, u32[]{:S(2)}, u32[]{:S(2)}) collective-permute-start(f32[8,128,256]{2,1,0:T(8,128)S(1)} %all-to-all-done.own_ref), channel_id=1, source_target_pairs={{0,32},{32,0},{1,33},{33,1},{2,34},{34,2},{3,35},{35,3},{4,36},{36... | collective-permute-start | bytes 3145736 | tf_op jit(solution)/shard_map/ppermute | solution.py:184
  28.1 2.1 %collective-permute-done.other_ref = f32[8,128,256]{2,1,0:T(8,128)S(1)} collective-permute-done((f32[8,128,256]{2,1,0:T(8,128)S(1)}, f32[8,128,256]{2,1,0:T(8,128)S(1)}, u32[]{:S(2)}, u32[]{:S(2)}) %collective-permute-start) | collective-permute-done | bytes 1048608 | tf_op jit(solution)/shard_map/ppermute | solution.py:184
  30.2 1.6 %copy-done = bf16[64,128,128]{2,1,0:T(8,128)(2,1)S(1)} copy-done((bf16[64,128,128]{2,1,0:T(8,128)(2,1)S(1)}, bf16[64,128,128]{2,1,0:T(8,128)(2,1)}, u32[]{:S(2)}) %copy-start) | copy-done | bytes 2097176
  31.8 2.5 %shard_map.86 = (f32[13,128,128]{2,1,0:T(8,128)S(1)}, f32[13,128,128]{2,1,0:T(8,128)S(1)}, bf16[16,128,256]{2,1,0:T(8,128)(2,1)S(1)}, bf16[16,128,256]{2,1,0:T(8,128)(2,1)S(1)}) custom-call(s32[8]{0:T(128)S(1)} %convert_reduce_fusion.1.starts_ref, s32[64]{0:T(128)S(1)} %select_reduce_fusion.order_ref, bf16[64,128,128]{2,1,0:T(8,128)(2,1)S(1)} %copy-done, ...), custom_call_target="tpu_custom_call" | custom-call | flops 1000000 | bytes 16384 | tf_op jit(solution)/shard_map/pallas_call | solution.py:140
  34.4 4.3 %collective-permute-start.1 = (f32[8,128,128]{2,1,0:T(8,128)S(1)}, f32[8,128,128]{2,1,0:T(8,128)S(1)}, u32[]{:S(2)}, u32[]{:S(2)}) collective-permute-start(f32[8,128,128]{2,1,0:T(8,128)S(1)} %slice.57), channel_id=1, source_target_pairs={{0,28},{4,8},{8,4},{12,16},{16,12},{20,24},{24,20},{28,0},{1,29},{... | collective-permute-start | bytes 1572872 | tf_op jit(solution)/shard_map/ppermute | solution.py:58
  38.8 1.9 %collective-permute-start.2 = (f32[8,128,128]{2,1,0:T(8,128)S(1)}, f32[8,128,128]{2,1,0:T(8,128)S(1)}, u32[]{:S(2)}, u32[]{:S(2)}) collective-permute-start(f32[8,128,128]{2,1,0:T(8,128)S(1)} %slice.60), channel_id=1, source_target_pairs={{0,4},{4,0},{8,12},{12,8},{16,20},{20,16},{24,28},{28,24},{1,5},{5... | collective-permute-start | bytes 1572872 | tf_op jit(solution)/shard_map/ppermute | solution.py:58
  40.7 4.4 %shard_map.87 = (f32[21,128,128]{2,1,0:T(8,128)S(1)}, f32[21,128,128]{2,1,0:T(8,128)S(1)}) custom-call(s32[8]{0:T(128)S(1)} %convert_reduce_fusion.1.starts_ref, s32[64]{0:T(128)S(1)} %select_reduce_fusion.order_ref, bf16[64,128,128]{2,1,0:T(8,128)(2,1)S(1)} %copy-done, bf16[64,128,128]{2,1,0:T(8,128)(2,1)S(1)} %get-tuple-element.52.left_low, ...), custom_call_target="tpu_custom_call" | custom-call | flops 1000000 | bytes 16384 | tf_op jit(solution)/shard_map/pallas_call | solution.py:140
  45.1 6.0 %collective-permute-done.1 = f32[8,128,128]{2,1,0:T(8,128)S(1)} collective-permute-done((f32[8,128,128]{2,1,0:T(8,128)S(1)}, f32[8,128,128]{2,1,0:T(8,128)S(1)}, u32[]{:S(2)}, u32[]{:S(2)}) %collective-permute-start.1) | collective-permute-done | bytes 524320 | tf_op jit(solution)/shard_map/ppermute | solution.py:58
  51.2 2.4 %collective-permute-start.5 = (f32[4,128,128]{2,1,0:T(8,128)S(1)}, f32[4,128,128]{2,1,0:T(8,128)S(1)}, u32[]{:S(2)}, u32[]{:S(2)}) collective-permute-start(f32[4,128,128]{2,1,0:T(8,128)S(1)} %slice_add_fusion.7), channel_id=1, source_target_pairs={{0,4},{4,0},{8,12},{12,8},{16,20},{20,16},{24,28},{28,24},{1,5},{5... | collective-permute-start | bytes 786440 | tf_op jit(solution)/shard_map/ppermute | solution.py:58
  53.6 0.7 collective-permute-done.2
  54.3 3.4 %collective-permute-start.4 = (f32[4,128,128]{2,1,0:T(8,128)S(1)}, f32[4,128,128]{2,1,0:T(8,128)S(1)}, u32[]{:S(2)}, u32[]{:S(2)}) collective-permute-start(f32[4,128,128]{2,1,0:T(8,128)S(1)} %slice_add_fusion.8), channel_id=1, source_target_pairs={{0,28},{4,8},{8,4},{12,16},{16,12},{20,24},{24,20},{28,0},{1,29},{... | collective-permute-start | bytes 786440 | tf_op jit(solution)/shard_map/ppermute | solution.py:58
  57.8 1.9 %collective-permute-start.3 = (f32[4,128,128]{2,1,0:T(8,128)S(1)}, f32[4,128,128]{2,1,0:T(8,128)S(1)}, u32[]{:S(2)}, u32[]{:S(2)}) collective-permute-start(f32[4,128,128]{2,1,0:T(8,128)S(1)} %slice_add_fusion.9), channel_id=1, source_target_pairs={{0,4},{4,0},{8,12},{12,8},{16,20},{20,16},{24,28},{28,24},{1,5},{5... | collective-permute-start | bytes 786440 | tf_op jit(solution)/shard_map/ppermute | solution.py:58
  59.7 3.8 %collective-permute-start.9 = (f32[4,128,128]{2,1,0:T(8,128)S(1)}, f32[4,128,128]{2,1,0:T(8,128)S(1)}, u32[]{:S(2)}, u32[]{:S(2)}) collective-permute-start(f32[4,128,128]{2,1,0:T(8,128)S(1)} %slice_add_fusion.4), channel_id=1, source_target_pairs={{0,28},{4,8},{8,4},{12,16},{16,12},{20,24},{24,20},{28,0},{1,29},{... | collective-permute-start | bytes 786440 | tf_op jit(solution)/shard_map/ppermute | solution.py:58
  63.6 2.7 %collective-permute-start.8 = (f32[4,128,128]{2,1,0:T(8,128)S(1)}, f32[4,128,128]{2,1,0:T(8,128)S(1)}, u32[]{:S(2)}, u32[]{:S(2)}) collective-permute-start(f32[4,128,128]{2,1,0:T(8,128)S(1)} %slice_add_fusion.5), channel_id=1, source_target_pairs={{0,28},{4,8},{8,4},{12,16},{16,12},{20,24},{24,20},{28,0},{1,29},{... | collective-permute-start | bytes 786440 | tf_op jit(solution)/shard_map/ppermute | solution.py:58
  66.3 2.2 %collective-permute-start.7 = (f32[4,128,128]{2,1,0:T(8,128)S(1)}, f32[4,128,128]{2,1,0:T(8,128)S(1)}, u32[]{:S(2)}, u32[]{:S(2)}) collective-permute-start(f32[4,128,128]{2,1,0:T(8,128)S(1)} %slice_add_fusion.6), channel_id=1, source_target_pairs={{0,4},{4,0},{8,12},{12,8},{16,20},{20,16},{24,28},{28,24},{1,5},{5... | collective-permute-start | bytes 786440 | tf_op jit(solution)/shard_map/ppermute | solution.py:58
  68.5 3.6 %collective-permute-start.6 = (f32[4,128,128]{2,1,0:T(8,128)S(1)}, f32[4,128,128]{2,1,0:T(8,128)S(1)}, u32[]{:S(2)}, u32[]{:S(2)}) collective-permute-start(f32[4,128,128]{2,1,0:T(8,128)S(1)} %slice_add_fusion.10), channel_id=1, source_target_pairs={{0,28},{4,8},{8,4},{12,16},{16,12},{20,24},{24,20},{28,0},{1,29},{... | collective-permute-start | bytes 786440 | tf_op jit(solution)/shard_map/ppermute | solution.py:58
  72.2 2.5 %collective-permute-start.11 = (f32[4,128,128]{2,1,0:T(8,128)S(1)}, f32[4,128,128]{2,1,0:T(8,128)S(1)}, u32[]{:S(2)}, u32[]{:S(2)}) collective-permute-start(f32[4,128,128]{2,1,0:T(8,128)S(1)} %slice_add_fusion.1), channel_id=1, source_target_pairs={{0,4},{4,0},{8,12},{12,8},{16,20},{20,16},{24,28},{28,24},{1,5},{5... | collective-permute-start | bytes 786440 | tf_op jit(solution)/shard_map/ppermute | solution.py:58
  74.6 0.6 collective-permute-done.8
  75.3 2.2 %collective-permute-start.10 = (f32[4,128,128]{2,1,0:T(8,128)S(1)}, f32[4,128,128]{2,1,0:T(8,128)S(1)}, u32[]{:S(2)}, u32[]{:S(2)}) collective-permute-start(f32[4,128,128]{2,1,0:T(8,128)S(1)} %slice_add_fusion.2), channel_id=1, source_target_pairs={{0,4},{4,0},{8,12},{12,8},{16,20},{20,16},{24,28},{28,24},{1,5},{5... | collective-permute-start | bytes 786440 | tf_op jit(solution)/shard_map/ppermute | solution.py:58
  77.6 3.7 %collective-permute-start.12 = (f32[4,128,128]{2,1,0:T(8,128)S(1)}, f32[4,128,128]{2,1,0:T(8,128)S(1)}, u32[]{:S(2)}, u32[]{:S(2)}) collective-permute-start(f32[4,128,128]{2,1,0:T(8,128)S(1)} %slice_add_fusion.3), channel_id=1, source_target_pairs={{0,28},{4,8},{8,4},{12,16},{16,12},{20,24},{24,20},{28,0},{1,29},{... | collective-permute-start | bytes 786440 | tf_op jit(solution)/shard_map/ppermute | solution.py:58
  81.4 3.9 %collective-permute-done.10 = f32[4,128,128]{2,1,0:T(8,128)S(1)} collective-permute-done((f32[4,128,128]{2,1,0:T(8,128)S(1)}, f32[4,128,128]{2,1,0:T(8,128)S(1)}, u32[]{:S(2)}, u32[]{:S(2)}) %collective-permute-start.10) | collective-permute-done | bytes 262176 | tf_op jit(solution)/shard_map/ppermute | solution.py:58
  85.4 0.5 collective-permute-done.12
  86.0 22.6 %all_to_all.25.terms_ref = f32[4,128,256]{2,1,0:T(8,128)S(1)} all-to-all(f32[4,128,256]{2,1,0:T(8,128)S(1)} %pad_maximum_fusion), channel_id=1, replica_groups=mesh['x'=4,'zl'=2,'c'=2,'yh'=4,'yl'=2,'zh'=4] {'zh'}, dimensions={0} | all-to-all | bytes 1048576 | tf_op jit(solution)/shard_map/all_to_all | solution.py:68
  108.6 1.0 shard_map.88
  109.5 17.2 %all_to_all.26 = f32[32,2,8,128]{3,2,1,0:T(8,128)S(1)} all-to-all(f32[32,2,8,128]{3,2,1,0:T(8,128)S(1)} %get-tuple-element.49), channel_id=1, replica_groups=mesh['x'=4,'zl'=2,'c'=2,'yh'=4,'yl'=2,'zh'=4] {'x','zl','c','yl'}, dimensions={0} | all-to-all | bytes 524288 | tf_op jit(solution)/shard_map/all_to_all | solution.py:68
  126.8 16.1 %all_to_all.27 = f32[16,2,8,128]{3,2,1,0:T(8,128)S(1)} all-to-all(f32[16,2,8,128]{3,2,1,0:T(8,128)S(1)} %broadcast_in_dim.76), channel_id=1, replica_groups=mesh['x'=4,'zl'=2,'c'=2,'yh'=4,'yl'=2,'zh'=4] {'yh','zh'}, dimensions={0} | all-to-all | bytes 262144 | tf_op jit(solution)/shard_map/all_to_all | solution.py:68
  143.0 13.1 %all_to_all.28 = f32[32,2,8,128]{3,2,1,0:T(8,128)S(1)} all-to-all(f32[32,2,8,128]{3,2,1,0:T(8,128)S(1)} %broadcast_in_dim.77), channel_id=1, replica_groups=mesh['x'=4,'zl'=2,'c'=2,'yh'=4,'yl'=2,'zh'=4] {'x','zl','c','yl'}, dimensions={0} | all-to-all | bytes 524288 | tf_op jit(solution)/shard_map/all_to_all | solution.py:68
  156.1 0.7 copy.11
  (44 shorter events, 1.2 us)
Async XLA Ops:
  0.6 9.3 %copy-start.3 = (s32[64]{0:T(128)S(1)}, s32[64]{0:T(128)}, u32[]{:S(2)}) copy-start(s32[64]{0:T(128)} %param.10) | copy-start | bytes 772
  0.6 9.3 %copy-start.4 = (s32[64]{0:T(128)S(1)}, s32[64]{0:T(128)}, u32[]{:S(2)}) copy-start(s32[64]{0:T(128)} %param.9) | copy-start | bytes 772
  2.6 18.8 %all-to-all-start = ((f32[8,128,256]{2,1,0:T(8,128)}), f32[8,128,256]{2,1,0:T(8,128)S(1)}, u32[]{:S(2)}, u32[]{:S(2)}) async-start(f32[8,128,256]{2,1,0:T(8,128)} %broadcast_in_dim.75), calls=%async_computation | async-start | bytes 2097152 | tf_op jit(solution)/shard_map/all_to_all | solution.py:68
  21.4 8.8 %collective-permute-start = (f32[8,128,256]{2,1,0:T(8,128)S(1)}, f32[8,128,256]{2,1,0:T(8,128)S(1)}, u32[]{:S(2)}, u32[]{:S(2)}) collective-permute-start(f32[8,128,256]{2,1,0:T(8,128)S(1)} %all-to-all-done.own_ref), channel_id=1, source_target_pairs={{0,32},{32,0},{1,33},{33,1},{2,34},{34,2},{3,35},{35,3},{4,36},{36... | collective-permute-start | bytes 3145736 | tf_op jit(solution)/shard_map/ppermute | solution.py:184
  30.2 1.6 %copy-start = (bf16[64,128,128]{2,1,0:T(8,128)(2,1)S(1)}, bf16[64,128,128]{2,1,0:T(8,128)(2,1)}, u32[]{:S(2)}) copy-start(bf16[64,128,128]{2,1,0:T(8,128)(2,1)} %get-tuple-element.53.left_high) | copy-start | bytes 6291460
  34.4 16.7 %collective-permute-start.1 = (f32[8,128,128]{2,1,0:T(8,128)S(1)}, f32[8,128,128]{2,1,0:T(8,128)S(1)}, u32[]{:S(2)}, u32[]{:S(2)}) collective-permute-start(f32[8,128,128]{2,1,0:T(8,128)S(1)} %slice.57), channel_id=1, source_target_pairs={{0,28},{4,8},{8,4},{12,16},{16,12},{20,24},{24,20},{28,0},{1,29},{... | collective-permute-start | bytes 1572872 | tf_op jit(solution)/shard_map/ppermute | solution.py:58
  38.8 15.5 %collective-permute-start.2 = (f32[8,128,128]{2,1,0:T(8,128)S(1)}, f32[8,128,128]{2,1,0:T(8,128)S(1)}, u32[]{:S(2)}, u32[]{:S(2)}) collective-permute-start(f32[8,128,128]{2,1,0:T(8,128)S(1)} %slice.60), channel_id=1, source_target_pairs={{0,4},{4,0},{8,12},{12,8},{16,20},{20,16},{24,28},{28,24},{1,5},{5... | collective-permute-start | bytes 1572872 | tf_op jit(solution)/shard_map/ppermute | solution.py:58
  51.2 12.3 %collective-permute-start.5 = (f32[4,128,128]{2,1,0:T(8,128)S(1)}, f32[4,128,128]{2,1,0:T(8,128)S(1)}, u32[]{:S(2)}, u32[]{:S(2)}) collective-permute-start(f32[4,128,128]{2,1,0:T(8,128)S(1)} %slice_add_fusion.7), channel_id=1, source_target_pairs={{0,4},{4,0},{8,12},{12,8},{16,20},{20,16},{24,28},{28,24},{1,5},{5... | collective-permute-start | bytes 786440 | tf_op jit(solution)/shard_map/ppermute | solution.py:58
  54.3 12.0 %collective-permute-start.4 = (f32[4,128,128]{2,1,0:T(8,128)S(1)}, f32[4,128,128]{2,1,0:T(8,128)S(1)}, u32[]{:S(2)}, u32[]{:S(2)}) collective-permute-start(f32[4,128,128]{2,1,0:T(8,128)S(1)} %slice_add_fusion.8), channel_id=1, source_target_pairs={{0,28},{4,8},{8,4},{12,16},{16,12},{20,24},{24,20},{28,0},{1,29},{... | collective-permute-start | bytes 786440 | tf_op jit(solution)/shard_map/ppermute | solution.py:58
  57.8 10.7 %collective-permute-start.3 = (f32[4,128,128]{2,1,0:T(8,128)S(1)}, f32[4,128,128]{2,1,0:T(8,128)S(1)}, u32[]{:S(2)}, u32[]{:S(2)}) collective-permute-start(f32[4,128,128]{2,1,0:T(8,128)S(1)} %slice_add_fusion.9), channel_id=1, source_target_pairs={{0,4},{4,0},{8,12},{12,8},{16,20},{20,16},{24,28},{28,24},{1,5},{5... | collective-permute-start | bytes 786440 | tf_op jit(solution)/shard_map/ppermute | solution.py:58
  59.7 12.4 %collective-permute-start.9 = (f32[4,128,128]{2,1,0:T(8,128)S(1)}, f32[4,128,128]{2,1,0:T(8,128)S(1)}, u32[]{:S(2)}, u32[]{:S(2)}) collective-permute-start(f32[4,128,128]{2,1,0:T(8,128)S(1)} %slice_add_fusion.4), channel_id=1, source_target_pairs={{0,28},{4,8},{8,4},{12,16},{16,12},{20,24},{24,20},{28,0},{1,29},{... | collective-permute-start | bytes 786440 | tf_op jit(solution)/shard_map/ppermute | solution.py:58
  63.6 11.7 %collective-permute-start.8 = (f32[4,128,128]{2,1,0:T(8,128)S(1)}, f32[4,128,128]{2,1,0:T(8,128)S(1)}, u32[]{:S(2)}, u32[]{:S(2)}) collective-permute-start(f32[4,128,128]{2,1,0:T(8,128)S(1)} %slice_add_fusion.5), channel_id=1, source_target_pairs={{0,28},{4,8},{8,4},{12,16},{16,12},{20,24},{24,20},{28,0},{1,29},{... | collective-permute-start | bytes 786440 | tf_op jit(solution)/shard_map/ppermute | solution.py:58
  66.3 11.2 %collective-permute-start.7 = (f32[4,128,128]{2,1,0:T(8,128)S(1)}, f32[4,128,128]{2,1,0:T(8,128)S(1)}, u32[]{:S(2)}, u32[]{:S(2)}) collective-permute-start(f32[4,128,128]{2,1,0:T(8,128)S(1)} %slice_add_fusion.6), channel_id=1, source_target_pairs={{0,4},{4,0},{8,12},{12,8},{16,20},{20,16},{24,28},{28,24},{1,5},{5... | collective-permute-start | bytes 786440 | tf_op jit(solution)/shard_map/ppermute | solution.py:58
  68.5 12.7 %collective-permute-start.6 = (f32[4,128,128]{2,1,0:T(8,128)S(1)}, f32[4,128,128]{2,1,0:T(8,128)S(1)}, u32[]{:S(2)}, u32[]{:S(2)}) collective-permute-start(f32[4,128,128]{2,1,0:T(8,128)S(1)} %slice_add_fusion.10), channel_id=1, source_target_pairs={{0,28},{4,8},{8,4},{12,16},{16,12},{20,24},{24,20},{28,0},{1,29},{... | collective-permute-start | bytes 786440 | tf_op jit(solution)/shard_map/ppermute | solution.py:58
  72.2 9.1 %collective-permute-start.11 = (f32[4,128,128]{2,1,0:T(8,128)S(1)}, f32[4,128,128]{2,1,0:T(8,128)S(1)}, u32[]{:S(2)}, u32[]{:S(2)}) collective-permute-start(f32[4,128,128]{2,1,0:T(8,128)S(1)} %slice_add_fusion.1), channel_id=1, source_target_pairs={{0,4},{4,0},{8,12},{12,8},{16,20},{20,16},{24,28},{28,24},{1,5},{5... | collective-permute-start | bytes 786440 | tf_op jit(solution)/shard_map/ppermute | solution.py:58
  75.3 10.0 %collective-permute-start.10 = (f32[4,128,128]{2,1,0:T(8,128)S(1)}, f32[4,128,128]{2,1,0:T(8,128)S(1)}, u32[]{:S(2)}, u32[]{:S(2)}) collective-permute-start(f32[4,128,128]{2,1,0:T(8,128)S(1)} %slice_add_fusion.2), channel_id=1, source_target_pairs={{0,4},{4,0},{8,12},{12,8},{16,20},{20,16},{24,28},{28,24},{1,5},{5... | collective-permute-start | bytes 786440 | tf_op jit(solution)/shard_map/ppermute | solution.py:58
  77.6 8.3 %collective-permute-start.12 = (f32[4,128,128]{2,1,0:T(8,128)S(1)}, f32[4,128,128]{2,1,0:T(8,128)S(1)}, u32[]{:S(2)}, u32[]{:S(2)}) collective-permute-start(f32[4,128,128]{2,1,0:T(8,128)S(1)} %slice_add_fusion.3), channel_id=1, source_target_pairs={{0,28},{4,8},{8,4},{12,16},{16,12},{20,24},{24,20},{28,0},{1,29},{... | collective-permute-start | bytes 786440 | tf_op jit(solution)/shard_map/ppermute | solution.py:58
  85.3 23.2 %copy-start.1 = (f32[256,256]{1,0:T(8,128)S(1)}, f32[256,256]{1,0:T(8,128)}, u32[]{:S(2)}) copy-start(f32[256,256]{1,0:T(8,128)} %weight_ref.1) | copy-start | bytes 786436
  85.3 23.2 %copy-start.2 = (f32[128,256]{1,0:T(8,128)S(1)}, f32[128,256]{1,0:T(8,128)}, u32[]{:S(2)}) copy-start(f32[128,256]{1,0:T(8,128)} %cot_ref.1) | copy-start | bytes 393220
